TPU v7x, 256 devices: a whole 4x4x8 slice. The times are simulated.
256 devices in a mesh: width: 16 (over y, x_hi, core), feat: 16 (over x_lo, z).
Axes of the slice: x: 4 (x_hi: 2, x_lo: 2; x = x_hi * 2 + x_lo), y: 4, z: 8, core: 2. Of those that a mesh axis runs over, the one named last changes fastest.
Arguments:
- acts: bfloat16 [4096, 2, 8192], P('feat', None, 'width'), may hold values from -6 to 6
- enc_weight: bfloat16 [16, 2, 8192, 1024], P('feat', None, 'width'), may hold values from -0.046875 to 0.046875
- enc_bias: float32 [16, 1024], P('feat'), may hold values from -6 to 6
- dec_weight: bfloat16 [16, 1024, 2, 8192], P('feat', None, None, 'width'), may hold values from -1 to 1
- dec_bias: float32 [2, 8192], P(None, 'width'), may hold values from -4 to 4
- routes: int32 [4096, 2], P('feat'), may hold values from 0 to 15, all different within a row; in each aligned block of 256 rows (0 to 255, 256 to 511, ...) at most 64 rows name the same one
- latent_index: int32 [4096, 2, 32], P('feat'), may hold values from 0 to 1023, as said below
Outputs:
- grad_enc: bfloat16 [16, 2, 8192, 1024], P('feat', None, 'width')
- grad_dec: bfloat16 [16, 1024, 2, 8192], P('feat', None, None, 'width')
Inputs may be any that keep to these rules, and one draw needn't show every extreme that they name: `routes`: within the 256 rows of one device no expert is named by more than 64 rows, a bound that some block reaches. `latent_index`: the 32 latents of one token and route are distinct.
All inputs are finite; a program needn't handle non-finite values.
Results may differ from a plain program's by a relative error of at most 0.0057.
Values may be sent and summed in bfloat16 or wider, within the bound.
No kernel may reach another device: no remote copies, remote signals or barrier semaphores. Data moves between devices by JAX's collectives and lax.ppermute only.
A program may use at most 128 MiB of HBM per device.

v0:
```python
import math

import jax
import jax.numpy as jnp
from jax import lax
from jax.sharding import PartitionSpec as P

D = 8192
L = 2


def silu_grad(value):
    sigmoid_value = jax.nn.sigmoid(value)
    return sigmoid_value * (1.0 + value * (1.0 - sigmoid_value))


def latent_mask(index_rows, latents):
    row_ids = jnp.arange(index_rows.shape[0], dtype=jnp.int32)[:, None]
    empty_mask = jnp.zeros((index_rows.shape[0], latents), jnp.bool_)
    return empty_mask.at[row_ids, index_rows].set(True, mode="drop")


def per_device(acts, enc_weight, enc_bias, dec_weight, dec_bias, routes, latent_index):
    groups = lax.axis_size("feat")
    tok_count, layers, width_dev = acts.shape
    inner_width = layers * width_dev
    latents = enc_weight.shape[3]
    route_count = routes.shape[1]
    pick_count = latent_index.shape[2]
    capacity = 2 * tok_count * route_count // groups
    slot_count = groups * capacity
    scale_factor = 1.0 / math.sqrt(L * D)
    tokens_here = acts.reshape(tok_count, inner_width)
    enc_local = enc_weight.reshape(inner_width, latents)
    dec_local = dec_weight.reshape(latents, inner_width)
    bias_row = enc_bias.reshape(latents)
    flat_routes = routes.reshape(tok_count * route_count)
    onehot = (flat_routes[:, None] == jnp.arange(groups, dtype=jnp.int32)[None, :]).astype(
        jnp.int32
    )
    position = jnp.sum(jnp.cumsum(onehot, axis=0) * onehot, axis=1) - 1
    slot_of = flat_routes * capacity + position
    token_rows = jnp.repeat(tokens_here, route_count, axis=0)
    send_rows = jnp.zeros((slot_count, inner_width), acts.dtype).at[slot_of].set(token_rows)
    send_index = jnp.full((slot_count, pick_count), latents, jnp.int32)
    send_index = send_index.at[slot_of].set(
        latent_index.reshape(tok_count * route_count, pick_count)
    )
    arrived, arrived_index = (
        lax.all_to_all(
            send_rows.reshape(groups, capacity, inner_width),
            "feat",
            split_axis=0,
            concat_axis=0,
            tiled=True,
        ),
        lax.all_to_all(
            send_index.reshape(groups, capacity, pick_count),
            "feat",
            split_axis=0,
            concat_axis=0,
            tiled=True,
        ),
    )
    expert_rows = arrived.reshape(slot_count, inner_width)
    kept_index = arrived_index.reshape(slot_count, pick_count)
    selected = latent_mask(kept_index, latents)
    partial_pre = jnp.dot(expert_rows, enc_local, preferred_element_type=jnp.float32)
    preact = lax.psum(partial_pre, "width") + bias_row
    activated = jax.nn.silu(preact).astype(jnp.bfloat16)
    latent = jnp.where(selected, activated, jnp.zeros((), jnp.bfloat16))
    decoded = jnp.dot(latent, dec_local, preferred_element_type=jnp.float32).astype(jnp.bfloat16)
    returned = lax.all_to_all(
        decoded.reshape(groups, capacity, inner_width),
        "feat",
        split_axis=0,
        concat_axis=0,
        tiled=True,
    )
    route_rows = returned.reshape(slot_count, inner_width)[slot_of].astype(jnp.float32)
    rebuilt = route_rows.reshape(tok_count, route_count, inner_width).sum(
        axis=1
    ) + dec_bias.reshape(inner_width)
    residual = (rebuilt - tokens_here.astype(jnp.float32)).astype(jnp.bfloat16)
    res_send = (
        jnp.zeros((slot_count, inner_width), jnp.bfloat16)
        .at[slot_of]
        .set(jnp.repeat(residual, route_count, axis=0))
    )
    res_expert = lax.all_to_all(
        res_send.reshape(groups, capacity, inner_width),
        "feat",
        split_axis=0,
        concat_axis=0,
        tiled=True,
    ).reshape(slot_count, inner_width)
    grad_dec = lax.dot_general(
        latent, res_expert, (((0,), (0,)), ((), ())), preferred_element_type=jnp.float32
    ).astype(jnp.bfloat16)
    partial_grad = lax.dot_general(
        res_expert, dec_local, (((1,), (1,)), ((), ())), preferred_element_type=jnp.float32
    )
    latent_grad = lax.psum(partial_grad, "width")
    slope = (latent_grad * silu_grad(preact)).astype(jnp.bfloat16)
    pre_grad = jnp.where(selected, slope, jnp.zeros((), jnp.bfloat16))
    grad_enc = lax.dot_general(
        expert_rows, pre_grad, (((0,), (0,)), ((), ())), preferred_element_type=jnp.float32
    )
    grad_enc = (grad_enc * scale_factor).astype(jnp.bfloat16)
    return (
        grad_enc.reshape(1, layers, width_dev, latents),
        grad_dec.reshape(1, latents, layers, width_dev),
    )


def solution(mesh):
    placed = (
        P("feat", None, "width"),
        P("feat", None, "width", None),
        P("feat", None),
        P("feat", None, None, "width"),
        P(None, "width"),
        P("feat", None),
        P("feat", None, None),
    )
    return jax.shard_map(
        per_device,
        mesh=mesh,
        in_specs=placed,
        out_specs=(P("feat", None, "width", None), P("feat", None, None, "width")),
        check_vma=False,
    )
```

profile of v0, /device:TPU:32, one launch (start us, length us, event | category | flops | bytes accessed | tf_op | source)
XLA Modules:
  0.0 573.4 jit_solution(9528535051465568450)
XLA Ops:
  7.2 0.8 broadcast_multiply_fusion
  8.0 0.8 copy.24
  8.9 0.1 eq.29
  9.0 0.1 eq.25
  9.3 0.1 mul.40
  9.5 1.2 reduce-window.6
  10.6 0.2 slice_reduce_fusion
  11.0 1.1 copy.33
  12.1 1.5 broadcast_in_dim.13
  13.6 2.2 reshape.172
  15.9 4.8 scatter_custom_fusion
  20.7 58.2 %all_to_all.20 = bf16[16,64,1024]{2,1,0:T(8,128)(2,1)S(1)} all-to-all(bf16[16,64,1024]{2,1,0:T(8,128)(2,1)} %bitcast.55), channel_id=1, replica_groups=mesh['width'=16,'feat'=16] {'feat'}, dimensions={0} | all-to-all | bytes 4194304 | tf_op jit(solution)/shard_map/all_to_all | solution.py:50
  78.9 1.4 copy-done.2
  80.2 4.3 fusion.16
  84.6 0.8 copy-done.6
  85.4 0.1 copy.27
  85.5 1.8 scatter_custom_fusion.1
  87.4 0.2 copy.28
  87.6 0.8 reshape.207
  88.4 5.8 %all-to-all-start.1 = ((s32[16,1,2048]{2,1,0:T(1,128)}), s32[16,1,2048]{2,1,0:T(1,128)S(1)}, u32[]{:S(2)}, u32[]{:S(2)}) async-start(s32[16,1,2048]{2,1,0:T(1,128)} %reshape.207), calls=%async_computation.1 | async-start | bytes 262144 | tf_op jit(solution)/shard_map/all_to_all | solution.py:57
  94.2 3.5 copy.34
  97.8 4.3 all-to-all-done.1
  102.1 0.5 broadcast.132
  102.6 0.9 reduce.6
  103.6 0.2 copy.29
  104.2 0.2 copy.30
  104.4 0.2 reshape.192
  104.6 138.0 %scatter_custom_fusion.3 = pred[1048576]{0:T(1024)(128)(4,1)} fusion(s32[32768]{0:T(1024)S(1)} %reshape.192, pred[32768]{0:T(1024)(128)(4,1)S(1)} %broadcast.102, pred[]{:T(512)} %constant.15.clone.1), kind=kCustom, calls=%fused_computation.11 | custom fusion | bytes 1048577
  242.6 3.9 reshape.158
  246.5 4.1 fusion.1
  250.7 3.7 convolution_convert_fusion.1
  254.3 7.3 %all-to-all-start.2 = ((bf16[16,64,1024]{2,1,0:T(8,128)(2,1)}), bf16[16,64,1024]{2,1,0:T(8,128)(2,1)}, u32[]{:S(2)}, u32[]{:S(2)}) async-start(bf16[16,64,1024]{2,1,0:T(8,128)(2,1)} %bitcast.66), calls=%async_computation.2 | async-start | bytes 4194304 | tf_op jit(solution)/shard_map/all_to_all | solution.py:73
  261.6 0.2 all-reduce.5.cloned.1.call-start
  261.9 46.5 %all-to-all-done.2 = bf16[16,64,1024]{2,1,0:T(8,128)(2,1)} async-done(((bf16[16,64,1024]{2,1,0:T(8,128)(2,1)}), bf16[16,64,1024]{2,1,0:T(8,128)(2,1)}, u32[]{:S(2)}, u32[]{:S(2)}) %all-to-all-start.2) | async-done | bytes 2097184 | tf_op jit(solution)/shard_map/all_to_all | solution.py:73
  308.4 5.3 gather_fusion
  313.7 3.3 reshape.159
  317.1 5.1 reduce_sum.19
  322.1 1.4 subtract_convert_fusion
  323.5 1.5 broadcast_in_dim.31
  325.0 2.3 reshape.188
  327.3 4.8 scatter_custom_fusion.2
  332.1 53.2 %all_to_all.21 = bf16[16,64,1024]{2,1,0:T(8,128)(2,1)S(1)} all-to-all(bf16[16,64,1024]{2,1,0:T(8,128)(2,1)} %bitcast.54), channel_id=1, replica_groups=mesh['width'=16,'feat'=16] {'feat'}, dimensions={0} | all-to-all | bytes 4194304 | tf_op jit(solution)/shard_map/all_to_all | solution.py:90
  385.3 1.3 copy-done.5
  386.6 4.3 fusion.17
  391.0 6.0 %convolution_convert_fusion = bf16[1024,1024]{0,1:T(8,128)(2,1)} fusion(bf16[1024,1024]{1,0:T(8,128)(2,1)} %copy-done.1, bf16[1024,1024]{1,0:T(8,128)(2,1)} %bitcast.65), kind=kOutput, calls=%fused_computation.13 | convolution fusion | flops 2148532224 | bytes 6291456 | tf_op jit(solution)/shard_map/dot_general | solution.py:97
  397.0 6.2 %copy.31 = bf16[1,1024,2,512]{3,2,1,0:T(2,128)(2,1)} copy(bf16[1,1024,2,512]{1,3,2,0:T(8,128)(2,1)} %bitcast.67) | data formatting | bytes 4194304
  403.1 154.8 %all-reduce.5.cloned.1.call-done = f32[1024,1024]{1,0:T(8,128)} async-done(((f32[1024,1024]{1,0:T(8,128)}), f32[1024,1024]{1,0:T(8,128)}) %all-reduce.5.cloned.1.call-update) | async-done | bytes 4194320 | tf_op jit(solution)/shard_map/psum | solution.py:103
  557.9 8.4 %multiply_convert_fusion = bf16[1024,1024]{1,0:T(8,128)(2,1)} fusion(bf16[1024,1024]{1,0:T(8,128)(2,1)} %bitcast.61, pred[1024,1024]{1,0:T(32,128)(4,1)} %reshape.158, f32[1024,1024]{1,0:T(8,128)} %all-reduce.5.cloned.1.call-done, f32[1024,1024]{1,0:T(8,128)} %all-reduce.3.cloned.1.call-done, f32[1024]{0:T(1024)S(1)} %bitcast.79), kind=kOutput, calls=%fused_computation.5 | convolution fusion | flops 2161115136 | bytes 13635584 | tf_op jit(solution)/shard_map/dot_general | solution.py:106
  (38 shorter events, 0.8 us)
Async XLA Ops:
  7.2 71.7 %copy-start = (bf16[1,2,512,1024]{3,2,1,0:T(8,128)(2,1)S(1)}, bf16[1,2,512,1024]{3,2,1,0:T(8,128)(2,1)}, u32[]{:S(2)}) copy-start(bf16[1,2,512,1024]{3,2,1,0:T(8,128)(2,1)} %param.8) | copy-start | bytes 6291460
  7.2 239.3 %all-reduce.3.cloned.1.call-start = ((), (), s32[]{:S(2)}) async-start(), calls=%async_computation.4 | async-start | bytes 8388608 | tf_op jit(solution)/shard_map/psum | solution.py:69
  78.8 1.4 copy-start.2
  84.5 0.8 copy-start.6
  88.4 13.7 %all-to-all-start.1 = ((s32[16,1,2048]{2,1,0:T(1,128)}), s32[16,1,2048]{2,1,0:T(1,128)S(1)}, u32[]{:S(2)}, u32[]{:S(2)}) async-start(s32[16,1,2048]{2,1,0:T(1,128)} %reshape.207), calls=%async_computation.1 | async-start | bytes 262144 | tf_op jit(solution)/shard_map/all_to_all | solution.py:57
  97.8 6.3 %copy-start.9 = (s32[2]{0:T(128)S(1)}, s32[2]{0:T(128)}, u32[]{:S(2)}) copy-start(s32[2]{0:T(128)} %constant.37) | copy-start | bytes 28
  104.2 142.3 %copy-start.7 = (f32[1,1024]{1,0:T(1,128)S(1)}, f32[1,1024]{1,0:T(1,128)}, u32[]{:S(2)}) copy-start(f32[1,1024]{1,0:T(1,128)} %param.9) | copy-start | bytes 12292
  246.5 4.2 copy-start.3
  250.6 3.7 copy-start.1
  254.3 7.6 %copy-start.8 = (f32[2,512]{1,0:T(2,128)S(1)}, f32[2,512]{1,0:T(2,128)}, u32[]{:S(2)}) copy-start(f32[2,512]{1,0:T(2,128)} %param.11) | copy-start | bytes 12292
  254.3 54.1 %all-to-all-start.2 = ((bf16[16,64,1024]{2,1,0:T(8,128)(2,1)}), bf16[16,64,1024]{2,1,0:T(8,128)(2,1)}, u32[]{:S(2)}, u32[]{:S(2)}) async-start(bf16[16,64,1024]{2,1,0:T(8,128)(2,1)} %bitcast.66), calls=%async_computation.2 | async-start | bytes 4194304 | tf_op jit(solution)/shard_map/all_to_all | solution.py:73
  261.6 296.3 %all-reduce.5.cloned.1.call-start = ((), (), s32[]{:S(2)}) async-start(), calls=%async_computation.5 | async-start | bytes 8388608 | tf_op jit(solution)/shard_map/psum | solution.py:103
  332.1 54.5 %copy-start.4 = (bf16[128,8,2,512]{3,1,2,0:T(8,128)(2,1)S(1)}, bf16[128,8,2,512]{3,1,2,0:T(8,128)(2,1)}, u32[]{:S(2)}) copy-start(bf16[128,8,2,512]{3,1,2,0:T(8,128)(2,1)} %copy.34) | copy-start | bytes 6291460
  385.3 1.3 copy-start.5
Sparse Core Ops, SparseCore 0:
  84.7 161.4 all-reduce.2
  391.1 166.7 all-reduce.4
where the time goes:
time: 581 us; the launch traced here: 573 us
  waiting for transfers between devices  206 us (35%)
  local copies, waits for them, and re-layouts  188 us (32%)
  blocking collectives  111 us (19%)
  matrix products  26.7 us (5%)
  between operations  14.5 us (2%)
  other arithmetic  13.8 us (2%)
  starting transfers between devices  13.4 us (2%)
    psum x1, waiting for transfers between devices, per_device(): latent_grad = lax.psum(partial_grad, 'width')  155 us
    unnamed x32, local copies, waits for them, and re-layouts  155 us
    all_to_all x1, blocking collectives, per_device(): lax.all_to_all(send_rows.reshape(groups, capacity, inner_width), 'feat',...  58.2 us
    all_to_all x1, blocking collectives, per_device(): lax.all_to_all(res_send.reshape(groups, capacity, inner_width), 'feat', s...  53.2 us
    all_to_all x1, waiting for transfers between devices, per_device(): lax.all_to_all(decoded.reshape(groups, capacity, inner_width), 'feat', sp...  46.5 us
  transfers between devices with their start and end apart: 4, of which 3 were waited for; matrix products, arithmetic and copies ran while one was open for 28% of the time, Pallas kernels for 0%

commit v1 on v0

v1 whole, which is shorter than its diff:
```python
import functools
import math

import jax
import jax.numpy as jnp
from jax import lax
from jax.experimental import pallas as pl
from jax.experimental.pallas import tpu as pltpu
from jax.sharding import PartitionSpec as P

D = 8192
L = 2
CAP = 64
GROUPS = 16
CHUNKS = (32, 32)
LANES = 128
KEPT = 32
PER = LANES // KEPT
BF16 = jnp.bfloat16
F32 = jnp.float32
I32 = jnp.int32
ROW_BLOCK = 256
VMEM_LIMIT = 48 * 1024 * 1024


def iota(shape, dim):
    return lax.broadcasted_iota(I32, shape, dim)


def params():
    return pltpu.CompilerParams(vmem_limit_bytes=VMEM_LIMIT)


def cost(flops, nbytes):
    return pl.CostEstimate(flops=int(flops), bytes_accessed=int(nbytes), transcendentals=0)


def whole():
    return pl.BlockSpec(memory_space=pltpu.VMEM)


def offsets():
    out, start = [], 0
    for cap in CHUNKS:
        out.append((start, cap))
        start += cap
    return out


def chunk_hits(info, off, cap, tokens):
    rows = iota((GROUPS * cap, tokens), 0)

    def slot(route, pos):
        inside = (pos >= off) & (pos < off + cap)
        return jnp.where(inside, route * cap + (pos - off), -1)

    return (rows == slot(info[0:1], info[1:2])) | (rows == slot(info[2:3], info[3:4]))


def pack_kernel(routes_ref, acts_ref, info_ref, *send_refs):
    tokens = routes_ref.shape[1]
    upper = (iota((tokens, tokens), 0) < iota((tokens, tokens), 1)).astype(F32).astype(BF16)
    experts = iota((GROUPS, tokens), 0)
    total = jnp.zeros((GROUPS, 1), F32)
    rows = []
    for j in range(2):
        route = routes_ref[j : j + 1, :]
        hit = experts == route
        hot = hit.astype(F32)
        before = jnp.dot(hot.astype(BF16), upper, preferred_element_type=F32) + total
        total = total + jnp.sum(hot, axis=1, keepdims=True)
        pos = jnp.sum(jnp.where(hit, before, 0.0), axis=0, keepdims=True).astype(I32)
        rows += [route, pos]
    info = jnp.concatenate(rows + [jnp.zeros((4, tokens), I32)], axis=0)
    info_ref[...] = info
    x = acts_ref[...]
    for (off, cap), send_ref in zip(offsets(), send_refs):
        hits = chunk_hits(info, off, cap, tokens).astype(F32).astype(BF16)
        send_ref[...] = jnp.dot(hits, x, preferred_element_type=F32).astype(BF16)


def pack(routes_t, x):
    tokens, width = x.shape
    return pl.pallas_call(
        pack_kernel,
        out_shape=(jax.ShapeDtypeStruct((8, tokens), I32),)
        + tuple(jax.ShapeDtypeStruct((GROUPS * c, width), BF16) for c in CHUNKS),
        in_specs=[whole(), whole()],
        out_specs=(whole(),) * (1 + len(CHUNKS)),
        compiler_params=params(),
        cost_estimate=cost(2 * GROUPS * CAP * tokens * width, 3 << 20),
        name="pack_tokens",
    )(routes_t, x)


def index_kernel(info_ref, index_ref, out_ref):
    tokens, cols = index_ref.shape
    index = index_ref[...]
    code = (((index & 127) + 128) << (index >> 7)).astype(F32).astype(BF16)
    info = info_ref[...]
    col = iota((cols, LANES), 0)
    lane = iota((cols, LANES), 1)
    rows_total = GROUPS * CAP // PER
    row = iota((rows_total, tokens), 0)
    per_group = CAP // PER
    expert, inner = row // per_group, row % per_group
    lane_q = iota((rows_total, LANES), 1) // KEPT
    result = jnp.zeros((rows_total, LANES), F32)
    for j in range(2):
        spread = (col == j * KEPT + lane % KEPT).astype(F32).astype(BF16)
        codes = jnp.dot(code, spread, preferred_element_type=F32).astype(BF16)
        key = info[2 * j : 2 * j + 1] * CAP + info[2 * j + 1 : 2 * j + 2]
        for q in range(PER):
            pos = jnp.zeros((rows_total, tokens), I32)
            for off, cap in offsets():
                here = (inner >= off // PER) & (inner < (off + cap) // PER)
                pos = jnp.where(here, off + (cap // PER) * q + inner - off // PER, pos)
            hit = (expert * CAP + pos == key).astype(F32).astype(BF16)
            picked = jnp.dot(hit, codes, preferred_element_type=F32)
            result = result + jnp.where(lane_q == q, picked, 0.0)
    out_ref[...] = result.astype(BF16)


def pack_index(info, index):
    return pl.pallas_call(
        index_kernel,
        out_shape=jax.ShapeDtypeStruct((GROUPS * CAP // PER, LANES), BF16),
        in_specs=[whole(), whole()],
        out_specs=whole(),
        compiler_params=params(),
        cost_estimate=cost(2 * 8 * 256 * 256 * 128, 1 << 18),
        name="pack_index",
    )(info, index)


def inverse_kernel(index_ref, low_ref, high_ref):
    packed_rows = index_ref.shape[1]
    lane = iota((8, LANES), 1)

    def step(g, carry):
        src = g // (packed_rows // 8)
        half = g % (packed_rows // 8)
        idx = index_ref[src, pl.ds(pl.multiple_of(half * 8, 8), 8), :]
        tile = idx >> 7
        low_word = jnp.where((tile >= 0) & (tile < 4), 1 << (jnp.clip(tile, 0, 3) * 6), 0)
        high_word = jnp.where(tile >= 4, 1 << (jnp.clip(tile - 4, 0, 3) * 6), 0)
        place = jnp.where(idx >= 0, idx & 127, -1)
        for q in range(PER):
            low = jnp.zeros((8, LANES), I32)
            high = jnp.zeros((8, LANES), I32)
            for k in range(KEPT):
                c = q * KEPT + k
                same = lane == place[:, c : c + 1]
                low = low + jnp.where(same, low_word[:, c : c + 1] * (k + 1), 0)
                high = high + jnp.where(same, high_word[:, c : c + 1] * (k + 1), 0)
            row = src * (packed_rows * PER) + q * packed_rows + half * 8
            row = pl.multiple_of(row, 8)
            low_ref[pl.ds(row, 8), :] = low
            high_ref[pl.ds(row, 8), :] = high
        return carry

    lax.fori_loop(0, GROUPS * packed_rows // 8, step, 0)


def inverse(index):
    rows = index.shape[0] * index.shape[1] * PER
    shape = jax.ShapeDtypeStruct((rows, LANES), I32)
    return pl.pallas_call(
        inverse_kernel,
        out_shape=(shape, shape),
        in_specs=[whole()],
        out_specs=(whole(), whole()),
        compiler_params=params(),
        cost_estimate=cost(rows * 2_000_000, 1 << 20),
        name="inverse_index",
    )(index)


def gather_kept(values_ref, index_ref, out_ref, groups, packed_rows):
    tiles = values_ref.shape[1] // LANES
    lane_q = iota((8, LANES), 1) // KEPT
    for src in range(groups):
        for half in range(packed_rows // 8):
            idx = index_ref[src, half * 8 : half * 8 + 8, :]
            spot, tile = idx & 127, idx >> 7
            result = jnp.zeros((8, LANES), F32)
            for q in range(PER):
                row = src * packed_rows * PER + q * packed_rows + half * 8
                here = jnp.where(lane_q == q, tile, -1)
                for t in range(tiles):
                    part = values_ref[row : row + 8, t * LANES : (t + 1) * LANES]
                    taken = jnp.take_along_axis(part, spot, axis=1, mode="promise_in_bounds")
                    result = jnp.where(here == t, taken, result)
            start = src * packed_rows + half * 8
            out_ref[start : start + 8, :] = result


def encode_kernel(x_ref, w_ref, bias_ref, index_ref, out_ref, values_ref):
    values_ref[...] = jnp.dot(x_ref[...], w_ref[...], preferred_element_type=F32) + bias_ref[...]
    gather_kept(values_ref, index_ref, out_ref, index_ref.shape[0], index_ref.shape[1])


def backproject_kernel(r_ref, w_ref, index_ref, out_ref, values_ref):
    values_ref[...] = lax.dot_general(
        r_ref[...], w_ref[...], (((1,), (1,)), ((), ())), preferred_element_type=F32
    )
    gather_kept(values_ref, index_ref, out_ref, index_ref.shape[0], index_ref.shape[1])


def kept_product(kernel, rows, weight, index, bias, name):
    total, inner = rows.shape
    latents = 1024
    packed_rows = index.shape[1]
    groups = ROW_BLOCK // (packed_rows * PER)
    operands = [rows, weight] + ([] if bias is None else [bias]) + [index]
    specs = [
        pl.BlockSpec((ROW_BLOCK, inner), lambda i: (i, 0)),
        pl.BlockSpec(weight.shape, lambda i: (0, 0)),
    ]
    if bias is not None:
        specs.append(pl.BlockSpec(bias.shape, lambda i: (0, 0)))
    specs.append(pl.BlockSpec((groups, packed_rows, LANES), lambda i: (i, 0, 0)))
    return pl.pallas_call(
        kernel,
        grid=(total // ROW_BLOCK,),
        out_shape=jax.ShapeDtypeStruct((total // PER, LANES), F32),
        in_specs=specs,
        out_specs=pl.BlockSpec((ROW_BLOCK // PER, LANES), lambda i: (i, 0)),
        scratch_shapes=[pltpu.VMEM((ROW_BLOCK, latents), F32)],
        compiler_params=params(),
        cost_estimate=cost(4 * total * inner * latents, 4 << 20),
        name=name,
    )(*operands)


def spread_kept(kept_ref, low_ref, high_ref, dense_ref, groups, packed_rows):
    for src in range(groups):
        for half in range(packed_rows // 8):
            start = src * packed_rows + half * 8
            kept = kept_ref[start : start + 8, :]
            for q in range(PER):
                row = src * packed_rows * PER + q * packed_rows + half * 8
                words = (low_ref[row : row + 8, :], high_ref[row : row + 8, :])
                for t in range(8):
                    place = (words[t // 4] >> (6 * (t % 4))) & 63
                    spot = jnp.maximum(place - 1, 0) + q * KEPT
                    taken = jnp.take_along_axis(kept, spot, axis=1, mode="promise_in_bounds")
                    dense_ref[row : row + 8, t * LANES : (t + 1) * LANES] = jnp.where(
                        place > 0, taken, 0.0
                    )


def decode_kernel(packed_rows, pre_ref, low_ref, high_ref, w_ref, latent_ref, out_ref, kept_ref, dense_ref):
    pre = pre_ref[...]
    kept_ref[...] = (pre / (1.0 + jnp.exp(-pre))).astype(BF16).astype(F32)
    spread_kept(kept_ref, low_ref, high_ref, dense_ref, ROW_BLOCK // (packed_rows * PER), packed_rows)
    latent = dense_ref[...].astype(BF16)
    latent_ref[...] = latent
    out_ref[...] = jnp.dot(latent, w_ref[...], preferred_element_type=F32).astype(BF16)


def decode(pre, low, high, weight, packed_rows):
    total = low.shape[0]
    latents, inner = weight.shape
    by_row = lambda i: (i, 0)
    return pl.pallas_call(
        functools.partial(decode_kernel, packed_rows),
        grid=(total // ROW_BLOCK,),
        out_shape=(
            jax.ShapeDtypeStruct((total, latents), BF16),
            jax.ShapeDtypeStruct((total, inner), BF16),
        ),
        in_specs=[
            pl.BlockSpec((ROW_BLOCK // PER, LANES), by_row),
            pl.BlockSpec((ROW_BLOCK, LANES), by_row),
            pl.BlockSpec((ROW_BLOCK, LANES), by_row),
            pl.BlockSpec(weight.shape, lambda i: (0, 0)),
        ],
        out_specs=(
            pl.BlockSpec((ROW_BLOCK, latents), by_row),
            pl.BlockSpec((ROW_BLOCK, inner), by_row),
        ),
        scratch_shapes=[
            pltpu.VMEM((ROW_BLOCK // PER, LANES), F32),
            pltpu.VMEM((ROW_BLOCK, latents), F32),
        ],
        compiler_params=params(),
        cost_estimate=cost(4 * total * inner * latents, 6 << 20),
        name="decode",
    )(pre, low, high, weight)


def residual_kernel(*refs):
    count = len(CHUNKS)
    info_ref, x_ref, bias_ref = refs[:3]
    back_refs, send_refs = refs[3 : 3 + count], refs[3 + count :]
    tokens = x_ref.shape[0]
    info = info_ref[...]
    hits = [chunk_hits(info, off, cap, tokens).astype(F32).astype(BF16) for off, cap in offsets()]
    total = jnp.zeros(x_ref.shape, F32)
    for hit, back_ref in zip(hits, back_refs):
        total = total + lax.dot_general(
            hit, back_ref[...], (((0,), (0,)), ((), ())), preferred_element_type=F32
        )
    residual = (total + bias_ref[...] - x_ref[...].astype(F32)).astype(BF16)
    for hit, send_ref in zip(hits, send_refs):
        send_ref[...] = jnp.dot(hit, residual, preferred_element_type=F32).astype(BF16)


def form_residual(info, x, bias, back):
    tokens, width = x.shape
    return pl.pallas_call(
        residual_kernel,
        out_shape=tuple(jax.ShapeDtypeStruct((GROUPS * c, width), BF16) for c in CHUNKS),
        in_specs=[whole()] * (3 + len(CHUNKS)),
        out_specs=(whole(),) * len(CHUNKS),
        compiler_params=params(),
        cost_estimate=cost(4 * GROUPS * CAP * tokens * width, 5 << 20),
        name="form_residual",
    )(info, x, bias, *back)


def encoder_grad_kernel(chunk, scale, first, lg_ref, pre_ref, low_ref, high_ref, xt_ref, out_ref, kept_ref, dense_ref, acc_ref):
    step = pl.program_id(0)
    pre = pre_ref[...]
    sig = 1.0 / (1.0 + jnp.exp(-pre))
    slope = lg_ref[...] * (sig * (1.0 + pre * (1.0 - sig)))
    kept_ref[...] = slope.astype(BF16).astype(F32)
    packed_rows = chunk // PER
    spread_kept(kept_ref, low_ref, high_ref, dense_ref, ROW_BLOCK // chunk, packed_rows)
    part = jnp.dot(xt_ref[...], dense_ref[...].astype(BF16), preferred_element_type=F32)

    @pl.when(step == 0)
    def _():
        acc_ref[...] = part

    @pl.when(step > 0)
    def _():
        acc_ref[...] += part

    @pl.when(step == pl.num_programs(0) - 1)
    def _():
        out_ref[...] = (acc_ref[...] * scale).astype(BF16)


def encoder_grad(lg, pre, low, high, x_t, chunk, scale):
    total = low.shape[0]
    inner, latents = x_t.shape[0], 1024
    by_row = lambda i: (i, 0)
    return pl.pallas_call(
        functools.partial(encoder_grad_kernel, chunk, scale, 0),
        grid=(total // ROW_BLOCK,),
        out_shape=jax.ShapeDtypeStruct((inner, latents), BF16),
        in_specs=[
            pl.BlockSpec((ROW_BLOCK // PER, LANES), by_row),
            pl.BlockSpec((ROW_BLOCK // PER, LANES), by_row),
            pl.BlockSpec((ROW_BLOCK, LANES), by_row),
            pl.BlockSpec((ROW_BLOCK, LANES), by_row),
            pl.BlockSpec((inner, ROW_BLOCK), lambda i: (0, i)),
        ],
        out_specs=pl.BlockSpec((inner, latents), lambda i: (0, 0)),
        scratch_shapes=[
            pltpu.VMEM((ROW_BLOCK // PER, LANES), F32),
            pltpu.VMEM((ROW_BLOCK, latents), F32),
            pltpu.VMEM((inner, latents), F32),
        ],
        compiler_params=params(),
        cost_estimate=cost(4 * total * inner * latents, 6 << 20),
        name="encoder_grad",
    )(lg, pre, low, high, x_t)


def exchange(rows):
    count, width = rows.shape
    return lax.all_to_all(
        rows.reshape(GROUPS, count // GROUPS, width), "feat", split_axis=0, concat_axis=0, tiled=True
    ).reshape(count, width)


def width_sum(part):
    size = lax.axis_size("width")
    bit = 1
    while bit < size:
        part = part + lax.ppermute(part, "width", [(a, a ^ bit) for a in range(size)])
        bit *= 2
    return part


def decode_index(codes):
    code = codes.astype(F32).astype(I32)
    tile = sum((code >= (256 << h)).astype(I32) for h in range(7))
    spot = (code >> tile) - 128
    return jnp.where(code > 0, tile * 128 + spot, -1)


def per_device(acts, enc_weight, enc_bias, dec_weight, dec_bias, routes, latent_index):
    tokens, layers, width_dev = acts.shape
    inner = layers * width_dev
    latents = enc_weight.shape[3]
    scale = 1.0 / math.sqrt(L * D)
    x_home = acts.reshape(tokens, inner)
    enc = enc_weight.reshape(inner, latents)
    dec = dec_weight.reshape(latents, inner)
    bias = jnp.where(lax.axis_index("width") == 0, enc_bias, 0.0)

    info, *sends = pack(routes.T, x_home)
    arrived = [exchange(sends[0])]
    codes = pack_index(info, latent_index.reshape(tokens, 2 * KEPT))
    index = decode_index(exchange(codes)).reshape(GROUPS, CAP // PER, LANES)
    arrived += [exchange(s) for s in sends[1:]]
    index_of = [index[:, off // PER : (off + cap) // PER] for off, cap in offsets()]
    maps = [inverse(i) for i in index_of]

    pre, latent, back = [], [], []
    for c, cap in enumerate(CHUNKS):
        part = kept_product(encode_kernel, arrived[c], enc, index_of[c], bias, "encode")
        pre.append(width_sum(part))
        lat, decoded = decode(pre[c], *maps[c], dec, cap // PER)
        latent.append(lat)
        back.append(exchange(decoded))

    outgoing = form_residual(info, x_home, dec_bias.reshape(1, inner), back)
    res = [exchange(o) for o in outgoing]
    slopes = []
    for c in range(len(CHUNKS)):
        part = kept_product(backproject_kernel, res[c], dec, index_of[c], None, "latent_gradient")
        slopes.append(width_sum(part))
    grad_dec = lax.dot_general(
        jnp.concatenate(latent, axis=0),
        jnp.concatenate(res, axis=0),
        (((0,), (0,)), ((), ())),
        preferred_element_type=F32,
    ).astype(BF16)
    x_t = jnp.concatenate(arrived, axis=0).T
    grad_enc = encoder_grad(
        jnp.concatenate(slopes, axis=0),
        jnp.concatenate(pre, axis=0),
        jnp.concatenate([m[0] for m in maps], axis=0),
        jnp.concatenate([m[1] for m in maps], axis=0),
        x_t,
        CHUNKS[0],
        scale,
    )
    return (
        grad_enc.reshape(1, layers, width_dev, latents),
        grad_dec.reshape(1, latents, layers, width_dev),
    )


def solution(mesh):
    placed = (
        P("feat", None, "width"),
        P("feat", None, "width", None),
        P("feat", None),
        P("feat", None, None, "width"),
        P(None, "width"),
        P("feat", None),
        P("feat", None, None),
    )
    return jax.shard_map(
        per_device,
        mesh=mesh,
        in_specs=placed,
        out_specs=(P("feat", None, "width", None), P("feat", None, None, "width")),
        check_vma=False,
    )
```

time: 581 us -> 286 us (0.49); the launches traced: 573 us -> 285 us
  local copies, waits for them, and re-layouts: 188 us -> 27.5 us
  waiting for transfers between devices: 206 us -> 65.2 us
  Pallas kernels: 0 us -> 49.6 us
  starting transfers between devices: 13.4 us -> 54.1 us
  blocking collectives: 111 us -> 75.2 us
  matrix products: 26.7 us -> 5.01 us
  between operations: 14.5 us -> 1.06 us
  other arithmetic: 13.8 us -> 7.36 us
    psum x2 -> x0, waiting for transfers between devices: 155 us -> none  [the longest x1 155 us: per_device(): latent_grad = lax.psum(partial_grad, 'width')]
    unnamed x32 -> x66, local copies, waits for them, and re-layouts: 155 us -> 23.9 us
    pallas_call x0 -> x12, Pallas kernels: none -> 49.6 us  [the longest x2 21.6 us: inverse(): pl.pallas_call(inverse_kernel, out_shape=(shape, shape), in_specs=[whole(...]
    all_to_all x2 -> x3, blocking collectives: 111 us -> 75.2 us  [exchange(): lax.all_to_all(rows.reshape(GROUPS, count // GROUPS, width), 'feat', spli...]
    ppermute x0 -> x16, starting transfers between devices: none -> 30 us  [width_sum(): lax.ppermute(part, 'width', [(a, a ^ bit) for a in range(size)])]
    dot_general x5 -> x1, matrix products: 26.7 us -> 5.01 us  [per_device(): lax.dot_general(jnp.concatenate(latent, axis=0), jnp.concatenate(res, axi...]
    ppermute x0 -> x16, waiting for transfers between devices: none -> 20 us  [width_sum(): lax.ppermute(part, 'width', [(a, a ^ bit) for a in range(size)])]
    scatter x4 -> x0, local copies, waits for them, and re-layouts: 15.3 us -> none  [the longest x1 4.79 us: per_device(): jnp.zeros((slot_count, inner_width), acts.dtype).at[slot_of].set(token_rows)]
  transfers between devices with their start and end apart: 4 -> 20, of which waited for: 3 -> 9; matrix products, arithmetic and copies ran while one was open for 28% -> 7% of each run, Pallas kernels for 0% -> 11%
where the time goes in v1:
time: 286 us; the launch traced here: 285 us
  blocking collectives  75.2 us (26%)
  waiting for transfers between devices  65.2 us (23%)
  starting transfers between devices  54.1 us (19%)
  Pallas kernels  49.6 us (17%)
  local copies, waits for them, and re-layouts  27.5 us (10%)
  other arithmetic  7.36 us (3%)
  matrix products  5.01 us (2%)
    all_to_all x3, blocking collectives, exchange(): lax.all_to_all(rows.reshape(GROUPS, count // GROUPS, width), 'feat', spli...  75.2 us
    all_to_all x4, waiting for transfers between devices, exchange(): lax.all_to_all(rows.reshape(GROUPS, count // GROUPS, width), 'feat', spli...  45.2 us
    ppermute x16, starting transfers between devices, width_sum(): lax.ppermute(part, 'width', [(a, a ^ bit) for a in range(size)])  30 us
    all_to_all x4, starting transfers between devices, exchange(): lax.all_to_all(rows.reshape(GROUPS, count // GROUPS, width), 'feat', spli...  24 us
    unnamed x66, local copies, waits for them, and re-layouts  23.9 us
    pallas_call x2, Pallas kernels, inverse(): pl.pallas_call(inverse_kernel, out_shape=(shape, shape), in_specs=[whole(...  21.6 us
    ppermute x16, waiting for transfers between devices, width_sum(): lax.ppermute(part, 'width', [(a, a ^ bit) for a in range(size)])  20 us
    pallas_call x4, Pallas kernels, kept_product(): pl.pallas_call(kernel, grid=(total // ROW_BLOCK,), out_shape=jax.ShapeDty...  9.48 us
  transfers between devices with their start and end apart: 20, of which 9 were waited for; matrix products, arithmetic and copies ran while one was open for 7% of the time, Pallas kernels for 11%

profile of v1, /device:TPU:32, one launch (start us, length us, event | category | flops | bytes accessed | tf_op | source)
XLA Modules:
  0.0 285.0 jit_solution(12997018854966660723)
XLA Ops:
  1.6 1.1 copy.19
  3.4 1.8 pack_tokens.1
  6.0 16.9 %all_to_all.35 = bf16[16,16,128]{2,1,0:T(8,128)(2,1)S(1)} all-to-all(bf16[16,16,128]{2,1,0:T(8,128)(2,1)S(1)} %bitcast.46), channel_id=1, replica_groups=mesh['width'=16,'feat'=16] {'feat'}, dimensions={0} | all-to-all | bytes 131072 | tf_op jit(solution)/shard_map/all_to_all | solution.py:375
  22.9 28.9 %all_to_all.36 = bf16[16,32,1024]{2,1,0:T(8,128)(2,1)S(1)} all-to-all(bf16[16,32,1024]{2,1,0:T(8,128)(2,1)S(1)} %bitcast.42), channel_id=1, replica_groups=mesh['width'=16,'feat'=16] {'feat'}, dimensions={0} | all-to-all | bytes 2097152 | tf_op jit(solution)/shard_map/all_to_all | solution.py:375
  51.8 5.1 %all-to-all-start.3 = ((bf16[16,32,1024]{2,1,0:T(8,128)(2,1)}), bf16[16,32,1024]{2,1,0:T(8,128)(2,1)S(1)}, u32[]{:S(2)}, u32[]{:S(2)}) async-start(bf16[16,32,1024]{2,1,0:T(8,128)(2,1)} %bitcast.8), calls=%async_computation.3 | async-start | bytes 2097152 | tf_op jit(solution)/shard_map/all_to_all | solution.py:375
  57.1 1.6 copy-done.21
  58.7 1.8 encode.2
  60.6 1.2 collective-permute-done
  61.8 2.8 collective-permute-start.1
  64.7 5.4 %collective-permute-done.1 = f32[128,128]{1,0:T(8,128)S(1)} collective-permute-done((f32[128,128]{1,0:T(8,128)S(1)}, f32[128,128]{1,0:T(8,128)S(1)}, u32[]{:S(2)}, u32[]{:S(2)}) %collective-permute-start.1) | collective-permute-done | bytes 65568 | tf_op jit(solution)/shard_map/ppermute | solution.py:384
  70.1 1.7 collective-permute-start.2
  72.3 2.1 collective-permute-done.2
  74.4 3.3 %collective-permute-start.3 = (f32[128,128]{1,0:T(8,128)S(1)}, f32[128,128]{1,0:T(8,128)S(1)}, u32[]{:S(2)}, u32[]{:S(2)}) collective-permute-start(f32[128,128]{1,0:T(8,128)S(1)} %add.87), channel_id=1, source_target_pairs={{0,128},{16,144},{32,160},{48,176},{64,192},{80,208},{96,224},{112... | collective-permute-start | bytes 196616 | tf_op jit(solution)/shard_map/ppermute | solution.py:384
  77.7 10.8 %inverse_index.2 = (s32[512,128]{1,0:T(8,128)S(1)}, s32[512,128]{1,0:T(8,128)S(1)}) custom-call(s32[16,8,128]{2,1,0:T(8,128)S(1)} %get-tuple-element.33.index_ref), custom_call_target="tpu_custom_call" | custom-call | flops 1024000000 | bytes 1048576 | tf_op jit(solution)/shard_map/inverse_index/pallas_call | solution.py:168
  88.6 2.5 decode.2
  93.8 6.4 %all-to-all-start.2 = ((bf16[16,32,1024]{2,1,0:T(8,128)(2,1)}), bf16[16,32,1024]{2,1,0:T(8,128)(2,1)S(1)}, u32[]{:S(2)}, u32[]{:S(2)}) async-start(bf16[16,32,1024]{2,1,0:T(8,128)(2,1)} %bitcast.39), calls=%async_computation.2 | async-start | bytes 2097152 | tf_op jit(solution)/shard_map/all_to_all | solution.py:375
  100.2 1.6 copy-done.22
  101.7 1.8 encode.3
  103.6 1.2 collective-permute-done.4
  104.9 3.1 %collective-permute-start.5 = (f32[128,128]{1,0:T(8,128)S(1)}, f32[128,128]{1,0:T(8,128)S(1)}, u32[]{:S(2)}, u32[]{:S(2)}) collective-permute-start(f32[128,128]{1,0:T(8,128)S(1)} %add.89), channel_id=1, source_target_pairs={{0,32},{16,48},{32,0},{48,16},{64,96},{80,112},{96,64},{112,80},{1... | collective-permute-start | bytes 196616 | tf_op jit(solution)/shard_map/ppermute | solution.py:384
  107.9 5.1 %collective-permute-done.5 = f32[128,128]{1,0:T(8,128)S(1)} collective-permute-done((f32[128,128]{1,0:T(8,128)S(1)}, f32[128,128]{1,0:T(8,128)S(1)}, u32[]{:S(2)}, u32[]{:S(2)}) %collective-permute-start.5) | collective-permute-done | bytes 65568 | tf_op jit(solution)/shard_map/ppermute | solution.py:384
  113.0 1.4 collective-permute-start.6
  114.5 2.9 %collective-permute-done.6 = f32[128,128]{1,0:T(8,128)S(1)} collective-permute-done((f32[128,128]{1,0:T(8,128)S(1)}, f32[128,128]{1,0:T(8,128)S(1)}, u32[]{:S(2)}, u32[]{:S(2)}) %collective-permute-start.6) | collective-permute-done | bytes 65568 | tf_op jit(solution)/shard_map/ppermute | solution.py:384
  118.2 10.8 %inverse_index.3 = (s32[512,128]{1,0:T(8,128)S(1)}, s32[512,128]{1,0:T(8,128)S(1)}) custom-call(s32[16,8,128]{2,1,0:T(8,128)S(1)} %get-tuple-element.32.index_ref), custom_call_target="tpu_custom_call" | custom-call | flops 1024000000 | bytes 1048576 | tf_op jit(solution)/shard_map/inverse_index/pallas_call | solution.py:168
  129.1 2.5 decode.3
  134.9 7.4 %all-to-all-start.4 = ((bf16[16,32,1024]{2,1,0:T(8,128)(2,1)}), bf16[16,32,1024]{2,1,0:T(8,128)(2,1)}, u32[]{:S(2)}, u32[]{:S(2)}) async-start(bf16[16,32,1024]{2,1,0:T(8,128)(2,1)} %bitcast.41), calls=%async_computation.4 | async-start | bytes 2097152 | tf_op jit(solution)/shard_map/all_to_all | solution.py:375
  142.4 24.7 %all-to-all-done.4 = bf16[16,32,1024]{2,1,0:T(8,128)(2,1)} async-done(((bf16[16,32,1024]{2,1,0:T(8,128)(2,1)}), bf16[16,32,1024]{2,1,0:T(8,128)(2,1)}, u32[]{:S(2)}, u32[]{:S(2)}) %all-to-all-start.4) | async-done | bytes 1048608 | tf_op jit(solution)/shard_map/all_to_all | solution.py:375
  168.2 2.6 form_residual.1
  170.8 29.5 %all_to_all.37 = bf16[16,32,1024]{2,1,0:T(8,128)(2,1)S(1)} all-to-all(bf16[16,32,1024]{2,1,0:T(8,128)(2,1)S(1)} %bitcast.43), channel_id=1, replica_groups=mesh['width'=16,'feat'=16] {'feat'}, dimensions={0} | all-to-all | bytes 2097152 | tf_op jit(solution)/shard_map/all_to_all | solution.py:375
  200.3 5.1 %all-to-all-start.5 = ((bf16[16,32,1024]{2,1,0:T(8,128)(2,1)}), bf16[16,32,1024]{2,1,0:T(8,128)(2,1)}, u32[]{:S(2)}, u32[]{:S(2)}) async-start(bf16[16,32,1024]{2,1,0:T(8,128)(2,1)} %bitcast.40), calls=%async_computation.5 | async-start | bytes 2097152 | tf_op jit(solution)/shard_map/all_to_all | solution.py:375
  205.4 1.6 copy-done.2
  207.9 2.4 latent_gradient.3
  210.3 20.4 %all-to-all-done.5 = bf16[16,32,1024]{2,1,0:T(8,128)(2,1)} async-done(((bf16[16,32,1024]{2,1,0:T(8,128)(2,1)}), bf16[16,32,1024]{2,1,0:T(8,128)(2,1)}, u32[]{:S(2)}, u32[]{:S(2)}) %all-to-all-start.5) | async-done | bytes 1048608 | tf_op jit(solution)/shard_map/all_to_all | solution.py:375
  230.7 1.6 copy-done.3
  233.2 3.6 %latent_gradient.2 = f32[128,128]{1,0:T(8,128)} custom-call(bf16[512,1024]{1,0:T(8,128)(2,1)} %bitcast.13.r_ref, bf16[1024,1024]{1,0:T(8,128)(2,1)S(1)} %bitcast.35, s32[16,8,128]{2,1,0:T(8,128)S(1)} %copy-done.18), custom_call_target="tpu_custom_call" | custom-call | flops 2147483648 | bytes 4194304 | tf_op jit(solution)/shard_map/latent_gradient/pallas_call | solution.py:223
  237.2 1.1 pad_add_fusion
  238.3 1.3 copy.17
  239.6 1.3 copy.16
  241.8 4.1 %collective-permute-start.9 = (f32[128,128]{1,0:T(8,128)S(1)}, f32[128,128]{1,0:T(8,128)S(1)}, u32[]{:S(2)}, u32[]{:S(2)}) collective-permute-start(f32[128,128]{1,0:T(8,128)S(1)} %add.93), channel_id=1, source_target_pairs={{0,32},{16,48},{32,0},{48,16},{64,96},{80,112},{96,64},{112,80},{1... | collective-permute-start | bytes 196616 | tf_op jit(solution)/shard_map/ppermute | solution.py:384
  246.9 1.9 maximum_bitcast_fusion.xt_ref
  248.8 1.8 collective-permute-start.10
  250.6 2.0 collective-permute-done.13
  252.6 1.8 collective-permute-start.14
  254.4 6.5 %collective-permute-start.11 = (f32[128,128]{1,0:T(8,128)S(1)}, f32[128,128]{1,0:T(8,128)}, u32[]{:S(2)}, u32[]{:S(2)}) collective-permute-start(f32[128,128]{1,0:T(8,128)S(1)} %add.95), channel_id=1, source_target_pairs={{0,128},{16,144},{32,160},{48,176},{64,192},{80,208},{96,224},{112... | collective-permute-start | bytes 196616 | tf_op jit(solution)/shard_map/ppermute | solution.py:384
  261.5 2.1 collective-permute-start.15
  263.7 5.0 %fusion.7 = bf16[1024,1024]{0,1:T(8,128)(2,1)} fusion(bf16[512,1024]{1,0:T(8,128)(2,1)S(1)} %bitcast.37, bf16[512,1024]{1,0:T(8,128)(2,1)} %bitcast.13.r_ref, bf16[512,1024]{1,0:T(8,128)(2,1)S(1)} %copy-done.27, bf16[512,1024]{1,0:T(8,128)(2,1)S(1)} %copy-done.25), kind=kOutput, calls=%fused_computation.8 | convolution fusion | flops 2156920832 | bytes 6291456 | tf_op jit(solution)/shard_map/dot_general | solution.py:428
  268.7 6.2 %copy.18 = bf16[1,1024,2,512]{3,2,1,0:T(2,128)(2,1)} copy(bf16[1,1024,2,512]{1,3,2,0:T(8,128)(2,1)} %bitcast.52) | data formatting | bytes 4194304
  276.7 8.3 %encoder_grad.1 = bf16[1024,1024]{1,0:T(8,128)(2,1)} custom-call(f32[256,128]{1,0:T(8,128)S(1)} %pad_maximum_fusion.lg_ref, f32[256,128]{1,0:T(8,128)S(1)} %pad_maximum_fusion.1.pre_ref, s32[1024,128]{1,0:T(8,128)S(1)} %copy-done.9, s32[1024,128]{1,0:T(8,128)S(1)} %copy-done.10, bf16[1024,1024]{1,0:T(8,128)(2,1)S(1)} %maximum_bitcast_fusion.xt_ref), custom_call_target="tpu_custom_call" | custom-call | flops 4294967296 | bytes 6291456 | tf_op jit(solution)/shard_map/encoder_grad/pallas_call | solution.py:350
  (100 shorter events, 17.9 us)
Async XLA Ops:
  2.7 49.1 %copy-start.7 = (bf16[32,8,2,512]{3,1,2,0:T(8,128)(2,1)}, bf16[32,8,2,512]{3,1,2,0:T(8,128)(2,1)S(1)}, u32[]{:S(2)}) copy-start(bf16[32,8,2,512]{3,1,2,0:T(8,128)(2,1)S(1)} %copy.19) | copy-start | bytes 1572868
  22.9 34.0 %copy-start.29 = (f32[1,1024]{1,0:T(1,128)S(1)}, f32[1,1024]{1,0:T(1,128)}, u32[]{:S(2)}) copy-start(f32[1,1024]{1,0:T(1,128)} %param.9) | copy-start | bytes 12292
  51.8 42.0 %all-to-all-start.3 = ((bf16[16,32,1024]{2,1,0:T(8,128)(2,1)}), bf16[16,32,1024]{2,1,0:T(8,128)(2,1)S(1)}, u32[]{:S(2)}, u32[]{:S(2)}) async-start(bf16[16,32,1024]{2,1,0:T(8,128)(2,1)} %bitcast.8), calls=%async_computation.3 | async-start | bytes 2097152 | tf_op jit(solution)/shard_map/all_to_all | solution.py:375
  57.1 20.6 %copy-start.17 = (s32[16,8,128]{2,1,0:T(8,128)}, s32[16,8,128]{2,1,0:T(8,128)S(1)}, u32[]{:S(2)}) copy-start(s32[16,8,128]{2,1,0:T(8,128)S(1)} %get-tuple-element.33.index_ref) | copy-start | bytes 196612
  57.1 61.1 %copy-start.19 = (s32[16,8,128]{2,1,0:T(8,128)}, s32[16,8,128]{2,1,0:T(8,128)S(1)}, u32[]{:S(2)}) copy-start(s32[16,8,128]{2,1,0:T(8,128)S(1)} %get-tuple-element.32.index_ref) | copy-start | bytes 196612
  57.1 1.6 copy-start.21
  58.7 13.0 %copy-start.28 = (bf16[1,1024,2,512]{3,2,1,0:T(2,128)(2,1)S(1)}, bf16[1,1024,2,512]{3,2,1,0:T(2,128)(2,1)}, u32[]{:S(2)}) copy-start(bf16[1,1024,2,512]{3,2,1,0:T(2,128)(2,1)} %param.10) | copy-start | bytes 6291460
  60.5 1.3 collective-permute-start
  61.8 8.2 %collective-permute-start.1 = (f32[128,128]{1,0:T(8,128)S(1)}, f32[128,128]{1,0:T(8,128)S(1)}, u32[]{:S(2)}, u32[]{:S(2)}) collective-permute-start(f32[128,128]{1,0:T(8,128)S(1)} %add.85), channel_id=1, source_target_pairs={{0,32},{16,48},{32,0},{48,16},{64,96},{80,112},{96,64},{112,80},{1... | collective-permute-start | bytes 196616 | tf_op jit(solution)/shard_map/ppermute | solution.py:384
  70.1 4.4 %collective-permute-start.2 = (f32[128,128]{1,0:T(8,128)S(1)}, f32[128,128]{1,0:T(8,128)S(1)}, u32[]{:S(2)}, u32[]{:S(2)}) collective-permute-start(f32[128,128]{1,0:T(8,128)S(1)} %add.86), channel_id=1, source_target_pairs={{0,64},{16,80},{32,96},{48,112},{64,0},{80,16},{96,32},{112,48},{1... | collective-permute-start | bytes 196616 | tf_op jit(solution)/shard_map/ppermute | solution.py:384
  72.3 16.2 %copy-start = (bf16[128,8,2,512]{3,1,2,0:T(8,128)(2,1)}, bf16[128,8,2,512]{3,1,2,0:T(8,128)(2,1)S(1)}, u32[]{:S(2)}) copy-start(bf16[128,8,2,512]{3,1,2,0:T(8,128)(2,1)S(1)} %copy.21) | copy-start | bytes 6291460
  74.4 14.1 %collective-permute-start.3 = (f32[128,128]{1,0:T(8,128)S(1)}, f32[128,128]{1,0:T(8,128)S(1)}, u32[]{:S(2)}, u32[]{:S(2)}) collective-permute-start(f32[128,128]{1,0:T(8,128)S(1)} %add.87), channel_id=1, source_target_pairs={{0,128},{16,144},{32,160},{48,176},{64,192},{80,208},{96,224},{112... | collective-permute-start | bytes 196616 | tf_op jit(solution)/shard_map/ppermute | solution.py:384
  91.1 1.0 copy-start.4
  92.8 1.0 copy-start.24
  93.8 41.1 %all-to-all-start.2 = ((bf16[16,32,1024]{2,1,0:T(8,128)(2,1)}), bf16[16,32,1024]{2,1,0:T(8,128)(2,1)S(1)}, u32[]{:S(2)}, u32[]{:S(2)}) async-start(bf16[16,32,1024]{2,1,0:T(8,128)(2,1)} %bitcast.39), calls=%async_computation.2 | async-start | bytes 2097152 | tf_op jit(solution)/shard_map/all_to_all | solution.py:375
  100.2 1.6 copy-start.22
  103.5 1.3 collective-permute-start.4
  104.9 8.2 %collective-permute-start.5 = (f32[128,128]{1,0:T(8,128)S(1)}, f32[128,128]{1,0:T(8,128)S(1)}, u32[]{:S(2)}, u32[]{:S(2)}) collective-permute-start(f32[128,128]{1,0:T(8,128)S(1)} %add.89), channel_id=1, source_target_pairs={{0,32},{16,48},{32,0},{48,16},{64,96},{80,112},{96,64},{112,80},{1... | collective-permute-start | bytes 196616 | tf_op jit(solution)/shard_map/ppermute | solution.py:384
  113.0 16.0 %copy-start.1 = (bf16[128,8,2,512]{3,1,2,0:T(8,128)(2,1)S(1)}, bf16[128,8,2,512]{3,1,2,0:T(8,128)(2,1)}, u32[]{:S(2)}) copy-start(bf16[128,8,2,512]{3,1,2,0:T(8,128)(2,1)} %copy-done) | copy-start | bytes 6291460
  113.0 4.4 %collective-permute-start.6 = (f32[128,128]{1,0:T(8,128)S(1)}, f32[128,128]{1,0:T(8,128)S(1)}, u32[]{:S(2)}, u32[]{:S(2)}) collective-permute-start(f32[128,128]{1,0:T(8,128)S(1)} %add.90), channel_id=1, source_target_pairs={{0,64},{16,80},{32,96},{48,112},{64,0},{80,16},{96,32},{112,48},{1... | collective-permute-start | bytes 196616 | tf_op jit(solution)/shard_map/ppermute | solution.py:384
  117.4 11.6 %collective-permute-start.7 = (f32[128,128]{1,0:T(8,128)S(1)}, f32[128,128]{1,0:T(8,128)S(1)}, u32[]{:S(2)}, u32[]{:S(2)}) collective-permute-start(f32[128,128]{1,0:T(8,128)S(1)} %add.91), channel_id=1, source_target_pairs={{0,128},{16,144},{32,160},{48,176},{64,192},{80,208},{96,224},{112... | collective-permute-start | bytes 196616 | tf_op jit(solution)/shard_map/ppermute | solution.py:384
  131.5 1.0 copy-start.6
  132.5 0.7 copy-start.13
  133.9 1.0 copy-start.26
  134.9 7.4 %copy-start.30 = (f32[2,512]{1,0:T(2,128)S(1)}, f32[2,512]{1,0:T(2,128)}, u32[]{:S(2)}) copy-start(f32[2,512]{1,0:T(2,128)} %param.11) | copy-start | bytes 12292
  134.9 32.2 %all-to-all-start.4 = ((bf16[16,32,1024]{2,1,0:T(8,128)(2,1)}), bf16[16,32,1024]{2,1,0:T(8,128)(2,1)}, u32[]{:S(2)}, u32[]{:S(2)}) async-start(bf16[16,32,1024]{2,1,0:T(8,128)(2,1)} %bitcast.41), calls=%async_computation.4 | async-start | bytes 2097152 | tf_op jit(solution)/shard_map/all_to_all | solution.py:375
  167.1 1.0 copy-start.8
  170.8 29.5 %copy-start.5 = (bf16[512,1024]{1,0:T(8,128)(2,1)}, bf16[512,1024]{1,0:T(8,128)(2,1)S(1)}, u32[]{:S(2)}) copy-start(bf16[512,1024]{1,0:T(8,128)(2,1)S(1)} %get-tuple-element.24) | copy-start | bytes 3145732
  200.3 30.4 %all-to-all-start.5 = ((bf16[16,32,1024]{2,1,0:T(8,128)(2,1)}), bf16[16,32,1024]{2,1,0:T(8,128)(2,1)}, u32[]{:S(2)}, u32[]{:S(2)}) async-start(bf16[16,32,1024]{2,1,0:T(8,128)(2,1)} %bitcast.40), calls=%async_computation.5 | async-start | bytes 2097152 | tf_op jit(solution)/shard_map/all_to_all | solution.py:375
  205.4 1.6 copy-start.2
  207.0 0.8 copy-start.20
  230.7 1.6 copy-start.3
  232.3 0.8 copy-start.18
  233.2 4.1 %copy-start.12 = (s32[512,128]{1,0:T(8,128)S(1)}, s32[512,128]{1,0:T(8,128)}, u32[]{:S(2)}) copy-start(s32[512,128]{1,0:T(8,128)} %copy-done.11) | copy-start | bytes 786436
  233.2 4.1 %copy-start.14 = (s32[512,128]{1,0:T(8,128)S(1)}, s32[512,128]{1,0:T(8,128)}, u32[]{:S(2)}) copy-start(s32[512,128]{1,0:T(8,128)} %copy-done.13) | copy-start | bytes 786436
  233.2 4.1 %copy-start.16 = (s32[512,128]{1,0:T(8,128)S(1)}, s32[512,128]{1,0:T(8,128)}, u32[]{:S(2)}) copy-start(s32[512,128]{1,0:T(8,128)} %copy-done.15) | copy-start | bytes 786436
  236.7 4.2 %collective-permute-start.8 = (f32[128,128]{1,0:T(8,128)}, f32[128,128]{1,0:T(8,128)}, u32[]{:S(2)}, u32[]{:S(2)}) collective-permute-start(f32[128,128]{1,0:T(8,128)} %latent_gradient.2), channel_id=1, source_target_pairs={{0,16},{16,0},{32,48},{48,32},{64,80},{80,64},{96,112},{112,96},{1... | collective-permute-start | bytes 196616 | tf_op jit(solution)/shard_map/ppermute | solution.py:384
  236.7 9.1 %collective-permute-start.12 = (f32[128,128]{1,0:T(8,128)}, f32[128,128]{1,0:T(8,128)}, u32[]{:S(2)}, u32[]{:S(2)}) collective-permute-start(f32[128,128]{1,0:T(8,128)} %latent_gradient.3), channel_id=1, source_target_pairs={{0,16},{16,0},{32,48},{48,32},{64,80},{80,64},{96,112},{112,96},{1... | collective-permute-start | bytes 196616 | tf_op jit(solution)/shard_map/ppermute | solution.py:384
  241.8 7.0 %collective-permute-start.9 = (f32[128,128]{1,0:T(8,128)S(1)}, f32[128,128]{1,0:T(8,128)S(1)}, u32[]{:S(2)}, u32[]{:S(2)}) collective-permute-start(f32[128,128]{1,0:T(8,128)S(1)} %add.93), channel_id=1, source_target_pairs={{0,32},{16,48},{32,0},{48,16},{64,96},{80,112},{96,64},{112,80},{1... | collective-permute-start | bytes 196616 | tf_op jit(solution)/shard_map/ppermute | solution.py:384
  246.7 16.9 %copy-start.25 = (bf16[512,1024]{1,0:T(8,128)(2,1)S(1)}, bf16[512,1024]{1,0:T(8,128)(2,1)}, u32[]{:S(2)}) copy-start(bf16[512,1024]{1,0:T(8,128)(2,1)} %copy-done.24) | copy-start | bytes 3145732
  246.8 16.9 %copy-start.27 = (bf16[512,1024]{1,0:T(8,128)(2,1)S(1)}, bf16[512,1024]{1,0:T(8,128)(2,1)}, u32[]{:S(2)}) copy-start(bf16[512,1024]{1,0:T(8,128)(2,1)} %copy-done.26) | copy-start | bytes 3145732
  246.8 5.9 %collective-permute-start.13 = (f32[128,128]{1,0:T(8,128)S(1)}, f32[128,128]{1,0:T(8,128)S(1)}, u32[]{:S(2)}, u32[]{:S(2)}) collective-permute-start(f32[128,128]{1,0:T(8,128)S(1)} %add.97), channel_id=1, source_target_pairs={{0,32},{16,48},{32,0},{48,16},{64,96},{80,112},{96,64},{112,80},{1... | collective-permute-start | bytes 196616 | tf_op jit(solution)/shard_map/ppermute | solution.py:384
  248.8 5.6 %collective-permute-start.10 = (f32[128,128]{1,0:T(8,128)S(1)}, f32[128,128]{1,0:T(8,128)S(1)}, u32[]{:S(2)}, u32[]{:S(2)}) collective-permute-start(f32[128,128]{1,0:T(8,128)S(1)} %add.94), channel_id=1, source_target_pairs={{0,64},{16,80},{32,96},{48,112},{64,0},{80,16},{96,32},{112,48},{1... | collective-permute-start | bytes 196616 | tf_op jit(solution)/shard_map/ppermute | solution.py:384
  252.6 8.3 %collective-permute-start.14 = (f32[128,128]{1,0:T(8,128)S(1)}, f32[128,128]{1,0:T(8,128)S(1)}, u32[]{:S(2)}, u32[]{:S(2)}) collective-permute-start(f32[128,128]{1,0:T(8,128)S(1)} %add.98), channel_id=1, source_target_pairs={{0,64},{16,80},{32,96},{48,112},{64,0},{80,16},{96,32},{112,48},{1... | collective-permute-start | bytes 196616 | tf_op jit(solution)/shard_map/ppermute | solution.py:384
  254.4 20.5 %collective-permute-start.11 = (f32[128,128]{1,0:T(8,128)S(1)}, f32[128,128]{1,0:T(8,128)}, u32[]{:S(2)}, u32[]{:S(2)}) collective-permute-start(f32[128,128]{1,0:T(8,128)S(1)} %add.95), channel_id=1, source_target_pairs={{0,128},{16,144},{32,160},{48,176},{64,192},{80,208},{96,224},{112... | collective-permute-start | bytes 196616 | tf_op jit(solution)/shard_map/ppermute | solution.py:384
  261.5 14.2 %collective-permute-start.15 = (f32[128,128]{1,0:T(8,128)}, f32[128,128]{1,0:T(8,128)}, u32[]{:S(2)}, u32[]{:S(2)}) collective-permute-start(f32[128,128]{1,0:T(8,128)} %add.99), channel_id=1, source_target_pairs={{0,128},{16,144},{32,160},{48,176},{64,192},{80,208},{96,224},{112... | collective-permute-start | bytes 196616 | tf_op jit(solution)/shard_map/ppermute | solution.py:384
  268.7 8.0 %copy-start.9 = (s32[1024,128]{1,0:T(8,128)S(1)}, s32[1024,128]{1,0:T(8,128)}, u32[]{:S(2)}) copy-start(s32[1024,128]{1,0:T(8,128)} %get-tuple-element.34.low_ref) | copy-start | bytes 1572868
  268.7 8.0 %copy-start.10 = (s32[1024,128]{1,0:T(8,128)S(1)}, s32[1024,128]{1,0:T(8,128)}, u32[]{:S(2)}) copy-start(s32[1024,128]{1,0:T(8,128)} %get-tuple-element.35.high_ref) | copy-start | bytes 1572868
  (3 other events, 2.1 us)

commit v2 on v1

v2 whole, which is shorter than its diff:
```python
import functools
import math

import jax
import jax.numpy as jnp
from jax import lax
from jax.experimental import pallas as pl
from jax.experimental.pallas import tpu as pltpu
from jax.sharding import PartitionSpec as P

D = 8192
L = 2
CAP = 64
GROUPS = 16
CHUNKS = (32, 32)
LANES = 128
KEPT = 32
PER = LANES // KEPT
BF16 = jnp.bfloat16
F32 = jnp.float32
I32 = jnp.int32
ROW_BLOCK = 256
VMEM_LIMIT = 20 * 1024 * 1024


def iota(shape, dim):
    return lax.broadcasted_iota(I32, shape, dim)


def params():
    return pltpu.CompilerParams(vmem_limit_bytes=VMEM_LIMIT)


def cost(flops, nbytes):
    return pl.CostEstimate(flops=int(flops), bytes_accessed=int(nbytes), transcendentals=0)


def whole():
    return pl.BlockSpec(memory_space=pltpu.VMEM)


def offsets():
    out, start = [], 0
    for cap in CHUNKS:
        out.append((start, cap))
        start += cap
    return out


def chunk_hits(info, off, cap, tokens):
    rows = iota((GROUPS * cap, tokens), 0)

    def slot(route, pos):
        inside = (pos >= off) & (pos < off + cap)
        return jnp.where(inside, route * cap + (pos - off), -1)

    return (rows == slot(info[0:1], info[1:2])) | (rows == slot(info[2:3], info[3:4]))


def pack_kernel(routes_ref, acts_ref, index_ref, info_ref, *send_refs):
    tokens, inner = acts_ref.shape
    upper = (iota((tokens, tokens), 0) < iota((tokens, tokens), 1)).astype(F32).astype(BF16)
    experts = iota((GROUPS, tokens), 0)
    total = jnp.zeros((GROUPS, 1), F32)
    rows = []
    for j in range(2):
        route = routes_ref[j : j + 1, :]
        hit = experts == route
        hot = hit.astype(F32)
        before = jnp.dot(hot.astype(BF16), upper, preferred_element_type=F32) + total
        total = total + jnp.sum(hot, axis=1, keepdims=True)
        pos = jnp.sum(jnp.where(hit, before, 0.0), axis=0, keepdims=True).astype(I32)
        rows += [route, pos]
    info = jnp.concatenate(rows + [jnp.zeros((4, tokens), I32)], axis=0)
    info_ref[...] = info
    x = acts_ref[...]
    for (off, cap), send_ref in zip(offsets(), send_refs):
        hits = chunk_hits(info, off, cap, tokens).astype(F32).astype(BF16)
        send_ref[:, :inner] = jnp.dot(hits, x, preferred_element_type=F32).astype(BF16)
    send_refs[0][:, inner:] = index_codes(info, index_ref[...])


def index_codes(info, index):
    tokens, cols = index.shape
    code = (((index & 127) + 128) << (index >> 7)).astype(F32).astype(BF16)
    col = iota((cols, LANES), 0)
    lane = iota((cols, LANES), 1)
    first = CHUNKS[0]
    rows_total = GROUPS * first
    row = iota((rows_total, tokens), 0)
    expert, inner = row // first, row % first
    base = jnp.full((rows_total, tokens), -(1 << 20), I32)
    step = jnp.zeros((rows_total, tokens), I32)
    for off, cap in offsets():
        here = (inner >= off // PER) & (inner < (off + cap) // PER)
        base = jnp.where(here, expert * CAP + off + inner - off // PER, base)
        step = jnp.where(here, cap // PER, step)
    lane_q = iota((rows_total, LANES), 1) // KEPT
    result = jnp.zeros((rows_total, LANES), F32)
    for j in range(2):
        spread = (col == j * KEPT + lane % KEPT).astype(F32).astype(BF16)
        codes = jnp.dot(code, spread, preferred_element_type=F32).astype(BF16)
        key = info[2 * j : 2 * j + 1] * CAP + info[2 * j + 1 : 2 * j + 2]
        for q in range(PER):
            hit = (base + step * q == key).astype(F32).astype(BF16)
            picked = jnp.dot(hit, codes, preferred_element_type=F32)
            result = result + jnp.where(lane_q == q, picked, 0.0)
    return result.astype(BF16)


def pack(routes_t, x, index):
    tokens, width = x.shape
    widths = [width + LANES] + [width] * (len(CHUNKS) - 1)
    return pl.pallas_call(
        pack_kernel,
        out_shape=(jax.ShapeDtypeStruct((8, tokens), I32),)
        + tuple(jax.ShapeDtypeStruct((GROUPS * c, w), BF16) for c, w in zip(CHUNKS, widths)),
        in_specs=[whole()] * 3,
        out_specs=(whole(),) * (1 + len(CHUNKS)),
        compiler_params=params(),
        cost_estimate=cost(2 * GROUPS * CAP * tokens * width, 3 << 20),
        name="pack_tokens",
    )(routes_t, x, index)


def maps_kernel(codes_ref, *refs):
    scratch_ref = refs[-1]
    first = CHUNKS[0]
    code = codes_ref[...].astype(F32).astype(I32)
    tile = jnp.zeros(code.shape, I32)
    for h in range(7):
        tile = tile + jnp.where(code >= (256 << h), 1, 0)
    numbers = jnp.where(code > 0, tile * 128 + (code >> tile) - 128, -1)
    for c, (off, cap) in enumerate(offsets()):
        index_ref, low_ref, high_ref = refs[3 * c : 3 * c + 3]
        packed = cap // PER
        rows = [
            numbers[src * first + off // PER : src * first + (off + cap) // PER] for src in range(GROUPS)
        ]
        idx = jnp.concatenate(rows, axis=0)
        for src in range(GROUPS):
            index_ref[src] = rows[src]
        turned = idx.T
        tile = turned >> 7
        scratch_ref[0] = jnp.where(turned >= 0, turned & 127, -1)
        place = (iota(turned.shape, 0) % KEPT) + 1
        scratch_ref[1] = jnp.where((tile >= 0) & (tile < 4), place << (jnp.clip(tile, 0, 3) * 6), 0)
        scratch_ref[2] = jnp.where(tile >= 4, place << (jnp.clip(tile - 4, 0, 3) * 6), 0)
        for q in range(PER):
            lows, highs = [], []
            for part in range(2):
                size = LANES // 2
                spot = iota((size, LANES), 0) + part * size
                low = jnp.zeros((size, LANES), I32)
                high = jnp.zeros((size, LANES), I32)
                for k in range(KEPT):
                    at = q * KEPT + k
                    same = spot == scratch_ref[0, at : at + 1, :]
                    low = low + jnp.where(same, scratch_ref[1, at : at + 1, :], 0)
                    high = high + jnp.where(same, scratch_ref[2, at : at + 1, :], 0)
                lows.append(low)
                highs.append(high)
            low = jnp.concatenate(lows, axis=0).T
            high = jnp.concatenate(highs, axis=0).T
            for src in range(GROUPS):
                row = src * cap + q * packed
                low_ref[row : row + packed, :] = low[src * packed : (src + 1) * packed]
                high_ref[row : row + packed, :] = high[src * packed : (src + 1) * packed]


def slot_maps(arrived):
    rows, width = arrived.shape
    shapes = []
    for cap in CHUNKS:
        shapes.append(jax.ShapeDtypeStruct((GROUPS, cap // PER, LANES), I32))
        shapes += [jax.ShapeDtypeStruct((GROUPS * cap, LANES), I32)] * 2
    out = pl.pallas_call(
        maps_kernel,
        grid=(1,),
        out_shape=tuple(shapes),
        in_specs=[pl.BlockSpec((rows, LANES), lambda i: (0, width // LANES - 1))],
        out_specs=tuple(
            pl.BlockSpec(s.shape, functools.partial(lambda n, i: (0,) * n, len(s.shape))) for s in shapes
        ),
        scratch_shapes=[pltpu.VMEM((3, LANES, LANES), I32)],
        compiler_params=params(),
        cost_estimate=cost(4_000_000_000, 1 << 20),
        name="slot_maps",
    )(arrived)
    return [out[3 * c : 3 * c + 3] for c in range(len(CHUNKS))]


def skipping(kernel, inputs, extra):
    def run(*refs):
        kernel(*refs[:inputs], *refs[inputs + extra :])

    return run


TOKEN = jax.ShapeDtypeStruct((8, LANES), F32)


def token_spec():
    return pl.BlockSpec((8, LANES), lambda *i: (0, 0))


def gather_kept(values_ref, index_ref, out_ref, groups, packed_rows):
    tiles = values_ref.shape[1] // LANES
    lane_q = iota((8, LANES), 1) // KEPT
    for src in range(groups):
        for half in range(packed_rows // 8):
            idx = index_ref[src, half * 8 : half * 8 + 8, :]
            spot, tile = idx & 127, idx >> 7
            result = jnp.zeros((8, LANES), F32)
            for q in range(PER):
                row = src * packed_rows * PER + q * packed_rows + half * 8
                here = jnp.where(lane_q == q, tile, -1)
                for t in range(tiles):
                    part = values_ref[row : row + 8, t * LANES : (t + 1) * LANES]
                    taken = jnp.take_along_axis(part, spot, axis=1, mode="promise_in_bounds")
                    result = jnp.where(here == t, taken, result)
            start = src * packed_rows + half * 8
            out_ref[start : start + 8, :] = result


def encode_kernel(x_ref, w_ref, bias_ref, index_ref, out_ref, values_ref):
    values_ref[...] = jnp.dot(x_ref[...], w_ref[...], preferred_element_type=F32) + bias_ref[...]
    gather_kept(values_ref, index_ref, out_ref, index_ref.shape[0], index_ref.shape[1])


def backproject_kernel(r_ref, w_ref, index_ref, out_ref, values_ref):
    values_ref[...] = lax.dot_general(
        r_ref[...], w_ref[...], (((1,), (1,)), ((), ())), preferred_element_type=F32
    )
    gather_kept(values_ref, index_ref, out_ref, index_ref.shape[0], index_ref.shape[1])


def kept_product(kernel, rows, weight, index, bias, name, after=()):
    total = rows.shape[0]
    inner, latents = 1024, 1024
    packed_rows = index.shape[1]
    groups = ROW_BLOCK // (packed_rows * PER)
    operands = [rows, weight] + ([] if bias is None else [bias]) + [index]
    specs = [
        pl.BlockSpec((ROW_BLOCK, inner), lambda i: (i, 0)),
        pl.BlockSpec(weight.shape, lambda i: (0, 0)),
    ]
    if bias is not None:
        specs.append(pl.BlockSpec(bias.shape, lambda i: (0, 0)))
    specs.append(pl.BlockSpec((groups, packed_rows, LANES), lambda i: (i, 0, 0)))
    return pl.pallas_call(
        skipping(kernel, len(operands), len(after)),
        grid=(total // ROW_BLOCK,),
        out_shape=jax.ShapeDtypeStruct((total // PER, LANES), F32),
        in_specs=specs + [token_spec()] * len(after),
        out_specs=pl.BlockSpec((ROW_BLOCK // PER, LANES), lambda i: (i, 0)),
        scratch_shapes=[pltpu.VMEM((ROW_BLOCK, latents), F32)],
        compiler_params=params(),
        cost_estimate=cost(4 * total * inner * latents, 4 << 20),
        name=name,
    )(*operands, *after)


def spread_kept(kept_ref, low_ref, high_ref, dense_ref, groups, packed_rows):
    for src in range(groups):
        for half in range(packed_rows // 8):
            start = src * packed_rows + half * 8
            kept = kept_ref[start : start + 8, :]
            for q in range(PER):
                row = src * packed_rows * PER + q * packed_rows + half * 8
                words = (low_ref[row : row + 8, :], high_ref[row : row + 8, :])
                for t in range(8):
                    place = (words[t // 4] >> (6 * (t % 4))) & 63
                    spot = jnp.maximum(place - 1, 0) + q * KEPT
                    taken = jnp.take_along_axis(kept, spot, axis=1, mode="promise_in_bounds")
                    dense_ref[row : row + 8, t * LANES : (t + 1) * LANES] = jnp.where(
                        place > 0, taken, 0.0
                    )


def decode_kernel(packed_rows, pre_ref, low_ref, high_ref, w_ref, latent_ref, out_ref, token_ref, kept_ref, dense_ref):
    token_ref[...] = jnp.zeros_like(token_ref)
    pre = pre_ref[...]
    kept_ref[...] = (pre / (1.0 + jnp.exp(-pre))).astype(BF16).astype(F32)
    spread_kept(kept_ref, low_ref, high_ref, dense_ref, ROW_BLOCK // (packed_rows * PER), packed_rows)
    latent = dense_ref[...].astype(BF16)
    latent_ref[...] = latent
    out_ref[...] = jnp.dot(latent, w_ref[...], preferred_element_type=F32).astype(BF16)


def decode(pre, low, high, weight, packed_rows):
    total = low.shape[0]
    latents, inner = weight.shape
    by_row = lambda i: (i, 0)
    return pl.pallas_call(
        functools.partial(decode_kernel, packed_rows),
        grid=(total // ROW_BLOCK,),
        out_shape=(
            jax.ShapeDtypeStruct((total, latents), BF16),
            jax.ShapeDtypeStruct((total, inner), BF16),
            TOKEN,
        ),
        in_specs=[
            pl.BlockSpec((ROW_BLOCK // PER, LANES), by_row),
            pl.BlockSpec((ROW_BLOCK, LANES), by_row),
            pl.BlockSpec((ROW_BLOCK, LANES), by_row),
            pl.BlockSpec(weight.shape, lambda i: (0, 0)),
        ],
        out_specs=(
            pl.BlockSpec((ROW_BLOCK, latents), by_row),
            pl.BlockSpec((ROW_BLOCK, inner), by_row),
            token_spec(),
        ),
        scratch_shapes=[
            pltpu.VMEM((ROW_BLOCK // PER, LANES), F32),
            pltpu.VMEM((ROW_BLOCK, latents), F32),
        ],
        compiler_params=params(),
        cost_estimate=cost(4 * total * inner * latents, 6 << 20),
        name="decode",
    )(pre, low, high, weight)


def residual_kernel(*refs):
    count = len(CHUNKS)
    info_ref, x_ref, bias_ref = refs[:3]
    back_refs, send_refs = refs[3 : 3 + count], refs[3 + count :]
    tokens = x_ref.shape[0]
    info = info_ref[...]
    hits = [chunk_hits(info, off, cap, tokens).astype(F32).astype(BF16) for off, cap in offsets()]
    total = jnp.zeros(x_ref.shape, F32)
    for hit, back_ref in zip(hits, back_refs):
        total = total + lax.dot_general(
            hit, back_ref[...], (((0,), (0,)), ((), ())), preferred_element_type=F32
        )
    residual = (total + bias_ref[...] - x_ref[...].astype(F32)).astype(BF16)
    for hit, send_ref in zip(hits, send_refs):
        send_ref[...] = jnp.dot(hit, residual, preferred_element_type=F32).astype(BF16)


def form_residual(info, x, bias, back, after):
    tokens, width = x.shape
    return pl.pallas_call(
        skipping(residual_kernel, 3 + len(CHUNKS), len(after)),
        out_shape=tuple(jax.ShapeDtypeStruct((GROUPS * c, width), BF16) for c in CHUNKS),
        in_specs=[whole()] * (3 + len(CHUNKS) + len(after)),
        out_specs=(whole(),) * len(CHUNKS),
        compiler_params=params(),
        cost_estimate=cost(4 * GROUPS * CAP * tokens * width, 5 << 20),
        name="form_residual",
    )(info, x, bias, *back, *after)


def turn_kernel(*refs):
    half = (len(refs) - 1) // 2
    refs[-1][...] = jnp.zeros(refs[-1].shape, F32)
    for src, dst in zip(refs[:half], refs[half:]):
        dst[...] = src[...].T


def turn(arrived, inner):
    return pl.pallas_call(
        turn_kernel,
        grid=(4,),
        out_shape=tuple(jax.ShapeDtypeStruct((inner, a.shape[0]), BF16) for a in arrived) + (TOKEN,),
        in_specs=[pl.BlockSpec((a.shape[0], inner // 4), lambda i: (0, i)) for a in arrived],
        out_specs=tuple(pl.BlockSpec((inner // 4, a.shape[0]), lambda i: (i, 0)) for a in arrived)
        + (token_spec(),),
        compiler_params=params(),
        cost_estimate=cost(4_000_000_000, 4 << 20),
        name="turn_rows",
    )(*arrived)


def encoder_grad_kernel(chunk, scale, *refs):
    lg_ref, pre_ref, low_ref, high_ref, xt_ref = refs[:5]
    if scale is None:
        out_ref, token_ref, kept_ref, dense_ref, grad_ref = refs[5:]
        token_ref[...] = jnp.zeros_like(token_ref)
    else:
        part_ref, out_ref, kept_ref, dense_ref, grad_ref = refs[5:]

    @pl.when(pl.program_id(0) == 0)
    def _():
        pre = pre_ref[...]
        sig = 1.0 / (1.0 + jnp.exp(-pre))
        slope = lg_ref[...] * (sig * (1.0 + pre * (1.0 - sig)))
        kept_ref[...] = slope.astype(BF16).astype(F32)
        spread_kept(kept_ref, low_ref, high_ref, dense_ref, GROUPS, chunk // PER)
        grad_ref[...] = dense_ref[...].astype(BF16)

    part = jnp.dot(xt_ref[...], grad_ref[...], preferred_element_type=F32)
    if scale is None:
        out_ref[...] = part
    else:
        out_ref[...] = ((part + part_ref[...]) * scale).astype(BF16)


def encoder_grad(lg, pre, low, high, x_t, chunk, scale=None, part=None):
    total = low.shape[0]
    inner, latents = x_t.shape[0], 1024
    block = 256
    all_of = lambda a: pl.BlockSpec(a.shape, lambda i: (0, 0))
    by_row = lambda i: (i, 0)
    operands = [lg, pre, low, high, x_t]
    specs = [all_of(a) for a in operands[:4]] + [pl.BlockSpec((block, total), by_row)]
    result = pl.BlockSpec((block, latents), by_row)
    if scale is None:
        shapes = (jax.ShapeDtypeStruct((inner, latents), F32), TOKEN)
        results = (result, token_spec())
    else:
        operands.append(part)
        specs.append(result)
        shapes, results = jax.ShapeDtypeStruct((inner, latents), BF16), result
    return pl.pallas_call(
        functools.partial(encoder_grad_kernel, chunk, scale),
        grid=(inner // block,),
        out_shape=shapes,
        in_specs=specs,
        out_specs=results,
        scratch_shapes=[
            pltpu.VMEM(lg.shape, F32),
            pltpu.VMEM((total, latents), F32),
            pltpu.VMEM((total, latents), BF16),
        ],
        compiler_params=params(),
        cost_estimate=cost(4 * total * inner * latents, 6 << 20),
        name="encoder_grad",
    )(*operands)


def decoder_grad_kernel(last, latent_ref, res_ref, *refs):
    part = lax.dot_general(
        latent_ref[...], res_ref[...], (((0,), (0,)), ((), ())), preferred_element_type=F32
    )
    if last:
        part_ref, out_ref = refs
        out_ref[...] = (part + part_ref[...]).astype(BF16)
    else:
        out_ref, token_ref = refs
        out_ref[...] = part
        token_ref[...] = jnp.zeros_like(token_ref)


def decoder_grad(latent, res, part=None):
    total, latents = latent.shape
    inner = res.shape[1]
    block = 256
    result = pl.BlockSpec((block, inner), lambda i: (i, 0))
    specs = [pl.BlockSpec((total, block), lambda i: (0, i)), pl.BlockSpec(res.shape, lambda i: (0, 0))]
    operands = [latent, res]
    if part is None:
        shapes = (jax.ShapeDtypeStruct((latents, inner), F32), TOKEN)
        results = (result, token_spec())
    else:
        operands.append(part)
        specs.append(result)
        shapes, results = jax.ShapeDtypeStruct((latents, inner), BF16), result
    return pl.pallas_call(
        functools.partial(decoder_grad_kernel, part is not None),
        grid=(latents // block,),
        out_shape=shapes,
        in_specs=specs,
        out_specs=results,
        compiler_params=params(),
        cost_estimate=cost(2 * total * inner * latents, 6 << 20),
        name="decoder_grad",
    )(*operands)


def exchange(rows):
    count, width = rows.shape
    return lax.all_to_all(
        rows.reshape(GROUPS, count // GROUPS, width), "feat", split_axis=0, concat_axis=0, tiled=True
    ).reshape(count, width)


def width_sum(part):
    for masks in ((1,), (2,), (4, 8, 12)):
        size = lax.axis_size("width")
        moved = [lax.ppermute(part, "width", [(a, a ^ m) for a in range(size)]) for m in masks]
        for other in moved:
            part = part + other
    return part


def per_device(acts, enc_weight, enc_bias, dec_weight, dec_bias, routes, latent_index):
    tokens, layers, width_dev = acts.shape
    inner = layers * width_dev
    latents = enc_weight.shape[3]
    scale = 1.0 / math.sqrt(L * D)
    x_home = acts.reshape(tokens, inner)
    enc = enc_weight.reshape(inner, latents)
    dec = dec_weight.reshape(latents, inner)
    bias = jnp.where(lax.axis_index("width") == 0, enc_bias, 0.0)

    info, *sends = pack(routes.T, x_home, latent_index.reshape(tokens, 2 * KEPT))
    arrived = [exchange(s) for s in sends]
    maps = slot_maps(arrived[0])

    pre, latent, back, after = [], [], [], ()
    for c, cap in enumerate(CHUNKS):
        index, low, high = maps[c]
        part = kept_product(encode_kernel, arrived[c], enc, index, bias, "encode", after)
        pre.append(width_sum(part))
        lat, decoded, token = decode(pre[c], low, high, dec, cap // PER)
        after = (token,)
        latent.append(lat)
        back.append(exchange(decoded))

    *turned, token = turn(arrived, inner)
    outgoing = form_residual(info, x_home, dec_bias.reshape(1, inner), back, (token,))
    res = [exchange(o) for o in outgoing]

    def latent_gradient(c, after):
        part = kept_product(backproject_kernel, res[c], dec, maps[c][0], None, "latent_gradient", after)
        return width_sum(part)

    enc_part, enc_token = encoder_grad(
        latent_gradient(0, ()), pre[0], maps[0][1], maps[0][2], turned[0], CHUNKS[0]
    )
    dec_part, dec_token = decoder_grad(latent[0], res[0])
    last = latent_gradient(1, (enc_token, dec_token))
    grad_dec = decoder_grad(latent[1], res[1], dec_part)
    grad_enc = encoder_grad(last, pre[1], maps[1][1], maps[1][2], turned[1], CHUNKS[1], scale, enc_part)
    return (
        grad_enc.reshape(1, layers, width_dev, latents),
        grad_dec.reshape(1, latents, layers, width_dev),
    )


def solution(mesh):
    placed = (
        P("feat", None, "width"),
        P("feat", None, "width", None),
        P("feat", None),
        P("feat", None, None, "width"),
        P(None, "width"),
        P("feat", None),
        P("feat", None, None),
    )
    return jax.shard_map(
        per_device,
        mesh=mesh,
        in_specs=placed,
        out_specs=(P("feat", None, "width", None), P("feat", None, None, "width")),
        check_vma=False,
    )
```

time: 286 us -> 244 us (0.85)
  waiting for transfers between devices: 65.2 us -> 46.9 us
  Pallas kernels: 49.6 us -> 36.9 us
  starting transfers between devices: 54.1 us -> 64 us
  other arithmetic: 7.36 us -> 0.15 us
  blocking collectives: 75.2 us -> 68.6 us
  matrix products: 5.01 us -> 0 us
  local copies, waits for them, and re-layouts: 27.5 us -> 24.6 us
    all_to_all x4, waiting for transfers between devices: 45.2 us -> 18.7 us  [exchange(): lax.all_to_all(rows.reshape(GROUPS, count // GROUPS, width), 'feat', spli...]
    pallas_call x9 -> x11, Pallas kernels: 42.8 us -> 29.7 us  [the longest x4 8.32 us: kept_product(): pl.pallas_call(skipping(kernel, len(operands), len(after)), grid=(total /...]
    ppermute x16 -> x20, waiting for transfers between devices: 20 us -> 28.2 us  [width_sum(): lax.ppermute(part, 'width', [(a, a ^ m) for a in range(size)])]
    all_to_all x3 -> x2, blocking collectives: 75.2 us -> 68.6 us  [exchange(): lax.all_to_all(rows.reshape(GROUPS, count // GROUPS, width), 'feat', spli...]
    all_to_all x4, starting transfers between devices: 24 us -> 29.4 us  [exchange(): lax.all_to_all(rows.reshape(GROUPS, count // GROUPS, width), 'feat', spli...]
    dot_general x1 -> x0, matrix products: 5.01 us -> none  [per_device(): lax.dot_general(jnp.concatenate(latent, axis=0), jnp.concatenate(res, axi...]
    ppermute x16 -> x20, starting transfers between devices: 30 us -> 34.6 us  [width_sum(): lax.ppermute(part, 'width', [(a, a ^ m) for a in range(size)])]
    add x16 -> x12, other arithmetic: 4.23 us -> 0.14 us  [width_sum(): part = part + other]
  transfers between devices with their start and end apart: 20 -> 24, of which waited for: 9 -> 14; matrix products, arithmetic and copies ran while one was open for 7% -> 1% of each run, Pallas kernels for 11% -> 11%
where the time goes in v2:
time: 244 us; the launch traced here: 242 us
  blocking collectives  68.6 us (28%)
  starting transfers between devices  64 us (26%)
  waiting for transfers between devices  46.9 us (19%)
  Pallas kernels  36.9 us (15%)
  local copies, waits for them, and re-layouts  24.6 us (10%)
    all_to_all x2, blocking collectives, exchange(): lax.all_to_all(rows.reshape(GROUPS, count // GROUPS, width), 'feat', spli...  68.6 us
    ppermute x20, starting transfers between devices, width_sum(): lax.ppermute(part, 'width', [(a, a ^ m) for a in range(size)])  34.6 us
    all_to_all x4, starting transfers between devices, exchange(): lax.all_to_all(rows.reshape(GROUPS, count // GROUPS, width), 'feat', spli...  29.4 us
    ppermute x20, waiting for transfers between devices, width_sum(): lax.ppermute(part, 'width', [(a, a ^ m) for a in range(size)])  28.2 us
    unnamed x73, local copies, waits for them, and re-layouts  21 us
    all_to_all x4, waiting for transfers between devices, exchange(): lax.all_to_all(rows.reshape(GROUPS, count // GROUPS, width), 'feat', spli...  18.7 us
    pallas_call x4, Pallas kernels, kept_product(): pl.pallas_call(skipping(kernel, len(operands), len(after)), grid=(total /...  8.32 us
    pallas_call x2, Pallas kernels, encoder_grad(): pl.pallas_call(functools.partial(encoder_grad_kernel, chunk, scale), grid...  7.77 us
  transfers between devices with their start and end apart: 24, of which 14 were waited for; matrix products, arithmetic and copies ran while one was open for 1% of the time, Pallas kernels for 11%

profile of v2, /device:TPU:32, one launch (start us, length us, event | category | flops | bytes accessed | tf_op | source)
XLA Modules:
  0.0 242.3 jit_solution(10801698317096100482)
XLA Ops:
  1.6 1.1 copy.11
  3.4 1.8 pack_tokens.1
  5.2 39.8 %all_to_all.30 = bf16[16,32,1152]{2,1,0:T(8,128)(2,1)S(1)} all-to-all(bf16[16,32,1152]{2,1,0:T(8,128)(2,1)S(1)} %bitcast.33), channel_id=1, replica_groups=mesh['width'=16,'feat'=16] {'feat'}, dimensions={0} | all-to-all | bytes 2359296 | tf_op jit(solution)/shard_map/all_to_all | solution.py:473
  45.1 4.8 %all-to-all-start.2 = ((bf16[16,32,1024]{2,1,0:T(8,128)(2,1)}), bf16[16,32,1024]{2,1,0:T(8,128)(2,1)}, u32[]{:S(2)}, u32[]{:S(2)}) async-start(bf16[16,32,1024]{2,1,0:T(8,128)(2,1)} %bitcast.7), calls=%async_computation.2 | async-start | bytes 2097152 | tf_op jit(solution)/shard_map/all_to_all | solution.py:473
  49.9 3.9 %slot_maps.1 = (s32[16,8,128]{2,1,0:T(8,128)S(1)}, s32[512,128]{1,0:T(8,128)S(1)}, s32[512,128]{1,0:T(8,128)S(1)}, s32[16,8,128]{2,1,0:T(8,128)S(1)}, s32[512,128]{1,0:T(8,128)S(1)}, /*index=5*/s32[512,128]{1,0:T(8,128)S(1)}) custom-call(bf16[512,1152]{1,0:T(8,128)(2,1)S(1)} %bitcast.30), custom_call_target="tpu_custom_call" | custom-call | flops 4000000000 | bytes 1048576 | tf_op jit(solution)/shard_map/slot_maps/pallas_call | solution.py:177
  54.6 1.9 encode.2
  56.5 1.2 collective-permute-done
  57.8 2.8 %collective-permute-start.1 = (f32[128,128]{1,0:T(8,128)S(1)}, f32[128,128]{1,0:T(8,128)S(1)}, u32[]{:S(2)}, u32[]{:S(2)}) collective-permute-start(f32[128,128]{1,0:T(8,128)S(1)} %add.60), channel_id=1, source_target_pairs={{0,32},{16,48},{32,0},{48,16},{64,96},{80,112},{96,64},{112,80},{1... | collective-permute-start | bytes 196616 | tf_op jit(solution)/shard_map/ppermute | solution.py:481
  60.6 3.8 %collective-permute-done.1 = f32[128,128]{1,0:T(8,128)S(1)} collective-permute-done((f32[128,128]{1,0:T(8,128)S(1)}, f32[128,128]{1,0:T(8,128)S(1)}, u32[]{:S(2)}, u32[]{:S(2)}) %collective-permute-start.1) | collective-permute-done | bytes 65568 | tf_op jit(solution)/shard_map/ppermute | solution.py:481
  64.4 3.1 %collective-permute-start.4 = (f32[128,128]{1,0:T(8,128)S(1)}, f32[128,128]{1,0:T(8,128)S(1)}, u32[]{:S(2)}, u32[]{:S(2)}) collective-permute-start(f32[128,128]{1,0:T(8,128)S(1)} %add.61), channel_id=1, source_target_pairs={{0,192},{16,208},{32,224},{48,240},{64,128},{80,144},{96,160},{112... | collective-permute-start | bytes 196616 | tf_op jit(solution)/shard_map/ppermute | solution.py:481
  70.0 3.3 %collective-permute-done.3 = f32[128,128]{1,0:T(8,128)S(1)} collective-permute-done((f32[128,128]{1,0:T(8,128)S(1)}, f32[128,128]{1,0:T(8,128)S(1)}, u32[]{:S(2)}, u32[]{:S(2)}) %collective-permute-start.3) | collective-permute-done | bytes 65568 | tf_op jit(solution)/shard_map/ppermute | solution.py:481
  73.3 2.5 %decode.2 = (bf16[512,1024]{1,0:T(8,128)(2,1)S(1)}, bf16[512,1024]{1,0:T(8,128)(2,1)S(1)}, f32[8,128]{1,0:T(8,128)S(1)}) custom-call(f32[128,128]{1,0:T(8,128)S(1)} %add_add_fusion.3.pre_ref.refs_1_, s32[512,128]{1,0:T(8,128)S(1)} %get-tuple-element.28.low_ref.refs_2_, s32[512,128]{1,0:T(8,128)S(1)} %get-tuple-element.29.high_ref.refs_3_, ...), custom_call_target="tpu_custom_call" | custom-call | flops 2147483648 | bytes 6291456 | tf_op jit(solution)/shard_map/decode/pallas_call | solution.py:295
  77.8 10.9 %all-to-all-start.1 = ((bf16[16,32,1024]{2,1,0:T(8,128)(2,1)}), bf16[16,32,1024]{2,1,0:T(8,128)(2,1)}, u32[]{:S(2)}, u32[]{:S(2)}) async-start(bf16[16,32,1024]{2,1,0:T(8,128)(2,1)} %bitcast.35), calls=%async_computation.1 | async-start | bytes 2097152 | tf_op jit(solution)/shard_map/all_to_all | solution.py:473
  88.8 1.6 copy-done.22
  90.4 2.9 %encode.3 = f32[128,128]{1,0:T(8,128)S(1)} custom-call(bf16[512,1024]{1,0:T(8,128)(2,1)} %bitcast.8.refs_0_.refs_1_, bf16[1024,1024]{1,0:T(8,128)(2,1)S(1)} %bitcast.44, f32[1,1024]{1,0:T(1,128)S(1)} %broadcast_select_fusion.refs_2_, s32[16,8,128]{2,1,0:T(8,128)S(1)} %get-tuple-element.32.refs_3_.refs_2_, f32[8,128]{1,0:T(8,128)S(1)} %get-tuple-element.33.refs_4_), custom_call_target="tpu_custom_call" | custom-call | flops 2147483648 | bytes 4194304 | tf_op jit(solution)/shard_map/encode/pallas_call | solution.py:251
  93.3 1.2 collective-permute-done.5
  94.6 2.8 %collective-permute-start.6 = (f32[128,128]{1,0:T(8,128)S(1)}, f32[128,128]{1,0:T(8,128)S(1)}, u32[]{:S(2)}, u32[]{:S(2)}) collective-permute-start(f32[128,128]{1,0:T(8,128)S(1)} %add.65), channel_id=1, source_target_pairs={{0,32},{16,48},{32,0},{48,16},{64,96},{80,112},{96,64},{112,80},{1... | collective-permute-start | bytes 196616 | tf_op jit(solution)/shard_map/ppermute | solution.py:481
  97.4 4.8 %collective-permute-done.6 = f32[128,128]{1,0:T(8,128)S(1)} collective-permute-done((f32[128,128]{1,0:T(8,128)S(1)}, f32[128,128]{1,0:T(8,128)S(1)}, u32[]{:S(2)}, u32[]{:S(2)}) %collective-permute-start.6) | collective-permute-done | bytes 65568 | tf_op jit(solution)/shard_map/ppermute | solution.py:481
  102.2 1.5 collective-permute-start.9
  104.5 1.8 collective-permute-start.7
  106.4 2.1 collective-permute-done.9
  108.5 1.5 collective-permute-done.8
  110.0 2.9 %decode.3 = (bf16[512,1024]{1,0:T(8,128)(2,1)S(1)}, bf16[512,1024]{1,0:T(8,128)(2,1)S(1)}, f32[8,128]{1,0:T(8,128)}) custom-call(f32[128,128]{1,0:T(8,128)S(1)} %add_add_fusion.2.pre_ref.refs_1_, s32[512,128]{1,0:T(8,128)S(1)} %copy-done.16, s32[512,128]{1,0:T(8,128)S(1)} %copy-done.19, bf16[1024,1024]{1,0:T(8,128)(2,1)S(1)} %bitcast.27), custom_call_target="tpu_custom_call" | custom-call | flops 2147483648 | bytes 6291456 | tf_op jit(solution)/shard_map/decode/pallas_call | solution.py:295
  114.9 8.5 %all-to-all-start.3 = ((bf16[16,32,1024]{2,1,0:T(8,128)(2,1)}), bf16[16,32,1024]{2,1,0:T(8,128)(2,1)}, u32[]{:S(2)}, u32[]{:S(2)}) async-start(bf16[16,32,1024]{2,1,0:T(8,128)(2,1)} %bitcast.38), calls=%async_computation.3 | async-start | bytes 2097152 | tf_op jit(solution)/shard_map/all_to_all | solution.py:473
  123.4 2.6 %turn_rows.1 = (bf16[1024,512]{1,0:T(8,128)(2,1)S(1)}, bf16[1024,512]{1,0:T(8,128)(2,1)S(1)}, f32[8,128]{1,0:T(8,128)S(1)}) custom-call(bf16[512,1152]{1,0:T(8,128)(2,1)S(1)} %bitcast.32, bf16[512,1024]{1,0:T(8,128)(2,1)} %bitcast.8.refs_0_.refs_1_), custom_call_target="tpu_custom_call" | custom-call | flops 4000000000 | bytes 4194304 | tf_op jit(solution)/shard_map/turn_rows/pallas_call | solution.py:362
  128.0 18.7 %all-to-all-done.3 = bf16[16,32,1024]{2,1,0:T(8,128)(2,1)} async-done(((bf16[16,32,1024]{2,1,0:T(8,128)(2,1)}), bf16[16,32,1024]{2,1,0:T(8,128)(2,1)}, u32[]{:S(2)}, u32[]{:S(2)}) %all-to-all-start.3) | async-done | bytes 1048608 | tf_op jit(solution)/shard_map/all_to_all | solution.py:473
  147.8 3.0 %form_residual.1 = (bf16[512,1024]{1,0:T(8,128)(2,1)S(1)}, bf16[512,1024]{1,0:T(8,128)(2,1)S(1)}) custom-call(s32[8,256]{1,0:T(8,128)S(1)} %get-tuple-element.25.refs_0_, bf16[256,1024]{1,0:T(8,128)(2,1)S(1)} %bitcast.41, f32[1,1024]{1,0:T(1,128)S(1)} %bitcast.42, bf16[512,1024]{1,0:T(8,128)(2,1)} %bitcast.6.refs_3_, bf16[512,1024]{1,0:T(8,128)(2,1)} %bitcast.10.refs_4_, ...), custom_call_target="tpu_custom_call" | custom-call | flops 1073741824 | bytes 5242880 | tf_op jit(solution)/shard_map/form_residual/pallas_call | solution.py:343
  150.7 28.8 %all_to_all.31 = bf16[16,32,1024]{2,1,0:T(8,128)(2,1)} all-to-all(bf16[16,32,1024]{2,1,0:T(8,128)(2,1)S(1)} %bitcast.39), channel_id=1, replica_groups=mesh['width'=16,'feat'=16] {'feat'}, dimensions={0} | all-to-all | bytes 2097152 | tf_op jit(solution)/shard_map/all_to_all | solution.py:473
  179.5 5.1 %all-to-all-start.4 = ((bf16[16,32,1024]{2,1,0:T(8,128)(2,1)}), bf16[16,32,1024]{2,1,0:T(8,128)(2,1)S(1)}, u32[]{:S(2)}, u32[]{:S(2)}) async-start(bf16[16,32,1024]{2,1,0:T(8,128)(2,1)} %bitcast.34), calls=%async_computation.4 | async-start | bytes 2097152 | tf_op jit(solution)/shard_map/all_to_all | solution.py:473
  184.7 1.2 copy-done.8
  185.9 1.8 latent_gradient.2
  187.8 1.2 collective-permute-done.10
  189.1 7.2 %collective-permute-start.11 = (f32[128,128]{1,0:T(8,128)S(1)}, f32[128,128]{1,0:T(8,128)S(1)}, u32[]{:S(2)}, u32[]{:S(2)}) collective-permute-start(f32[128,128]{1,0:T(8,128)S(1)} %add.70), channel_id=1, source_target_pairs={{0,32},{16,48},{32,0},{48,16},{64,96},{80,112},{96,64},{112,80},{1... | collective-permute-start | bytes 196616 | tf_op jit(solution)/shard_map/ppermute | solution.py:481
  196.3 4.3 %collective-permute-done.11 = f32[128,128]{1,0:T(8,128)S(1)} collective-permute-done((f32[128,128]{1,0:T(8,128)S(1)}, f32[128,128]{1,0:T(8,128)S(1)}, u32[]{:S(2)}, u32[]{:S(2)}) %collective-permute-start.11) | collective-permute-done | bytes 65568 | tf_op jit(solution)/shard_map/ppermute | solution.py:481
  201.3 3.8 %collective-permute-start.13 = (f32[128,128]{1,0:T(8,128)S(1)}, f32[128,128]{1,0:T(8,128)S(1)}, u32[]{:S(2)}, u32[]{:S(2)}) collective-permute-start(f32[128,128]{1,0:T(8,128)S(1)} %add.71), channel_id=1, source_target_pairs={{0,128},{16,144},{32,160},{48,176},{64,192},{80,208},{96,224},{112... | collective-permute-start | bytes 196616 | tf_op jit(solution)/shard_map/ppermute | solution.py:481
  205.2 2.1 decoder_grad.2
  207.2 2.0 copy-done.2
  209.4 3.3 %encoder_grad.2 = (f32[1024,1024]{1,0:T(8,128)S(1)}, f32[8,128]{1,0:T(8,128)S(1)}) custom-call(f32[128,128]{1,0:T(8,128)S(1)} %add_add_fusion.1.refs_0_, f32[128,128]{1,0:T(8,128)S(1)} %add_add_fusion.3.pre_ref.refs_1_, s32[512,128]{1,0:T(8,128)S(1)} %copy-done.29, s32[512,128]{1,0:T(8,128)S(1)} %copy-done.31, bf16[1024,512]{1,0:T(8,128)(2,1)S(1)} %copy-done.27), custom_call_target="tpu_custom_call" | custom-call | flops 2147483648 | bytes 6291456 | tf_op jit(solution)/shard_map/encoder_grad/pallas_call | solution.py:415
  212.8 2.0 copy-done
  214.8 1.8 latent_gradient.3
  216.7 1.2 collective-permute-done.15
  217.9 4.4 %collective-permute-start.16 = (f32[128,128]{1,0:T(8,128)S(1)}, f32[128,128]{1,0:T(8,128)S(1)}, u32[]{:S(2)}, u32[]{:S(2)}) collective-permute-start(f32[128,128]{1,0:T(8,128)S(1)} %add.75), channel_id=1, source_target_pairs={{0,32},{16,48},{32,0},{48,16},{64,96},{80,112},{96,64},{112,80},{1... | collective-permute-start | bytes 196616 | tf_op jit(solution)/shard_map/ppermute | solution.py:481
  222.3 2.4 collective-permute-done.16
  225.5 3.2 %collective-permute-start.18 = (f32[128,128]{1,0:T(8,128)S(1)}, f32[128,128]{1,0:T(8,128)S(1)}, u32[]{:S(2)}, u32[]{:S(2)}) collective-permute-start(f32[128,128]{1,0:T(8,128)S(1)} %add.76), channel_id=1, source_target_pairs={{0,128},{16,144},{32,160},{48,176},{64,192},{80,208},{96,224},{112... | collective-permute-start | bytes 196616 | tf_op jit(solution)/shard_map/ppermute | solution.py:481
  228.9 2.0 decoder_grad.3
  231.0 2.8 %reshape.79 = bf16[1,1024,2,512]{3,2,1,0:T(2,128)(2,1)} reshape(bf16[1024,1024]{1,0:T(8,128)(2,1)S(1)} %decoder_grad.3) | data formatting | bytes 4194304 | tf_op jit(solution)/shard_map/reshape | solution.py:528
  233.8 2.2 copy-done.1
  237.9 4.5 %encoder_grad.3 = bf16[1024,1024]{1,0:T(8,128)(2,1)} custom-call(f32[128,128]{1,0:T(8,128)S(1)} %add_add_fusion.refs_0_, f32[128,128]{1,0:T(8,128)S(1)} %add_add_fusion.2.pre_ref.refs_1_, s32[512,128]{1,0:T(8,128)S(1)} %copy-done.17, s32[512,128]{1,0:T(8,128)S(1)} %copy-done.20, bf16[1024,512]{1,0:T(8,128)(2,1)S(1)} %copy-done.5, f32[1024,1024]{1,0:T(8,128)S(1)} %copy-done.1), custom_call_target="tpu_custom_call" | custom-call | flops 2147483648 | bytes 6291456 | tf_op jit(solution)/shard_map/encoder_grad/pallas_call | solution.py:415
  (104 shorter events, 16.8 us)
Async XLA Ops:
  2.7 42.4 %copy-start.13 = (bf16[32,8,2,512]{3,1,2,0:T(8,128)(2,1)}, bf16[32,8,2,512]{3,1,2,0:T(8,128)(2,1)S(1)}, u32[]{:S(2)}) copy-start(bf16[32,8,2,512]{3,1,2,0:T(8,128)(2,1)S(1)} %copy.11) | copy-start | bytes 1572868
  5.2 44.7 %copy-start.33 = (f32[1,1024]{1,0:T(1,128)S(1)}, f32[1,1024]{1,0:T(1,128)}, u32[]{:S(2)}) copy-start(f32[1,1024]{1,0:T(1,128)} %param.9) | copy-start | bytes 12292
  45.1 32.8 %all-to-all-start.2 = ((bf16[16,32,1024]{2,1,0:T(8,128)(2,1)}), bf16[16,32,1024]{2,1,0:T(8,128)(2,1)}, u32[]{:S(2)}, u32[]{:S(2)}) async-start(bf16[16,32,1024]{2,1,0:T(8,128)(2,1)} %bitcast.7), calls=%async_computation.2 | async-start | bytes 2097152 | tf_op jit(solution)/shard_map/all_to_all | solution.py:473
  49.9 4.6 %copy-start.21 = (bf16[1,2,512,1024]{3,2,1,0:T(8,128)(2,1)S(1)}, bf16[1,2,512,1024]{3,2,1,0:T(8,128)(2,1)}, u32[]{:S(2)}) copy-start(bf16[1,2,512,1024]{3,2,1,0:T(8,128)(2,1)} %param.8) | copy-start | bytes 6291460
  54.5 1.9 copy-start.18
  54.5 18.8 %copy-start.28 = (s32[512,128]{1,0:T(8,128)}, s32[512,128]{1,0:T(8,128)S(1)}, u32[]{:S(2)}) copy-start(s32[512,128]{1,0:T(8,128)S(1)} %get-tuple-element.28.low_ref.refs_2_) | copy-start | bytes 786436
  54.5 18.8 %copy-start.30 = (s32[512,128]{1,0:T(8,128)}, s32[512,128]{1,0:T(8,128)S(1)}, u32[]{:S(2)}) copy-start(s32[512,128]{1,0:T(8,128)S(1)} %get-tuple-element.29.high_ref.refs_3_) | copy-start | bytes 786436
  54.6 14.0 %copy-start.32 = (bf16[1,1024,2,512]{3,2,1,0:T(2,128)(2,1)S(1)}, bf16[1,1024,2,512]{3,2,1,0:T(2,128)(2,1)}, u32[]{:S(2)}) copy-start(bf16[1,1024,2,512]{3,2,1,0:T(2,128)(2,1)} %param.10) | copy-start | bytes 6291460
  56.4 1.3 collective-permute-start
  57.8 6.6 %collective-permute-start.1 = (f32[128,128]{1,0:T(8,128)S(1)}, f32[128,128]{1,0:T(8,128)S(1)}, u32[]{:S(2)}, u32[]{:S(2)}) collective-permute-start(f32[128,128]{1,0:T(8,128)S(1)} %add.60), channel_id=1, source_target_pairs={{0,32},{16,48},{32,0},{48,16},{64,96},{80,112},{96,64},{112,80},{1... | collective-permute-start | bytes 196616 | tf_op jit(solution)/shard_map/ppermute | solution.py:481
  64.4 5.6 %collective-permute-start.4 = (f32[128,128]{1,0:T(8,128)S(1)}, f32[128,128]{1,0:T(8,128)S(1)}, u32[]{:S(2)}, u32[]{:S(2)}) collective-permute-start(f32[128,128]{1,0:T(8,128)S(1)} %add.61), channel_id=1, source_target_pairs={{0,192},{16,208},{32,224},{48,240},{64,128},{80,144},{96,160},{112... | collective-permute-start | bytes 196616 | tf_op jit(solution)/shard_map/ppermute | solution.py:481
  67.5 5.8 %collective-permute-start.3 = (f32[128,128]{1,0:T(8,128)S(1)}, f32[128,128]{1,0:T(8,128)S(1)}, u32[]{:S(2)}, u32[]{:S(2)}) collective-permute-start(f32[128,128]{1,0:T(8,128)S(1)} %add.61), channel_id=1, source_target_pairs={{0,128},{16,144},{32,160},{48,176},{64,192},{80,208},{96,224},{112... | collective-permute-start | bytes 196616 | tf_op jit(solution)/shard_map/ppermute | solution.py:481
  68.1 5.1 %collective-permute-start.2 = (f32[128,128]{1,0:T(8,128)S(1)}, f32[128,128]{1,0:T(8,128)S(1)}, u32[]{:S(2)}, u32[]{:S(2)}) collective-permute-start(f32[128,128]{1,0:T(8,128)S(1)} %add.61), channel_id=1, source_target_pairs={{0,64},{16,80},{32,96},{48,112},{64,0},{80,16},{96,32},{112,48},{1... | collective-permute-start | bytes 196616 | tf_op jit(solution)/shard_map/ppermute | solution.py:481
  77.8 37.0 %all-to-all-start.1 = ((bf16[16,32,1024]{2,1,0:T(8,128)(2,1)}), bf16[16,32,1024]{2,1,0:T(8,128)(2,1)}, u32[]{:S(2)}, u32[]{:S(2)}) async-start(bf16[16,32,1024]{2,1,0:T(8,128)(2,1)} %bitcast.35), calls=%async_computation.1 | async-start | bytes 2097152 | tf_op jit(solution)/shard_map/all_to_all | solution.py:473
  88.8 1.6 copy-start.22
  90.3 19.7 %copy-start.16 = (s32[512,128]{1,0:T(8,128)S(1)}, s32[512,128]{1,0:T(8,128)}, u32[]{:S(2)}) copy-start(s32[512,128]{1,0:T(8,128)} %copy-done.15) | copy-start | bytes 786436
  90.3 19.7 %copy-start.19 = (s32[512,128]{1,0:T(8,128)S(1)}, s32[512,128]{1,0:T(8,128)}, u32[]{:S(2)}) copy-start(s32[512,128]{1,0:T(8,128)} %copy-done.18) | copy-start | bytes 786436
  93.2 1.3 collective-permute-start.5
  94.6 7.6 %collective-permute-start.6 = (f32[128,128]{1,0:T(8,128)S(1)}, f32[128,128]{1,0:T(8,128)S(1)}, u32[]{:S(2)}, u32[]{:S(2)}) collective-permute-start(f32[128,128]{1,0:T(8,128)S(1)} %add.65), channel_id=1, source_target_pairs={{0,32},{16,48},{32,0},{48,16},{64,96},{80,112},{96,64},{112,80},{1... | collective-permute-start | bytes 196616 | tf_op jit(solution)/shard_map/ppermute | solution.py:481
  102.2 6.3 %collective-permute-start.9 = (f32[128,128]{1,0:T(8,128)S(1)}, f32[128,128]{1,0:T(8,128)S(1)}, u32[]{:S(2)}, u32[]{:S(2)}) collective-permute-start(f32[128,128]{1,0:T(8,128)S(1)} %add.66), channel_id=1, source_target_pairs={{0,192},{16,208},{32,224},{48,240},{64,128},{80,144},{96,160},{112... | collective-permute-start | bytes 196616 | tf_op jit(solution)/shard_map/ppermute | solution.py:481
  103.7 6.2 %collective-permute-start.8 = (f32[128,128]{1,0:T(8,128)S(1)}, f32[128,128]{1,0:T(8,128)S(1)}, u32[]{:S(2)}, u32[]{:S(2)}) collective-permute-start(f32[128,128]{1,0:T(8,128)S(1)} %add.66), channel_id=1, source_target_pairs={{0,128},{16,144},{32,160},{48,176},{64,192},{80,208},{96,224},{112... | collective-permute-start | bytes 196616 | tf_op jit(solution)/shard_map/ppermute | solution.py:481
  104.5 5.5 %collective-permute-start.7 = (f32[128,128]{1,0:T(8,128)S(1)}, f32[128,128]{1,0:T(8,128)S(1)}, u32[]{:S(2)}, u32[]{:S(2)}) collective-permute-start(f32[128,128]{1,0:T(8,128)S(1)} %add.66), channel_id=1, source_target_pairs={{0,64},{16,80},{32,96},{48,112},{64,0},{80,16},{96,32},{112,48},{1... | collective-permute-start | bytes 196616 | tf_op jit(solution)/shard_map/ppermute | solution.py:481
  114.9 8.5 %copy-start.34 = (f32[2,512]{1,0:T(2,128)S(1)}, f32[2,512]{1,0:T(2,128)}, u32[]{:S(2)}) copy-start(f32[2,512]{1,0:T(2,128)} %param.11) | copy-start | bytes 12292
  114.9 31.8 %all-to-all-start.3 = ((bf16[16,32,1024]{2,1,0:T(8,128)(2,1)}), bf16[16,32,1024]{2,1,0:T(8,128)(2,1)}, u32[]{:S(2)}, u32[]{:S(2)}) async-start(bf16[16,32,1024]{2,1,0:T(8,128)(2,1)} %bitcast.38), calls=%async_computation.3 | async-start | bytes 2097152 | tf_op jit(solution)/shard_map/all_to_all | solution.py:473
  150.7 28.8 %copy-start.6 = (bf16[512,1024]{1,0:T(8,128)(2,1)}, bf16[512,1024]{1,0:T(8,128)(2,1)S(1)}, u32[]{:S(2)}) copy-start(bf16[512,1024]{1,0:T(8,128)(2,1)S(1)} %get-tuple-element.38) | copy-start | bytes 3145732
  179.5 35.2 %all-to-all-start.4 = ((bf16[16,32,1024]{2,1,0:T(8,128)(2,1)}), bf16[16,32,1024]{2,1,0:T(8,128)(2,1)S(1)}, u32[]{:S(2)}, u32[]{:S(2)}) async-start(bf16[16,32,1024]{2,1,0:T(8,128)(2,1)} %bitcast.34), calls=%async_computation.4 | async-start | bytes 2097152 | tf_op jit(solution)/shard_map/all_to_all | solution.py:473
  184.7 1.2 copy-start.8
  185.9 19.2 %copy-start.9 = (bf16[16,32,1024]{2,1,0:T(8,128)(2,1)S(1)}, bf16[16,32,1024]{2,1,0:T(8,128)(2,1)}, u32[]{:S(2)}) copy-start(bf16[16,32,1024]{2,1,0:T(8,128)(2,1)} %all_to_all.31) | copy-start | bytes 3145732
  185.9 19.2 %copy-start.25 = (bf16[512,1024]{1,0:T(8,128)(2,1)S(1)}, bf16[512,1024]{1,0:T(8,128)(2,1)}, u32[]{:S(2)}) copy-start(bf16[512,1024]{1,0:T(8,128)(2,1)} %copy-done.24) | copy-start | bytes 3145732
  187.7 1.3 collective-permute-start.10
  189.1 11.5 %collective-permute-start.11 = (f32[128,128]{1,0:T(8,128)S(1)}, f32[128,128]{1,0:T(8,128)S(1)}, u32[]{:S(2)}, u32[]{:S(2)}) collective-permute-start(f32[128,128]{1,0:T(8,128)S(1)} %add.70), channel_id=1, source_target_pairs={{0,32},{16,48},{32,0},{48,16},{64,96},{80,112},{96,64},{112,80},{1... | collective-permute-start | bytes 196616 | tf_op jit(solution)/shard_map/ppermute | solution.py:481
  200.6 8.6 %collective-permute-start.14 = (f32[128,128]{1,0:T(8,128)S(1)}, f32[128,128]{1,0:T(8,128)S(1)}, u32[]{:S(2)}, u32[]{:S(2)}) collective-permute-start(f32[128,128]{1,0:T(8,128)S(1)} %add.71), channel_id=1, source_target_pairs={{0,192},{16,208},{32,224},{48,240},{64,128},{80,144},{96,160},{112... | collective-permute-start | bytes 196616 | tf_op jit(solution)/shard_map/ppermute | solution.py:481
  201.3 7.9 %collective-permute-start.13 = (f32[128,128]{1,0:T(8,128)S(1)}, f32[128,128]{1,0:T(8,128)S(1)}, u32[]{:S(2)}, u32[]{:S(2)}) collective-permute-start(f32[128,128]{1,0:T(8,128)S(1)} %add.71), channel_id=1, source_target_pairs={{0,128},{16,144},{32,160},{48,176},{64,192},{80,208},{96,224},{112... | collective-permute-start | bytes 196616 | tf_op jit(solution)/shard_map/ppermute | solution.py:481
  205.1 4.3 %collective-permute-start.12 = (f32[128,128]{1,0:T(8,128)S(1)}, f32[128,128]{1,0:T(8,128)S(1)}, u32[]{:S(2)}, u32[]{:S(2)}) collective-permute-start(f32[128,128]{1,0:T(8,128)S(1)} %add.71), channel_id=1, source_target_pairs={{0,64},{16,80},{32,96},{48,112},{64,0},{80,16},{96,32},{112,48},{1... | collective-permute-start | bytes 196616 | tf_op jit(solution)/shard_map/ppermute | solution.py:481
  205.1 4.3 %copy-start.27 = (bf16[1024,512]{1,0:T(8,128)(2,1)S(1)}, bf16[1024,512]{1,0:T(8,128)(2,1)}, u32[]{:S(2)}) copy-start(bf16[1024,512]{1,0:T(8,128)(2,1)} %copy-done.26) | copy-start | bytes 3145732
  205.1 4.3 %copy-start.29 = (s32[512,128]{1,0:T(8,128)S(1)}, s32[512,128]{1,0:T(8,128)}, u32[]{:S(2)}) copy-start(s32[512,128]{1,0:T(8,128)} %copy-done.28) | copy-start | bytes 786436
  205.2 4.3 %copy-start.31 = (s32[512,128]{1,0:T(8,128)S(1)}, s32[512,128]{1,0:T(8,128)}, u32[]{:S(2)}) copy-start(s32[512,128]{1,0:T(8,128)} %copy-done.30) | copy-start | bytes 786436
  207.2 2.0 copy-start.2
  212.8 2.0 copy-start
  214.8 14.2 %copy-start.3 = (f32[1024,1024]{1,0:T(8,128)S(1)}, f32[1024,1024]{1,0:T(8,128)}, u32[]{:S(2)}) copy-start(f32[1024,1024]{1,0:T(8,128)} %copy-done.2) | copy-start | bytes 12582916
  214.8 14.2 %copy-start.12 = (bf16[512,1024]{1,0:T(8,128)(2,1)S(1)}, bf16[512,1024]{1,0:T(8,128)(2,1)}, u32[]{:S(2)}) copy-start(bf16[512,1024]{1,0:T(8,128)(2,1)} %copy-done.11) | copy-start | bytes 3145732
  216.6 1.3 collective-permute-start.15
  217.9 6.8 %collective-permute-start.16 = (f32[128,128]{1,0:T(8,128)S(1)}, f32[128,128]{1,0:T(8,128)S(1)}, u32[]{:S(2)}, u32[]{:S(2)}) collective-permute-start(f32[128,128]{1,0:T(8,128)S(1)} %add.75), channel_id=1, source_target_pairs={{0,32},{16,48},{32,0},{48,16},{64,96},{80,112},{96,64},{112,80},{1... | collective-permute-start | bytes 196616 | tf_op jit(solution)/shard_map/ppermute | solution.py:481
  224.7 9.0 %collective-permute-start.19 = (f32[128,128]{1,0:T(8,128)S(1)}, f32[128,128]{1,0:T(8,128)S(1)}, u32[]{:S(2)}, u32[]{:S(2)}) collective-permute-start(f32[128,128]{1,0:T(8,128)S(1)} %add.76), channel_id=1, source_target_pairs={{0,192},{16,208},{32,224},{48,240},{64,128},{80,144},{96,160},{112... | collective-permute-start | bytes 196616 | tf_op jit(solution)/shard_map/ppermute | solution.py:481
  225.5 8.2 %collective-permute-start.18 = (f32[128,128]{1,0:T(8,128)S(1)}, f32[128,128]{1,0:T(8,128)S(1)}, u32[]{:S(2)}, u32[]{:S(2)}) collective-permute-start(f32[128,128]{1,0:T(8,128)S(1)} %add.76), channel_id=1, source_target_pairs={{0,128},{16,144},{32,160},{48,176},{64,192},{80,208},{96,224},{112... | collective-permute-start | bytes 196616 | tf_op jit(solution)/shard_map/ppermute | solution.py:481
  228.8 5.0 %collective-permute-start.17 = (f32[128,128]{1,0:T(8,128)S(1)}, f32[128,128]{1,0:T(8,128)S(1)}, u32[]{:S(2)}, u32[]{:S(2)}) collective-permute-start(f32[128,128]{1,0:T(8,128)S(1)} %add.76), channel_id=1, source_target_pairs={{0,64},{16,80},{32,96},{48,112},{64,0},{80,16},{96,32},{112,48},{1... | collective-permute-start | bytes 196616 | tf_op jit(solution)/shard_map/ppermute | solution.py:481
  231.0 2.8 %copy-start.5 = (bf16[1024,512]{1,0:T(8,128)(2,1)S(1)}, bf16[1024,512]{1,0:T(8,128)(2,1)}, u32[]{:S(2)}) copy-start(bf16[1024,512]{1,0:T(8,128)(2,1)} %copy-done.4) | copy-start | bytes 3145732
  233.8 2.2 copy-start.1
  (11 other events, 10.3 us)

commit v3 on v2

v3 whole, which is shorter than its diff:
```python
import functools
import math

import jax
import jax.numpy as jnp
from jax import lax
from jax.experimental import pallas as pl
from jax.experimental.pallas import tpu as pltpu
from jax.sharding import PartitionSpec as P

D = 8192
L = 2
CAP = 64
GROUPS = 16
CHUNKS = (32, 32)
LANES = 128
KEPT = 32
PER = LANES // KEPT
BF16 = jnp.bfloat16
F32 = jnp.float32
I32 = jnp.int32
ROW_BLOCK = 256
VMEM_LIMIT = 20 * 1024 * 1024


def iota(shape, dim):
    return lax.broadcasted_iota(I32, shape, dim)


def params():
    return pltpu.CompilerParams(vmem_limit_bytes=VMEM_LIMIT)


def cost(flops, nbytes):
    return pl.CostEstimate(flops=int(flops), bytes_accessed=int(nbytes), transcendentals=0)


def hbm(shape, dtype):
    return pltpu.HBM(shape, dtype)


def vmem(shape, dtype):
    return pltpu.VMEM(shape, dtype)


def in_hbm(x):
    return pltpu.with_memory_space_constraint(x, pltpu.HBM)


def in_vmem(x):
    return pltpu.with_memory_space_constraint(x, pltpu.VMEM)


def whole():
    return pl.BlockSpec(memory_space=pltpu.VMEM)


def offsets():
    out, start = [], 0
    for cap in CHUNKS:
        out.append((start, cap))
        start += cap
    return out


def chunk_hits(info, off, cap, tokens):
    rows = iota((GROUPS * cap, tokens), 0)

    def slot(route, pos):
        inside = (pos >= off) & (pos < off + cap)
        return jnp.where(inside, route * cap + (pos - off), -1)

    return (rows == slot(info[0:1], info[1:2])) | (rows == slot(info[2:3], info[3:4]))


def pack_kernel(routes_ref, acts_ref, index_ref, info_ref, *send_refs):
    tokens, inner = acts_ref.shape
    upper = (iota((tokens, tokens), 0) < iota((tokens, tokens), 1)).astype(F32).astype(BF16)
    experts = iota((GROUPS, tokens), 0)
    total = jnp.zeros((GROUPS, 1), F32)
    rows = []
    for j in range(2):
        route = routes_ref[j : j + 1, :]
        hit = experts == route
        hot = hit.astype(F32)
        before = jnp.dot(hot.astype(BF16), upper, preferred_element_type=F32) + total
        total = total + jnp.sum(hot, axis=1, keepdims=True)
        pos = jnp.sum(jnp.where(hit, before, 0.0), axis=0, keepdims=True).astype(I32)
        rows += [route, pos]
    info = jnp.concatenate(rows + [jnp.zeros((4, tokens), I32)], axis=0)
    info_ref[...] = info
    x = acts_ref[...]
    for (off, cap), send_ref in zip(offsets(), send_refs):
        hits = chunk_hits(info, off, cap, tokens).astype(F32).astype(BF16)
        send_ref[:, :inner] = jnp.dot(hits, x, preferred_element_type=F32).astype(BF16)
    send_refs[0][:, inner:] = index_codes(info, index_ref[...])


def index_codes(info, index):
    tokens, cols = index.shape
    code = (((index & 127) + 128) << (index >> 7)).astype(F32).astype(BF16)
    col = iota((cols, LANES), 0)
    lane = iota((cols, LANES), 1)
    first = CHUNKS[0]
    rows_total = GROUPS * first
    row = iota((rows_total, tokens), 0)
    expert, inner = row // first, row % first
    base = jnp.full((rows_total, tokens), -(1 << 20), I32)
    step = jnp.zeros((rows_total, tokens), I32)
    for off, cap in offsets():
        here = (inner >= off // PER) & (inner < (off + cap) // PER)
        base = jnp.where(here, expert * CAP + off + inner - off // PER, base)
        step = jnp.where(here, cap // PER, step)
    lane_q = iota((rows_total, LANES), 1) // KEPT
    result = jnp.zeros((rows_total, LANES), F32)
    for j in range(2):
        spread = (col == j * KEPT + lane % KEPT).astype(F32).astype(BF16)
        codes = jnp.dot(code, spread, preferred_element_type=F32).astype(BF16)
        key = info[2 * j : 2 * j + 1] * CAP + info[2 * j + 1 : 2 * j + 2]
        for q in range(PER):
            hit = (base + step * q == key).astype(F32).astype(BF16)
            picked = jnp.dot(hit, codes, preferred_element_type=F32)
            result = result + jnp.where(lane_q == q, picked, 0.0)
    return result.astype(BF16)


def pack(routes_t, x, index):
    tokens, width = x.shape
    widths = [width + LANES] + [width] * (len(CHUNKS) - 1)
    return pl.pallas_call(
        pack_kernel,
        out_shape=(jax.ShapeDtypeStruct((8, tokens), I32),)
        + tuple(jax.ShapeDtypeStruct((GROUPS * c, w), BF16) for c, w in zip(CHUNKS, widths)),
        in_specs=[whole()] * 3,
        out_specs=(whole(),) * (1 + len(CHUNKS)),
        compiler_params=params(),
        cost_estimate=cost(2 * GROUPS * CAP * tokens * width, 3 << 20),
        name="pack_tokens",
    )(routes_t, x, index)


def numbers_kernel(codes_ref, *refs):
    first = CHUNKS[0]
    code = codes_ref[...].astype(F32).astype(I32)
    tile = jnp.zeros(code.shape, I32)
    for h in range(7):
        tile = tile + jnp.where(code >= (256 << h), 1, 0)
    numbers = jnp.where(code > 0, tile * 128 + (code >> tile) - 128, -1)
    for (off, cap), index_ref in zip(offsets(), refs):
        for src in range(GROUPS):
            start = src * first + off // PER
            index_ref[src] = numbers[start : start + cap // PER]
    maps_kernel(refs[0], *refs[len(CHUNKS) :])


def maps_kernel(index_ref, low_ref, high_ref, scratch_ref):
    packed = index_ref.shape[1]
    cap = packed * PER
    turned = jnp.concatenate([index_ref[src] for src in range(GROUPS)], axis=0).T
    tile = turned >> 7
    scratch_ref[0] = jnp.where(turned >= 0, turned & 127, -1)
    place = (iota(turned.shape, 0) % KEPT) + 1
    scratch_ref[1] = jnp.where((tile >= 0) & (tile < 4), place << (jnp.clip(tile, 0, 3) * 6), 0)
    scratch_ref[2] = jnp.where(tile >= 4, place << (jnp.clip(tile - 4, 0, 3) * 6), 0)
    for q in range(PER):
        lows, highs = [], []
        for part in range(2):
            size = LANES // 2
            spot = iota((size, LANES), 0) + part * size
            low = jnp.zeros((size, LANES), I32)
            high = jnp.zeros((size, LANES), I32)
            for k in range(KEPT):
                at = q * KEPT + k
                same = spot == scratch_ref[0, at : at + 1, :]
                low = low + jnp.where(same, scratch_ref[1, at : at + 1, :], 0)
                high = high + jnp.where(same, scratch_ref[2, at : at + 1, :], 0)
            lows.append(low)
            highs.append(high)
        low = jnp.concatenate(lows, axis=0).T
        high = jnp.concatenate(highs, axis=0).T
        for src in range(GROUPS):
            row = src * cap + q * packed
            low_ref[row : row + packed, :] = low[src * packed : (src + 1) * packed]
            high_ref[row : row + packed, :] = high[src * packed : (src + 1) * packed]


def map_shapes(cap):
    return [jax.ShapeDtypeStruct((GROUPS * cap, LANES), I32)] * 2


def slot_numbers(arrived):
    rows, width = arrived.shape
    shapes = [jax.ShapeDtypeStruct((GROUPS, cap // PER, LANES), I32) for cap in CHUNKS]
    shapes += map_shapes(CHUNKS[0])
    out = pl.pallas_call(
        numbers_kernel,
        grid=(1,),
        out_shape=tuple(shapes),
        in_specs=[pl.BlockSpec((rows, LANES), lambda i: (0, width // LANES - 1))],
        out_specs=tuple(
            pl.BlockSpec(s.shape, functools.partial(lambda n, i: (0,) * n, len(s.shape))) for s in shapes
        ),
        scratch_shapes=[pltpu.VMEM((3, LANES, LANES), I32)],
        compiler_params=params(),
        cost_estimate=cost(2_000_000_000, 1 << 20),
        name="slot_numbers",
    )(arrived)
    return out[: len(CHUNKS)], [out[len(CHUNKS) :]]


def later_maps_kernel(index_ref, low_ref, high_ref, token_ref, scratch_ref):
    token_ref[...] = jnp.zeros_like(token_ref)
    maps_kernel(index_ref, low_ref, high_ref, scratch_ref)


def slot_maps(index):
    cap = index.shape[1] * PER
    return pl.pallas_call(
        later_maps_kernel,
        out_shape=tuple(map_shapes(cap)) + (TOKEN,),
        in_specs=[whole()],
        out_specs=(whole(),) * 3,
        scratch_shapes=[pltpu.VMEM((3, LANES, LANES), I32)],
        compiler_params=params(),
        cost_estimate=cost(2_000_000_000, 1 << 20),
        name="slot_maps",
    )(index)


def skipping(kernel, inputs, extra):
    def run(*refs):
        kernel(*refs[:inputs], *refs[inputs + extra :])

    return run


TOKEN = jax.ShapeDtypeStruct((8, LANES), F32)


def token_spec():
    return pl.BlockSpec((8, LANES), lambda *i: (0, 0))


def gather_kept(values_ref, index_ref, out_ref, stride, base, start):
    tiles = values_ref.shape[1] // LANES
    packed_rows = index_ref.shape[1]
    lane_q = iota((8, LANES), 1) // KEPT
    for src in range(GROUPS):
        for half in range(packed_rows // 8):
            idx = index_ref[src, half * 8 : half * 8 + 8, :]
            spot, tile = idx & 127, idx >> 7
            result = jnp.zeros((8, LANES), F32)
            for q in range(PER):
                row = src * stride + base + q * packed_rows + half * 8
                here = jnp.where(lane_q == q, tile, -1)
                for t in range(tiles):
                    part = values_ref[row : row + 8, t * LANES : (t + 1) * LANES]
                    taken = jnp.take_along_axis(part, spot, axis=1, mode="promise_in_bounds")
                    result = jnp.where(here == t, taken, result)
            place = start + src * packed_rows + half * 8
            out_ref[place : place + 8, :] = result


def encode_kernel(x_ref, w_ref, bias_ref, index_ref, out_ref, values_ref):
    inner = w_ref.shape[0]
    values_ref[...] = (
        jnp.dot(x_ref[:, :inner], w_ref[...], preferred_element_type=F32) + bias_ref[...]
    )
    gather_kept(values_ref, index_ref, out_ref, index_ref.shape[1] * PER, 0, 0)


def encode(rows, weight, bias, index, after):
    total, latents = rows.shape[0], weight.shape[1]
    return pl.pallas_call(
        skipping(encode_kernel, 4, len(after)),
        out_shape=jax.ShapeDtypeStruct((total // PER, LANES), F32),
        in_specs=[whole()] * (4 + len(after)),
        out_specs=whole(),
        scratch_shapes=[pltpu.VMEM((total, latents), F32)],
        compiler_params=params(),
        cost_estimate=cost(4 * total * 1024 * latents, 4 << 20),
        name="encode",
    )(rows, weight, bias, index, *after)


def latent_gradient_kernel(r_ref, w_ref, *refs):
    index_refs, out_ref, values_ref = refs[:-2], refs[-2], refs[-1]
    values_ref[...] = lax.dot_general(
        r_ref[...], w_ref[...], (((1,), (1,)), ((), ())), preferred_element_type=F32
    )
    start = 0
    for (off, cap), index_ref in zip(offsets(), index_refs):
        gather_kept(values_ref, index_ref, out_ref, CAP, off, start)
        start += GROUPS * cap // PER


def latent_gradient(rows, weight, index):
    total, latents = rows.shape[0], weight.shape[0]
    return pl.pallas_call(
        latent_gradient_kernel,
        out_shape=jax.ShapeDtypeStruct((total // PER, LANES), F32),
        in_specs=[whole()] * (2 + len(index)),
        out_specs=whole(),
        scratch_shapes=[pltpu.VMEM((total, latents), F32)],
        compiler_params=params(),
        cost_estimate=cost(4 * total * 1024 * latents, 4 << 20),
        name="latent_gradient",
    )(rows, weight, *index)


def spread_kept(kept_ref, low_ref, high_ref, dense_ref, groups, packed_rows, source=0, target=0):
    for src in range(groups):
        for q in range(0, PER, 2):
            row = src * packed_rows * PER + q * packed_rows
            kept = kept_ref[src * packed_rows : (src + 1) * packed_rows, :]
            rows = pl.ds(source + row, 2 * packed_rows)
            words = (low_ref[rows, :], high_ref[rows, :])
            kept = jnp.concatenate([kept, kept], axis=0)
            shift = (iota((2 * packed_rows, LANES), 0) // packed_rows + q) * KEPT
            for t in range(8):
                which = (words[t // 4] >> (6 * (t % 4))) & 63
                spot = jnp.maximum(which - 1, 0) + shift
                taken = jnp.take_along_axis(kept, spot, axis=1, mode="promise_in_bounds")
                dense_ref[target + row : target + row + 2 * packed_rows, t * LANES : (t + 1) * LANES] = (
                    jnp.where(which > 0, taken, 0.0).astype(BF16)
                )


def decode_kernel(packed_rows, pre_ref, low_ref, high_ref, w_ref, latent_ref, out_ref, token_ref, kept_ref):
    token_ref[...] = jnp.zeros_like(token_ref)
    pre = pre_ref[...]
    kept_ref[...] = (pre / (1.0 + jnp.exp(-pre))).astype(BF16).astype(F32)
    base = pl.multiple_of(pl.program_id(0) * ROW_BLOCK, ROW_BLOCK)
    groups = ROW_BLOCK // (packed_rows * PER)
    spread_kept(kept_ref, low_ref, high_ref, latent_ref, groups, packed_rows, base)
    out_ref[...] = jnp.dot(latent_ref[...], w_ref[...], preferred_element_type=F32).astype(BF16)


def decode(pre, low, high, weight, packed_rows, after):
    total = low.shape[0]
    latents, inner = weight.shape
    by_row = lambda i: (i, 0)
    return pl.pallas_call(
        skipping(functools.partial(decode_kernel, packed_rows), 4, len(after)),
        grid=(total // ROW_BLOCK,),
        out_shape=(hbm((total, latents), BF16), hbm((total, inner), BF16), TOKEN),
        in_specs=[pl.BlockSpec((ROW_BLOCK // PER, LANES), by_row)] + [whole()] * (3 + len(after)),
        out_specs=(
            pl.BlockSpec((ROW_BLOCK, latents), by_row),
            pl.BlockSpec((ROW_BLOCK, inner), by_row),
            token_spec(),
        ),
        scratch_shapes=[pltpu.VMEM((ROW_BLOCK // PER, LANES), F32)],
        compiler_params=params(),
        cost_estimate=cost(4 * total * inner * latents, 6 << 20),
        name="decode",
    )(pre, low, high, weight, *after)


def residual_kernel(*refs):
    count = len(CHUNKS)
    info_ref, x_ref, bias_ref = refs[:3]
    back_refs, send_ref = refs[3 : 3 + count], refs[3 + count]
    tokens = x_ref.shape[0]
    info = info_ref[...]
    total = jnp.zeros(x_ref.shape, F32)
    for (off, cap), back_ref in zip(offsets(), back_refs):
        hit = chunk_hits(info, off, cap, tokens).astype(F32).astype(BF16)
        total = total + lax.dot_general(
            hit, back_ref[...], (((0,), (0,)), ((), ())), preferred_element_type=F32
        )
    residual = (total + bias_ref[...] - x_ref[...].astype(F32)).astype(BF16)
    hit = chunk_hits(info, 0, CAP, tokens).astype(F32).astype(BF16)
    send_ref[...] = jnp.dot(hit, residual, preferred_element_type=F32).astype(BF16)


def form_residual(info, x, bias, back, after):
    tokens, width = x.shape
    return pl.pallas_call(
        skipping(residual_kernel, 3 + len(CHUNKS), len(after)),
        out_shape=jax.ShapeDtypeStruct((GROUPS * CAP, width), BF16),
        in_specs=[whole()] * (3 + len(CHUNKS) + len(after)),
        out_specs=whole(),
        compiler_params=params(),
        cost_estimate=cost(4 * GROUPS * CAP * tokens * width, 5 << 20),
        name="form_residual",
    )(info, x, bias, *back, *after)


def turn_kernel(*refs):
    half = (len(refs) - 1) // 2
    refs[-1][...] = jnp.zeros(refs[-1].shape, F32)
    for src, dst in zip(refs[:half], refs[half:]):
        block = dst.shape[0]
        here = pl.ds(pl.multiple_of(pl.program_id(0) * block, block), block)
        dst[...] = src[:, here].T


def turn(arrived, inner):
    return pl.pallas_call(
        turn_kernel,
        grid=(4,),
        out_shape=tuple(hbm((inner, a.shape[0]), BF16) for a in arrived) + (TOKEN,),
        in_specs=[whole()] * len(arrived),
        out_specs=tuple(pl.BlockSpec((inner // 4, a.shape[0]), lambda i: (i, 0)) for a in arrived)
        + (token_spec(),),
        compiler_params=params(),
        cost_estimate=cost(4_000_000_000, 4 << 20),
        name="turn_rows",
    )(*arrived)


def encoder_grad_kernel(scale, lg_ref, *refs):
    count = len(CHUNKS)
    pre_refs, map_refs, x_refs = refs[:count], refs[count : 3 * count], refs[3 * count : 4 * count]
    out_ref, grad_ref, kept_ref = refs[4 * count :]

    @pl.when(pl.program_id(0) == 0)
    def _():
        start = 0
        for c, cap in enumerate(CHUNKS):
            packed = GROUPS * cap // PER
            pre = pre_refs[c][...]
            sig = 1.0 / (1.0 + jnp.exp(-pre))
            slope = lg_ref[start : start + packed, :] * (sig * (1.0 + pre * (1.0 - sig)))
            kept_ref[...] = slope.astype(BF16).astype(F32)
            words = map_refs[2 * c : 2 * c + 2]
            spread_kept(kept_ref, *words, grad_ref, GROUPS, cap // PER, 0, start * PER)
            start += packed

    total, start = None, 0
    for c, cap in enumerate(CHUNKS):
        rows = GROUPS * cap
        part = jnp.dot(
            x_refs[c][...], grad_ref[start : start + rows, :], preferred_element_type=F32
        )
        total = part if total is None else total + part
        start += rows
    out_ref[...] = (total * scale).astype(BF16)


def encoder_grad(lg, pre, maps, turned, scale):
    latents = 1024
    inner = turned[0].shape[0]
    block = 256
    rows = GROUPS * CHUNKS[0]
    operands = [lg, *pre, *[m for pair in maps for m in pair]]
    return pl.pallas_call(
        functools.partial(encoder_grad_kernel, scale),
        grid=(inner // block,),
        out_shape=jax.ShapeDtypeStruct((inner, latents), BF16),
        in_specs=[whole()] * len(operands)
        + [pl.BlockSpec((block, t.shape[1]), lambda i: (i, 0)) for t in turned],
        out_specs=pl.BlockSpec((block, latents), lambda i: (i, 0)),
        scratch_shapes=[
            pltpu.VMEM((GROUPS * CAP, latents), BF16),
            pltpu.VMEM((rows // PER, LANES), F32),
        ],
        compiler_params=params(),
        cost_estimate=cost(4 * 1024 * inner * latents, 6 << 20),
        name="encoder_grad",
    )(*operands, *[in_hbm(t) for t in turned])


def decoder_grad_kernel(*refs):
    latent_refs, res_ref, out_ref = refs[:-2], refs[-2], refs[-1]
    block = out_ref.shape[0]
    here = pl.ds(pl.multiple_of(pl.program_id(0) * block, block), block)
    total = None
    for (off, cap), latent_ref in zip(offsets(), latent_refs):
        rows = [res_ref[src * CAP + off : src * CAP + off + cap, :] for src in range(GROUPS)]
        part = lax.dot_general(
            latent_ref[:, here],
            jnp.concatenate(rows, axis=0),
            (((0,), (0,)), ((), ())),
            preferred_element_type=F32,
        )
        total = part if total is None else total + part
    out_ref[...] = total.astype(BF16)


def decoder_grad(latent, res):
    latents, inner = latent[0].shape[1], res.shape[1]
    block = 256
    return pl.pallas_call(
        decoder_grad_kernel,
        grid=(latents // block,),
        out_shape=jax.ShapeDtypeStruct((latents, inner), BF16),
        in_specs=[whole()] * (len(latent) + 1),
        out_specs=pl.BlockSpec((block, inner), lambda i: (i, 0)),
        compiler_params=params(),
        cost_estimate=cost(2 * 1024 * inner * latents, 6 << 20),
        name="decoder_grad",
    )(*latent, res)


def exchange(rows):
    count, width = rows.shape
    return lax.all_to_all(
        rows.reshape(GROUPS, count // GROUPS, width), "feat", split_axis=0, concat_axis=0, tiled=True
    ).reshape(count, width)


def width_sum(part):
    for masks in ((1,), (4, 8, 12), (2,)):
        size = lax.axis_size("width")
        moved = [lax.ppermute(part, "width", [(a, a ^ m) for a in range(size)]) for m in masks]
        for other in moved:
            part = part + other
    return part


def per_device(acts, enc_weight, enc_bias, dec_weight, dec_bias, routes, latent_index):
    tokens, layers, width_dev = acts.shape
    inner = layers * width_dev
    latents = enc_weight.shape[3]
    scale = 1.0 / math.sqrt(L * D)
    x_home = in_vmem(acts.reshape(tokens, inner))
    enc = in_vmem(enc_weight.reshape(inner, latents))
    dec = in_vmem(dec_weight.reshape(latents, inner))
    bias = jnp.where(lax.axis_index("width") == 0, enc_bias, 0.0)

    info, *sends = pack(routes.T, x_home, latent_index.reshape(tokens, 2 * KEPT))
    arrived = [exchange(s) for s in sends]
    index, maps = slot_numbers(arrived[0])
    *later, token = slot_maps(index[1])
    maps.append(later)

    pre, latent, back, after, tokens_in = [], [], [], (), (token,)
    for c, cap in enumerate(CHUNKS):
        part = encode(in_vmem(arrived[c]), enc, bias, index[c], after)
        pre.append(width_sum(part))
        lat, decoded, token = decode(pre[c], *maps[c], dec, cap // PER, tokens_in)
        after, tokens_in = (token,), ()
        latent.append(lat)
        back.append(exchange(decoded))

    *turned, token = turn(arrived, inner)
    res = exchange(form_residual(info, x_home, dec_bias.reshape(1, inner), back, (token,)))
    lg = width_sum(latent_gradient(res, dec, index))
    grad_dec = decoder_grad(latent, res)
    grad_enc = encoder_grad(lg, pre, maps, turned, scale)
    return (
        grad_enc.reshape(1, layers, width_dev, latents),
        grad_dec.reshape(1, latents, layers, width_dev),
    )


def solution(mesh):
    placed = (
        P("feat", None, "width"),
        P("feat", None, "width", None),
        P("feat", None),
        P("feat", None, None, "width"),
        P(None, "width"),
        P("feat", None),
        P("feat", None, None),
    )
    return jax.shard_map(
        per_device,
        mesh=mesh,
        in_specs=placed,
        out_specs=(P("feat", None, "width", None), P("feat", None, None, "width")),
        check_vma=False,
    )
```

time: 244 us -> 228 us (0.934)
  blocking collectives: 68.6 us -> 94 us
  starting transfers between devices: 64 us -> 39 us
  local copies, waits for them, and re-layouts: 24.6 us -> 8.97 us
    all_to_all x2, blocking collectives: 68.6 us -> 94 us  [exchange(): lax.all_to_all(rows.reshape(GROUPS, count // GROUPS, width), 'feat', spli...]
    unnamed x73 -> x41, local copies, waits for them, and re-layouts: 21 us -> 5.29 us
    ppermute x20 -> x15, starting transfers between devices: 34.6 us -> 19.9 us  [width_sum(): lax.ppermute(part, 'width', [(a, a ^ m) for a in range(size)])]
    all_to_all x4 -> x3, starting transfers between devices: 29.4 us -> 19 us  [exchange(): lax.all_to_all(rows.reshape(GROUPS, count // GROUPS, width), 'feat', spli...]
    all_to_all x4 -> x3, waiting for transfers between devices: 18.7 us -> 22.9 us  [exchange(): lax.all_to_all(rows.reshape(GROUPS, count // GROUPS, width), 'feat', spli...]
    ppermute x20 -> x15, waiting for transfers between devices: 28.2 us -> 25.5 us  [width_sum(): lax.ppermute(part, 'width', [(a, a ^ m) for a in range(size)])]
    pallas_call x12 -> x10, Pallas kernels: 32.1 us -> 32.9 us  [the longest x1 8.24 us: encoder_grad(): pl.pallas_call(functools.partial(encoder_grad_kernel, scale), grid=(inner...]
  transfers between devices with their start and end apart: 24 -> 18, of which waited for: 14 -> 13; matrix products, arithmetic and copies ran while one was open for 1% -> 1% of each run, Pallas kernels for 11% -> 10%
where the time goes in v3:
time: 228 us
  blocking collectives  94 us (41%)
  waiting for transfers between devices  48.4 us (21%)
  starting transfers between devices  39 us (17%)
  Pallas kernels  36.1 us (16%)
  local copies, waits for them, and re-layouts  8.97 us (4%)
    all_to_all x2, blocking collectives, exchange(): lax.all_to_all(rows.reshape(GROUPS, count // GROUPS, width), 'feat', spli...  94 us
    ppermute x15, waiting for transfers between devices, width_sum(): lax.ppermute(part, 'width', [(a, a ^ m) for a in range(size)])  25.5 us
    all_to_all x3, waiting for transfers between devices, exchange(): lax.all_to_all(rows.reshape(GROUPS, count // GROUPS, width), 'feat', spli...  22.9 us
    ppermute x15, starting transfers between devices, width_sum(): lax.ppermute(part, 'width', [(a, a ^ m) for a in range(size)])  19.9 us
    all_to_all x3, starting transfers between devices, exchange(): lax.all_to_all(rows.reshape(GROUPS, count // GROUPS, width), 'feat', spli...  19 us
    pallas_call x1, Pallas kernels, encoder_grad(): pl.pallas_call(functools.partial(encoder_grad_kernel, scale), grid=(inner...  8.24 us
    pallas_call x2, Pallas kernels, decode(): pl.pallas_call(skipping(functools.partial(decode_kernel, packed_rows), 4,...  7.25 us
    unnamed x41, local copies, waits for them, and re-layouts  5.29 us
  transfers between devices with their start and end apart: 18, of which 13 were waited for; matrix products, arithmetic and copies ran while one was open for 1% of the time, Pallas kernels for 10%

profile of v3, /device:TPU:32, one launch (start us, length us, event | category | flops | bytes accessed | tf_op | source)
XLA Modules:
  0.0 227.6 jit_solution(7519693851331301582)
XLA Ops:
  0.6 0.9 copy.10.index_ref
  1.6 1.1 copy.11
  2.7 0.7 copy-done.7
  3.4 1.8 pack_tokens.1
  5.2 39.8 %all_to_all.25 = bf16[16,32,1152]{2,1,0:T(8,128)(2,1)S(1)} all-to-all(bf16[16,32,1152]{2,1,0:T(8,128)(2,1)S(1)} %bitcast.35), channel_id=1, replica_groups=mesh['width'=16,'feat'=16] {'feat'}, dimensions={0} | all-to-all | bytes 2359296 | tf_op jit(solution)/shard_map/all_to_all | solution.py:499
  45.1 4.8 %all-to-all-start.2 = ((bf16[16,32,1024]{2,1,0:T(8,128)(2,1)}), bf16[16,32,1024]{2,1,0:T(8,128)(2,1)}, u32[]{:S(2)}, u32[]{:S(2)}) async-start(bf16[16,32,1024]{2,1,0:T(8,128)(2,1)} %bitcast.7), calls=%async_computation.2 | async-start | bytes 2097152 | tf_op jit(solution)/shard_map/all_to_all | solution.py:499
  49.9 2.1 slot_numbers.1
  52.0 1.5 encode.2
  53.6 1.2 collective-permute-done
  54.9 3.1 %collective-permute-start.3 = (f32[128,128]{1,0:T(8,128)S(1)}, f32[128,128]{1,0:T(8,128)S(1)}, u32[]{:S(2)}, u32[]{:S(2)}) collective-permute-start(f32[128,128]{1,0:T(8,128)S(1)} %add.45), channel_id=1, source_target_pairs={{0,192},{16,208},{32,224},{48,240},{64,128},{80,144},{96,160},{112... | collective-permute-start | bytes 196616 | tf_op jit(solution)/shard_map/ppermute | solution.py:507
  58.0 0.6 collective-permute-start.2
  58.6 0.4 collective-permute-start.1
  59.1 0.6 copy.13
  59.6 1.4 collective-permute-done.3
  61.1 3.0 %collective-permute-done.2 = f32[128,128]{1,0:T(8,128)S(1)} collective-permute-done((f32[128,128]{1,0:T(8,128)S(1)}, f32[128,128]{1,0:T(8,128)S(1)}, u32[]{:S(2)}, u32[]{:S(2)}) %collective-permute-start.2) | collective-permute-done | bytes 65568 | tf_op jit(solution)/shard_map/ppermute | solution.py:507
  64.1 2.8 %collective-permute-start.4 = (f32[128,128]{1,0:T(8,128)S(1)}, f32[128,128]{1,0:T(8,128)S(1)}, u32[]{:S(2)}, u32[]{:S(2)}) collective-permute-start(f32[128,128]{1,0:T(8,128)S(1)} %add_add_fusion.2), channel_id=1, source_target_pairs={{0,32},{16,48},{32,0},{48,16},{64,96},{80,112},{96,64},{112,80},{1... | collective-permute-start | bytes 196616 | tf_op jit(solution)/shard_map/ppermute | solution.py:507
  66.9 2.0 slot_maps.1
  68.9 2.5 %collective-permute-done.4 = f32[128,128]{1,0:T(8,128)S(1)} collective-permute-done((f32[128,128]{1,0:T(8,128)S(1)}, f32[128,128]{1,0:T(8,128)S(1)}, u32[]{:S(2)}, u32[]{:S(2)}) %collective-permute-start.4) | collective-permute-done | bytes 65568 | tf_op jit(solution)/shard_map/ppermute | solution.py:507
  71.4 3.6 %decode.2 = (bf16[512,1024]{1,0:T(8,128)(2,1)}, bf16[512,1024]{1,0:T(8,128)(2,1)}, f32[8,128]{1,0:T(8,128)S(1)}) custom-call(f32[128,128]{1,0:T(8,128)S(1)} %add.49.refs_0_, s32[512,128]{1,0:T(8,128)S(1)} %get-tuple-element.23.refs_1_.refs_2_, s32[512,128]{1,0:T(8,128)S(1)} %get-tuple-element.24.refs_2_.refs_3_, bf16[1024,1024]{1,0:T(8,128)(2,1)S(1)} %bitcast.27, ...), custom_call_target="tpu_custom_call" | custom-call | flops 2147483648 | bytes 6291456 | tf_op jit(solution)/shard_map/decode/pallas_call | solution.py:343
  75.1 8.4 %all-to-all-start.1 = ((bf16[16,32,1024]{2,1,0:T(8,128)(2,1)}), bf16[16,32,1024]{2,1,0:T(8,128)(2,1)S(1)}, u32[]{:S(2)}, u32[]{:S(2)}) async-start(bf16[16,32,1024]{2,1,0:T(8,128)(2,1)} %bitcast.41), calls=%async_computation.1 | async-start | bytes 2097152 | tf_op jit(solution)/shard_map/all_to_all | solution.py:499
  83.4 1.6 copy-done.6
  85.0 2.9 %encode.3 = f32[128,128]{1,0:T(8,128)S(1)} custom-call(bf16[512,1024]{1,0:T(8,128)(2,1)} %bitcast.8.refs_0_.refs_1_, bf16[1024,1024]{1,0:T(8,128)(2,1)S(1)} %bitcast.38, f32[1,1024]{1,0:T(1,128)S(1)} %broadcast_select_fusion.refs_2_, s32[16,8,128]{2,1,0:T(8,128)S(1)} %get-tuple-element.25.index_ref.refs_3_.refs_1_, f32[8,128]{1,0:T(8,128)S(1)} %get-tuple-element.29.refs_4_), custom_call_target="tpu_custom_call" | custom-call | flops 2147483648 | bytes 4194304 | tf_op jit(solution)/shard_map/encode/pallas_call | solution.py:274
  88.0 1.2 collective-permute-done.5
  89.3 0.6 collective-permute-start.8
  89.9 0.9 collective-permute-start.7
  90.8 2.7 %collective-permute-start.6 = (f32[128,128]{1,0:T(8,128)S(1)}, f32[128,128]{1,0:T(8,128)S(1)}, u32[]{:S(2)}, u32[]{:S(2)}) collective-permute-start(f32[128,128]{1,0:T(8,128)S(1)} %add.50), channel_id=1, source_target_pairs={{0,64},{16,80},{32,96},{48,112},{64,0},{80,16},{96,32},{112,48},{1... | collective-permute-start | bytes 196616 | tf_op jit(solution)/shard_map/ppermute | solution.py:507
  93.4 2.7 %collective-permute-done.8 = f32[128,128]{1,0:T(8,128)S(1)} collective-permute-done((f32[128,128]{1,0:T(8,128)S(1)}, f32[128,128]{1,0:T(8,128)S(1)}, u32[]{:S(2)}, u32[]{:S(2)}) %collective-permute-start.8) | collective-permute-done | bytes 65568 | tf_op jit(solution)/shard_map/ppermute | solution.py:507
  96.1 0.6 collective-permute-done.6
  96.7 2.4 %collective-permute-start.9 = (f32[128,128]{1,0:T(8,128)S(1)}, f32[128,128]{1,0:T(8,128)S(1)}, u32[]{:S(2)}, u32[]{:S(2)}) collective-permute-start(f32[128,128]{1,0:T(8,128)S(1)} %add_add_fusion.1), channel_id=1, source_target_pairs={{0,32},{16,48},{32,0},{48,16},{64,96},{80,112},{96,64},{112,80},{1... | collective-permute-start | bytes 196616 | tf_op jit(solution)/shard_map/ppermute | solution.py:507
  99.1 4.9 %collective-permute-done.9 = f32[128,128]{1,0:T(8,128)S(1)} collective-permute-done((f32[128,128]{1,0:T(8,128)S(1)}, f32[128,128]{1,0:T(8,128)S(1)}, u32[]{:S(2)}, u32[]{:S(2)}) %collective-permute-start.9) | collective-permute-done | bytes 65568 | tf_op jit(solution)/shard_map/ppermute | solution.py:507
  104.0 3.6 %decode.3 = (bf16[512,1024]{1,0:T(8,128)(2,1)}, bf16[512,1024]{1,0:T(8,128)(2,1)}, f32[8,128]{1,0:T(8,128)}) custom-call(f32[128,128]{1,0:T(8,128)S(1)} %add.54.refs_0_.refs_1_, s32[512,128]{1,0:T(8,128)S(1)} %get-tuple-element.30.refs_1_.refs_4_, s32[512,128]{1,0:T(8,128)S(1)} %get-tuple-element.31.refs_2_.refs_5_, bf16[1024,1024]{1,0:T(8,128)(2,1)S(1)} %bitcast.28), custom_call_target="tpu_custom_call" | custom-call | flops 2147483648 | bytes 6291456 | tf_op jit(solution)/shard_map/decode/pallas_call | solution.py:343
  107.6 1.2 all-to-all-done.1
  108.9 5.9 %all-to-all-start.3 = ((bf16[16,32,1024]{2,1,0:T(8,128)(2,1)}), bf16[16,32,1024]{2,1,0:T(8,128)(2,1)S(1)}, u32[]{:S(2)}, u32[]{:S(2)}) async-start(bf16[16,32,1024]{2,1,0:T(8,128)(2,1)} %bitcast.42), calls=%async_computation.3 | async-start | bytes 2097152 | tf_op jit(solution)/shard_map/all_to_all | solution.py:499
  114.7 1.3 copy-done.4
  116.0 3.3 %turn_rows.1 = (bf16[1024,512]{1,0:T(8,128)(2,1)}, bf16[1024,512]{1,0:T(8,128)(2,1)}, f32[8,128]{1,0:T(8,128)S(1)}) custom-call(bf16[512,1152]{1,0:T(8,128)(2,1)S(1)} %bitcast.34, bf16[512,1024]{1,0:T(8,128)(2,1)} %bitcast.8.refs_0_.refs_1_), custom_call_target="tpu_custom_call" | custom-call | flops 4000000000 | bytes 4194304 | tf_op jit(solution)/shard_map/turn_rows/pallas_call | solution.py:400
  119.3 21.6 %all-to-all-done.3 = bf16[16,32,1024]{2,1,0:T(8,128)(2,1)S(1)} async-done(((bf16[16,32,1024]{2,1,0:T(8,128)(2,1)}), bf16[16,32,1024]{2,1,0:T(8,128)(2,1)S(1)}, u32[]{:S(2)}, u32[]{:S(2)}) %all-to-all-start.3) | async-done | bytes 1048608 | tf_op jit(solution)/shard_map/all_to_all | solution.py:499
  140.9 1.4 form_residual.1
  142.3 54.1 %all_to_all.26 = bf16[16,64,1024]{2,1,0:T(8,128)(2,1)S(1)} all-to-all(bf16[16,64,1024]{2,1,0:T(8,128)(2,1)S(1)} %bitcast.22), channel_id=1, replica_groups=mesh['width'=16,'feat'=16] {'feat'}, dimensions={0} | all-to-all | bytes 4194304 | tf_op jit(solution)/shard_map/all_to_all | solution.py:499
  196.5 2.8 %latent_gradient.1 = f32[256,128]{1,0:T(8,128)S(1)} custom-call(bf16[1024,1024]{1,0:T(8,128)(2,1)S(1)} %bitcast.30, bf16[1024,1024]{1,0:T(8,128)(2,1)S(1)} %bitcast.29, s32[16,8,128]{2,1,0:T(8,128)S(1)} %copy-done.13, s32[16,8,128]{2,1,0:T(8,128)S(1)} %copy-done.15), custom_call_target="tpu_custom_call" | custom-call | flops 4294967296 | bytes 4194304 | tf_op jit(solution)/shard_map/latent_gradient/pallas_call | solution.py:299
  199.4 1.3 collective-permute-done.10
  200.7 3.0 %collective-permute-start.13 = (f32[256,128]{1,0:T(8,128)S(1)}, f32[256,128]{1,0:T(8,128)S(1)}, u32[]{:S(2)}, u32[]{:S(2)}) collective-permute-start(f32[256,128]{1,0:T(8,128)S(1)} %add.55), channel_id=1, source_target_pairs={{0,192},{16,208},{32,224},{48,240},{64,128},{80,144},{96,160},{112... | collective-permute-start | bytes 393224 | tf_op jit(solution)/shard_map/ppermute | solution.py:507
  203.7 1.2 collective-permute-start.12
  204.9 4.6 %collective-permute-done.13 = f32[256,128]{1,0:T(8,128)S(1)} collective-permute-done((f32[256,128]{1,0:T(8,128)S(1)}, f32[256,128]{1,0:T(8,128)S(1)}, u32[]{:S(2)}, u32[]{:S(2)}) %collective-permute-start.13) | collective-permute-done | bytes 131104 | tf_op jit(solution)/shard_map/ppermute | solution.py:507
  209.6 2.0 collective-permute-done.12
  211.6 1.9 collective-permute-start.14
  213.5 3.0 %decoder_grad.1 = bf16[1024,1024]{1,0:T(8,128)(2,1)S(1)} custom-call(bf16[512,1024]{1,0:T(8,128)(2,1)S(1)} %copy-done.8, bf16[512,1024]{1,0:T(8,128)(2,1)S(1)} %copy-done.9, bf16[1024,1024]{1,0:T(8,128)(2,1)S(1)} %bitcast.31), custom_call_target="tpu_custom_call" | custom-call | flops 2147483648 | bytes 6291456 | tf_op jit(solution)/shard_map/decoder_grad/pallas_call | solution.py:485
  216.5 2.8 %reshape.71 = bf16[1,1024,2,512]{3,2,1,0:T(2,128)(2,1)} reshape(bf16[1024,1024]{1,0:T(8,128)(2,1)S(1)} %decoder_grad.1) | data formatting | bytes 4194304 | tf_op jit(solution)/shard_map/reshape | solution.py:545
  219.3 8.2 %encoder_grad.1 = bf16[1024,1024]{1,0:T(8,128)(2,1)} custom-call(f32[256,128]{1,0:T(8,128)S(1)} %add.59.lg_ref, f32[128,128]{1,0:T(8,128)S(1)} %add.49.refs_0_, f32[128,128]{1,0:T(8,128)S(1)} %add.54.refs_0_.refs_1_, s32[512,128]{1,0:T(8,128)S(1)} %get-tuple-element.23.refs_1_.refs_2_, s32[512,128]{1,0:T(8,128)S(1)} %get-tuple-element.24.refs_2_.refs_3_, ...), custom_call_target="tpu_custom_call" | custom-call | flops 4294967296 | bytes 6291456 | tf_op jit(solution)/shard_map/encoder_grad/pallas_call | solution.py:448
  (55 shorter events, 0.6 us)
Async XLA Ops:
  2.7 0.7 copy-start.7
  5.2 44.6 %copy-start.17 = (f32[1,1024]{1,0:T(1,128)S(1)}, f32[1,1024]{1,0:T(1,128)}, u32[]{:S(2)}) copy-start(f32[1,1024]{1,0:T(1,128)} %param.9) | copy-start | bytes 12292
  45.0 6.9 %copy-start.3 = (bf16[16,32,1152]{2,1,0:T(8,128)(2,1)}, bf16[16,32,1152]{2,1,0:T(8,128)(2,1)S(1)}, u32[]{:S(2)}) copy-start(bf16[16,32,1152]{2,1,0:T(8,128)(2,1)S(1)} %all_to_all.25) | copy-start | bytes 3538948
  45.1 30.0 %all-to-all-start.2 = ((bf16[16,32,1024]{2,1,0:T(8,128)(2,1)}), bf16[16,32,1024]{2,1,0:T(8,128)(2,1)}, u32[]{:S(2)}, u32[]{:S(2)}) async-start(bf16[16,32,1024]{2,1,0:T(8,128)(2,1)} %bitcast.7), calls=%async_computation.2 | async-start | bytes 2097152 | tf_op jit(solution)/shard_map/all_to_all | solution.py:499
  49.9 2.1 copy-start.5
  52.0 1.5 copy-start.12
  52.0 31.5 %copy-start.14 = (s32[16,8,128]{2,1,0:T(8,128)}, s32[16,8,128]{2,1,0:T(8,128)S(1)}, u32[]{:S(2)}) copy-start(s32[16,8,128]{2,1,0:T(8,128)S(1)} %get-tuple-element.25.index_ref.refs_3_.refs_1_) | copy-start | bytes 196612
  52.0 7.1 %copy-start.16 = (bf16[1,1024,2,512]{3,2,1,0:T(2,128)(2,1)S(1)}, bf16[1,1024,2,512]{3,2,1,0:T(2,128)(2,1)}, u32[]{:S(2)}) copy-start(bf16[1,1024,2,512]{3,2,1,0:T(2,128)(2,1)} %param.10) | copy-start | bytes 6291460
  53.5 1.3 collective-permute-start
  54.9 6.2 %collective-permute-start.3 = (f32[128,128]{1,0:T(8,128)S(1)}, f32[128,128]{1,0:T(8,128)S(1)}, u32[]{:S(2)}, u32[]{:S(2)}) collective-permute-start(f32[128,128]{1,0:T(8,128)S(1)} %add.45), channel_id=1, source_target_pairs={{0,192},{16,208},{32,224},{48,240},{64,128},{80,144},{96,160},{112... | collective-permute-start | bytes 196616 | tf_op jit(solution)/shard_map/ppermute | solution.py:507
  58.0 6.1 %collective-permute-start.2 = (f32[128,128]{1,0:T(8,128)S(1)}, f32[128,128]{1,0:T(8,128)S(1)}, u32[]{:S(2)}, u32[]{:S(2)}) collective-permute-start(f32[128,128]{1,0:T(8,128)S(1)} %add.45), channel_id=1, source_target_pairs={{0,128},{16,144},{32,160},{48,176},{64,192},{80,208},{96,224},{112... | collective-permute-start | bytes 196616 | tf_op jit(solution)/shard_map/ppermute | solution.py:507
  58.6 5.5 %collective-permute-start.1 = (f32[128,128]{1,0:T(8,128)S(1)}, f32[128,128]{1,0:T(8,128)S(1)}, u32[]{:S(2)}, u32[]{:S(2)}) collective-permute-start(f32[128,128]{1,0:T(8,128)S(1)} %add.45), channel_id=1, source_target_pairs={{0,64},{16,80},{32,96},{48,112},{64,0},{80,16},{96,32},{112,48},{1... | collective-permute-start | bytes 196616 | tf_op jit(solution)/shard_map/ppermute | solution.py:507
  59.6 11.8 %copy-start = (bf16[128,8,2,512]{3,1,2,0:T(8,128)(2,1)}, bf16[128,8,2,512]{3,1,2,0:T(8,128)(2,1)S(1)}, u32[]{:S(2)}) copy-start(bf16[128,8,2,512]{3,1,2,0:T(8,128)(2,1)S(1)} %copy.13) | copy-start | bytes 6291460
  64.1 7.3 %collective-permute-start.4 = (f32[128,128]{1,0:T(8,128)S(1)}, f32[128,128]{1,0:T(8,128)S(1)}, u32[]{:S(2)}, u32[]{:S(2)}) collective-permute-start(f32[128,128]{1,0:T(8,128)S(1)} %add_add_fusion.2), channel_id=1, source_target_pairs={{0,32},{16,48},{32,0},{48,16},{64,96},{80,112},{96,64},{112,80},{1... | collective-permute-start | bytes 196616 | tf_op jit(solution)/shard_map/ppermute | solution.py:507
  68.9 35.1 %copy-start.10 = (s32[512,128]{1,0:T(8,128)}, s32[512,128]{1,0:T(8,128)S(1)}, u32[]{:S(2)}) copy-start(s32[512,128]{1,0:T(8,128)S(1)} %get-tuple-element.31.refs_2_.refs_5_) | copy-start | bytes 786436
  75.1 33.8 %all-to-all-start.1 = ((bf16[16,32,1024]{2,1,0:T(8,128)(2,1)}), bf16[16,32,1024]{2,1,0:T(8,128)(2,1)S(1)}, u32[]{:S(2)}, u32[]{:S(2)}) async-start(bf16[16,32,1024]{2,1,0:T(8,128)(2,1)} %bitcast.41), calls=%async_computation.1 | async-start | bytes 2097152 | tf_op jit(solution)/shard_map/all_to_all | solution.py:499
  83.4 1.6 copy-start.6
  85.0 19.0 %copy-start.1 = (bf16[128,8,2,512]{3,1,2,0:T(8,128)(2,1)S(1)}, bf16[128,8,2,512]{3,1,2,0:T(8,128)(2,1)}, u32[]{:S(2)}) copy-start(bf16[128,8,2,512]{3,1,2,0:T(8,128)(2,1)} %copy-done) | copy-start | bytes 6291460
  87.9 1.3 collective-permute-start.5
  89.3 6.9 %collective-permute-start.8 = (f32[128,128]{1,0:T(8,128)S(1)}, f32[128,128]{1,0:T(8,128)S(1)}, u32[]{:S(2)}, u32[]{:S(2)}) collective-permute-start(f32[128,128]{1,0:T(8,128)S(1)} %add.50), channel_id=1, source_target_pairs={{0,192},{16,208},{32,224},{48,240},{64,128},{80,144},{96,160},{112... | collective-permute-start | bytes 196616 | tf_op jit(solution)/shard_map/ppermute | solution.py:507
  89.9 6.2 %collective-permute-start.7 = (f32[128,128]{1,0:T(8,128)S(1)}, f32[128,128]{1,0:T(8,128)S(1)}, u32[]{:S(2)}, u32[]{:S(2)}) collective-permute-start(f32[128,128]{1,0:T(8,128)S(1)} %add.50), channel_id=1, source_target_pairs={{0,128},{16,144},{32,160},{48,176},{64,192},{80,208},{96,224},{112... | collective-permute-start | bytes 196616 | tf_op jit(solution)/shard_map/ppermute | solution.py:507
  90.8 5.9 %collective-permute-start.6 = (f32[128,128]{1,0:T(8,128)S(1)}, f32[128,128]{1,0:T(8,128)S(1)}, u32[]{:S(2)}, u32[]{:S(2)}) collective-permute-start(f32[128,128]{1,0:T(8,128)S(1)} %add.50), channel_id=1, source_target_pairs={{0,64},{16,80},{32,96},{48,112},{64,0},{80,16},{96,32},{112,48},{1... | collective-permute-start | bytes 196616 | tf_op jit(solution)/shard_map/ppermute | solution.py:507
  96.7 7.3 %collective-permute-start.9 = (f32[128,128]{1,0:T(8,128)S(1)}, f32[128,128]{1,0:T(8,128)S(1)}, u32[]{:S(2)}, u32[]{:S(2)}) collective-permute-start(f32[128,128]{1,0:T(8,128)S(1)} %add_add_fusion.1), channel_id=1, source_target_pairs={{0,32},{16,48},{32,0},{48,16},{64,96},{80,112},{96,64},{112,80},{1... | collective-permute-start | bytes 196616 | tf_op jit(solution)/shard_map/ppermute | solution.py:507
  107.6 7.1 %copy-start.18 = (f32[2,512]{1,0:T(2,128)S(1)}, f32[2,512]{1,0:T(2,128)}, u32[]{:S(2)}) copy-start(f32[2,512]{1,0:T(2,128)} %param.11) | copy-start | bytes 12292
  108.9 32.1 %all-to-all-start.3 = ((bf16[16,32,1024]{2,1,0:T(8,128)(2,1)}), bf16[16,32,1024]{2,1,0:T(8,128)(2,1)S(1)}, u32[]{:S(2)}, u32[]{:S(2)}) async-start(bf16[16,32,1024]{2,1,0:T(8,128)(2,1)} %bitcast.42), calls=%async_computation.3 | async-start | bytes 2097152 | tf_op jit(solution)/shard_map/all_to_all | solution.py:499
  114.7 1.3 copy-start.4
  142.3 54.2 %copy-start.2 = (bf16[128,8,2,512]{3,1,2,0:T(8,128)(2,1)S(1)}, bf16[128,8,2,512]{3,1,2,0:T(8,128)(2,1)}, u32[]{:S(2)}) copy-start(bf16[128,8,2,512]{3,1,2,0:T(8,128)(2,1)} %copy-done) | copy-start | bytes 6291460
  142.3 54.1 %copy-start.13 = (s32[16,8,128]{2,1,0:T(8,128)S(1)}, s32[16,8,128]{2,1,0:T(8,128)}, u32[]{:S(2)}) copy-start(s32[16,8,128]{2,1,0:T(8,128)} %copy-done.12) | copy-start | bytes 196612
  142.3 54.1 %copy-start.15 = (s32[16,8,128]{2,1,0:T(8,128)S(1)}, s32[16,8,128]{2,1,0:T(8,128)}, u32[]{:S(2)}) copy-start(s32[16,8,128]{2,1,0:T(8,128)} %copy-done.14) | copy-start | bytes 196612
  196.5 17.0 %copy-start.8 = (bf16[512,1024]{1,0:T(8,128)(2,1)S(1)}, bf16[512,1024]{1,0:T(8,128)(2,1)}, u32[]{:S(2)}) copy-start(bf16[512,1024]{1,0:T(8,128)(2,1)} %get-tuple-element.36.refs_0_) | copy-start | bytes 3145732
  196.5 17.0 %copy-start.9 = (bf16[512,1024]{1,0:T(8,128)(2,1)S(1)}, bf16[512,1024]{1,0:T(8,128)(2,1)}, u32[]{:S(2)}) copy-start(bf16[512,1024]{1,0:T(8,128)(2,1)} %get-tuple-element.37.refs_1_) | copy-start | bytes 3145732
  199.3 1.4 collective-permute-start.10
  200.7 8.8 %collective-permute-start.13 = (f32[256,128]{1,0:T(8,128)S(1)}, f32[256,128]{1,0:T(8,128)S(1)}, u32[]{:S(2)}, u32[]{:S(2)}) collective-permute-start(f32[256,128]{1,0:T(8,128)S(1)} %add.55), channel_id=1, source_target_pairs={{0,192},{16,208},{32,224},{48,240},{64,128},{80,144},{96,160},{112... | collective-permute-start | bytes 393224 | tf_op jit(solution)/shard_map/ppermute | solution.py:507
  203.7 7.9 %collective-permute-start.12 = (f32[256,128]{1,0:T(8,128)S(1)}, f32[256,128]{1,0:T(8,128)S(1)}, u32[]{:S(2)}, u32[]{:S(2)}) collective-permute-start(f32[256,128]{1,0:T(8,128)S(1)} %add.55), channel_id=1, source_target_pairs={{0,128},{16,144},{32,160},{48,176},{64,192},{80,208},{96,224},{112... | collective-permute-start | bytes 393224 | tf_op jit(solution)/shard_map/ppermute | solution.py:507
  204.8 6.7 %collective-permute-start.11 = (f32[256,128]{1,0:T(8,128)S(1)}, f32[256,128]{1,0:T(8,128)S(1)}, u32[]{:S(2)}, u32[]{:S(2)}) collective-permute-start(f32[256,128]{1,0:T(8,128)S(1)} %add.55), channel_id=1, source_target_pairs={{0,64},{16,80},{32,96},{48,112},{64,0},{80,16},{96,32},{112,48},{1... | collective-permute-start | bytes 393224 | tf_op jit(solution)/shard_map/ppermute | solution.py:507
  211.6 7.7 %collective-permute-start.14 = (f32[256,128]{1,0:T(8,128)S(1)}, f32[256,128]{1,0:T(8,128)S(1)}, u32[]{:S(2)}, u32[]{:S(2)}) collective-permute-start(f32[256,128]{1,0:T(8,128)S(1)} %add_add_fusion), channel_id=1, source_target_pairs={{0,32},{16,48},{32,0},{48,16},{64,96},{80,112},{96,64},{112,80},{1... | collective-permute-start | bytes 393224 | tf_op jit(solution)/shard_map/ppermute | solution.py:507
  216.5 2.8 %copy-start.11 = (s32[512,128]{1,0:T(8,128)S(1)}, s32[512,128]{1,0:T(8,128)}, u32[]{:S(2)}) copy-start(s32[512,128]{1,0:T(8,128)} %copy-done.10) | copy-start | bytes 786436

commit v4 on v3

--- a/solution.py
+++ b/solution.py
@@ -14,12 +14,12 @@
 GROUPS = 16
 CHUNKS = (32, 32)
 LANES = 128
+BLOCK = 256
 KEPT = 32
 PER = LANES // KEPT
 BF16 = jnp.bfloat16
 F32 = jnp.float32
 I32 = jnp.int32
-ROW_BLOCK = 256
 VMEM_LIMIT = 20 * 1024 * 1024
 
 
@@ -283,6 +283,51 @@
     )(rows, weight, bias, index, *after)
 
 
+def encode_streamed_kernel(x_ref, w_ref, bias_ref, index_ref, out_ref, values_ref, x_held, w_held, sem_ref):
+    inner, latents = w_ref.shape
+    steps = inner // BLOCK
+    reads = []
+    for k in range(steps):
+        here = pl.ds(k * BLOCK, BLOCK)
+        reads.append(
+            (
+                pltpu.make_async_copy(x_ref.at[:, here], x_held.at[:, here], sem_ref.at[0, k]),
+                pltpu.make_async_copy(w_ref.at[here, :], w_held.at[here, :], sem_ref.at[1, k]),
+            )
+        )
+        for copy in reads[-1]:
+            copy.start()
+    for k in range(steps):
+        for copy in reads[k]:
+            copy.wait()
+        here = pl.ds(k * BLOCK, BLOCK)
+        part = jnp.dot(x_held[:, here], w_held[here, :], preferred_element_type=F32)
+        if k == 0:
+            values_ref[...] = part + bias_ref[...]
+        else:
+            values_ref[...] += part
+    gather_kept(values_ref, index_ref, out_ref, index_ref.shape[1] * PER, 0, 0)
+
+
+def encode_streamed(rows, weight, bias, index, after):
+    total, (inner, latents) = rows.shape[0], weight.shape
+    return pl.pallas_call(
+        skipping(encode_streamed_kernel, 4, len(after)),
+        out_shape=jax.ShapeDtypeStruct((total // PER, LANES), F32),
+        in_specs=[pl.BlockSpec(memory_space=pl.ANY)] * 2 + [whole()] * (2 + len(after)),
+        out_specs=whole(),
+        scratch_shapes=[
+            pltpu.VMEM((total, latents), F32),
+            pltpu.VMEM((total, inner), BF16),
+            pltpu.VMEM((inner, latents), BF16),
+            pltpu.SemaphoreType.DMA((2, inner // BLOCK)),
+        ],
+        compiler_params=params(),
+        cost_estimate=cost(4 * total * inner * latents, 4 << 20),
+        name="encode_streamed",
+    )(in_hbm(rows), in_hbm(weight), bias, index, *after)
+
+
 def latent_gradient_kernel(r_ref, w_ref, *refs):
     index_refs, out_ref, values_ref = refs[:-2], refs[-2], refs[-1]
     values_ref[...] = lax.dot_general(
@@ -308,53 +353,104 @@
     )(rows, weight, *index)
 
 
-def spread_kept(kept_ref, low_ref, high_ref, dense_ref, groups, packed_rows, source=0, target=0):
-    for src in range(groups):
+def spread_kept(kept_ref, low_ref, high_ref, dense_ref, packed_rows, tiles, source=0, target=0):
+    for src in range(GROUPS):
+        place = source + src * packed_rows
+        kept = kept_ref[place : place + packed_rows, :]
         for q in range(0, PER, 2):
             row = src * packed_rows * PER + q * packed_rows
-            kept = kept_ref[src * packed_rows : (src + 1) * packed_rows, :]
-            rows = pl.ds(source + row, 2 * packed_rows)
-            words = (low_ref[rows, :], high_ref[rows, :])
-            kept = jnp.concatenate([kept, kept], axis=0)
-            shift = (iota((2 * packed_rows, LANES), 0) // packed_rows + q) * KEPT
-            for t in range(8):
-                which = (words[t // 4] >> (6 * (t % 4))) & 63
-                spot = jnp.maximum(which - 1, 0) + shift
-                taken = jnp.take_along_axis(kept, spot, axis=1, mode="promise_in_bounds")
-                dense_ref[target + row : target + row + 2 * packed_rows, t * LANES : (t + 1) * LANES] = (
-                    jnp.where(which > 0, taken, 0.0).astype(BF16)
-                )
-
-
-def decode_kernel(packed_rows, pre_ref, low_ref, high_ref, w_ref, latent_ref, out_ref, token_ref, kept_ref):
-    token_ref[...] = jnp.zeros_like(token_ref)
+            for column, t in enumerate(tiles):
+                word_ref = (low_ref, high_ref)[t // 4]
+                pieces = []
+                for half in range(2):
+                    start = row + half * packed_rows
+                    which = (word_ref[start : start + packed_rows, :] >> (6 * (t % 4))) & 63
+                    spot = jnp.maximum(which - 1, 0) + (q + half) * KEPT
+                    taken = jnp.take_along_axis(kept, spot, axis=1, mode="promise_in_bounds")
+                    pieces.append(jnp.where(which > 0, taken, 0.0))
+                rows = slice(target + row, target + row + 2 * packed_rows)
+                dense_ref[rows, column * LANES : (column + 1) * LANES] = jnp.concatenate(
+                    pieces, axis=0
+                ).astype(BF16)
+
+
+def spread_latents(pre_ref, low_ref, high_ref, kept_ref, rows_ref):
     pre = pre_ref[...]
     kept_ref[...] = (pre / (1.0 + jnp.exp(-pre))).astype(BF16).astype(F32)
-    base = pl.multiple_of(pl.program_id(0) * ROW_BLOCK, ROW_BLOCK)
-    groups = ROW_BLOCK // (packed_rows * PER)
-    spread_kept(kept_ref, low_ref, high_ref, latent_ref, groups, packed_rows, base)
-    out_ref[...] = jnp.dot(latent_ref[...], w_ref[...], preferred_element_type=F32).astype(BF16)
-
-
-def decode(pre, low, high, weight, packed_rows, after):
+    tiles = range(rows_ref.shape[1] // LANES)
+    spread_kept(kept_ref, low_ref, high_ref, rows_ref, pre_ref.shape[0] // GROUPS, tiles)
+
+
+def decode_kernel(pre_ref, low_ref, high_ref, w_ref, out_ref, token_ref, kept_ref, rows_ref, made_ref, sem_ref):
+    token_ref[...] = jnp.zeros_like(token_ref)
+    spread_latents(pre_ref, low_ref, high_ref, kept_ref, rows_ref)
+    copies = []
+    for j in range(w_ref.shape[1] // BLOCK):
+        here = pl.ds(j * BLOCK, BLOCK)
+        made_ref[:, here] = jnp.dot(
+            rows_ref[...], w_ref[:, here], preferred_element_type=F32
+        ).astype(BF16)
+        copy = pltpu.make_async_copy(made_ref.at[:, here], out_ref.at[:, here], sem_ref.at[j])
+        copy.start()
+        copies.append(copy)
+    for copy in copies:
+        copy.wait()
+
+
+def anywhere():
+    return pl.BlockSpec(memory_space=pl.ANY)
+
+
+def decode(pre, low, high, weight, after):
     total = low.shape[0]
     latents, inner = weight.shape
-    by_row = lambda i: (i, 0)
-    return pl.pallas_call(
-        skipping(functools.partial(decode_kernel, packed_rows), 4, len(after)),
-        grid=(total // ROW_BLOCK,),
-        out_shape=(hbm((total, latents), BF16), hbm((total, inner), BF16), TOKEN),
-        in_specs=[pl.BlockSpec((ROW_BLOCK // PER, LANES), by_row)] + [whole()] * (3 + len(after)),
-        out_specs=(
-            pl.BlockSpec((ROW_BLOCK, latents), by_row),
-            pl.BlockSpec((ROW_BLOCK, inner), by_row),
-            token_spec(),
-        ),
-        scratch_shapes=[pltpu.VMEM((ROW_BLOCK // PER, LANES), F32)],
+    return pl.pallas_call(
+        skipping(decode_kernel, 4, len(after)),
+        out_shape=(hbm((total, inner), BF16), TOKEN),
+        in_specs=[whole()] * (4 + len(after)),
+        out_specs=(anywhere(), whole()),
+        scratch_shapes=[
+            pltpu.VMEM(pre.shape, F32),
+            pltpu.VMEM((total, latents), BF16),
+            pltpu.VMEM((total, inner), BF16),
+            pltpu.SemaphoreType.DMA((inner // BLOCK,)),
+        ],
         compiler_params=params(),
         cost_estimate=cost(4 * total * inner * latents, 6 << 20),
         name="decode",
     )(pre, low, high, weight, *after)
+
+
+def latents_kernel(*refs):
+    count = len(CHUNKS)
+    pre_refs, map_refs = refs[:count], refs[count : 3 * count]
+    out_refs, token_ref, rows_refs = refs[3 * count : 4 * count], refs[4 * count], refs[4 * count + 1 : 5 * count + 1]
+    kept_refs, sem_ref = refs[5 * count + 1 : -1], refs[-1]
+    token_ref[...] = jnp.zeros_like(token_ref)
+    copies = []
+    for c in range(count):
+        spread_latents(pre_refs[c], *map_refs[2 * c : 2 * c + 2], kept_refs[c], rows_refs[c])
+        copies.append(pltpu.make_async_copy(rows_refs[c], out_refs[c], sem_ref.at[c]))
+        copies[-1].start()
+    for copy in copies:
+        copy.wait()
+
+
+def make_latents(pre, maps, latents):
+    rows = [p.shape[0] * PER for p in pre]
+    *out, token = pl.pallas_call(
+        latents_kernel,
+        out_shape=tuple(hbm((n, latents), BF16) for n in rows) + (TOKEN,),
+        in_specs=[whole()] * (3 * len(pre)),
+        out_specs=(anywhere(),) * len(pre) + (whole(),),
+        scratch_shapes=[pltpu.VMEM((n, latents), BF16) for n in rows]
+        + [pltpu.VMEM(p.shape, F32) for p in pre]
+        + [pltpu.SemaphoreType.DMA((len(pre),))],
+        compiler_params=params(),
+        cost_estimate=cost(4_000_000_000, 4 << 20),
+        name="make_latents",
+    )(*pre, *[m for pair in maps for m in pair])
+    return out, token
 
 
 def residual_kernel(*refs):
@@ -413,49 +509,72 @@
 def encoder_grad_kernel(scale, lg_ref, *refs):
     count = len(CHUNKS)
     pre_refs, map_refs, x_refs = refs[:count], refs[count : 3 * count], refs[3 * count : 4 * count]
-    out_ref, grad_ref, kept_ref = refs[4 * count :]
-
-    @pl.when(pl.program_id(0) == 0)
-    def _():
-        start = 0
+    out_ref, kept_ref, grad_ref, made_ref = refs[4 * count : 4 * count + 4]
+    held_refs, read_sem, sem_ref = refs[4 * count + 4 : -2], refs[-2], refs[-1]
+    reads = [
+        pltpu.make_async_copy(x_ref, held_ref, read_sem.at[c])
+        for c, (x_ref, held_ref) in enumerate(zip(x_refs, held_refs))
+    ]
+    for copy in reads:
+        copy.start()
+    starts, start = [], 0
+    for c, cap in enumerate(CHUNKS):
+        packed = GROUPS * cap // PER
+        pre = pre_refs[c][...]
+        sig = 1.0 / (1.0 + jnp.exp(-pre))
+        slope = lg_ref[start : start + packed, :] * (sig * (1.0 + pre * (1.0 - sig)))
+        kept_ref[start : start + packed, :] = slope.astype(BF16).astype(F32)
+        starts.append(start)
+        start += packed
+
+    def spread(j):
         for c, cap in enumerate(CHUNKS):
-            packed = GROUPS * cap // PER
-            pre = pre_refs[c][...]
-            sig = 1.0 / (1.0 + jnp.exp(-pre))
-            slope = lg_ref[start : start + packed, :] * (sig * (1.0 + pre * (1.0 - sig)))
-            kept_ref[...] = slope.astype(BF16).astype(F32)
+            tiles = range(j * BLOCK // LANES, (j + 1) * BLOCK // LANES)
             words = map_refs[2 * c : 2 * c + 2]
-            spread_kept(kept_ref, *words, grad_ref, GROUPS, cap // PER, 0, start * PER)
-            start += packed
-
-    total, start = None, 0
-    for c, cap in enumerate(CHUNKS):
-        rows = GROUPS * cap
-        part = jnp.dot(
-            x_refs[c][...], grad_ref[start : start + rows, :], preferred_element_type=F32
+            spread_kept(
+                kept_ref, *words, grad_ref.at[j], cap // PER, tiles, starts[c], starts[c] * PER
+            )
+
+    blocks = grad_ref.shape[0]
+    spread(0)
+    for copy in reads:
+        copy.wait()
+    writes = []
+    for j in range(blocks):
+        if j + 1 < blocks:
+            spread(j + 1)
+        total = None
+        for c, cap in enumerate(CHUNKS):
+            rows = slice(starts[c] * PER, starts[c] * PER + GROUPS * cap)
+            part = jnp.dot(held_refs[c][...], grad_ref[j, rows, :], preferred_element_type=F32)
+            total = part if total is None else total + part
+        made_ref[j] = (total * scale).astype(BF16)
+        copy = pltpu.make_async_copy(
+            made_ref.at[j], out_ref.at[:, pl.ds(j * BLOCK, BLOCK)], sem_ref.at[j]
         )
-        total = part if total is None else total + part
-        start += rows
-    out_ref[...] = (total * scale).astype(BF16)
+        copy.start()
+        writes.append(copy)
+    for copy in writes:
+        copy.wait()
 
 
 def encoder_grad(lg, pre, maps, turned, scale):
     latents = 1024
     inner = turned[0].shape[0]
-    block = 256
-    rows = GROUPS * CHUNKS[0]
+    blocks = latents // BLOCK
     operands = [lg, *pre, *[m for pair in maps for m in pair]]
     return pl.pallas_call(
         functools.partial(encoder_grad_kernel, scale),
-        grid=(inner // block,),
         out_shape=jax.ShapeDtypeStruct((inner, latents), BF16),
-        in_specs=[whole()] * len(operands)
-        + [pl.BlockSpec((block, t.shape[1]), lambda i: (i, 0)) for t in turned],
-        out_specs=pl.BlockSpec((block, latents), lambda i: (i, 0)),
+        in_specs=[whole()] * len(operands) + [anywhere()] * len(turned),
+        out_specs=anywhere(),
         scratch_shapes=[
-            pltpu.VMEM((GROUPS * CAP, latents), BF16),
-            pltpu.VMEM((rows // PER, LANES), F32),
-        ],
+            pltpu.VMEM(lg.shape, F32),
+            pltpu.VMEM((blocks, GROUPS * CAP, BLOCK), BF16),
+            pltpu.VMEM((blocks, inner, BLOCK), BF16),
+        ]
+        + [pltpu.VMEM(t.shape, BF16) for t in turned]
+        + [pltpu.SemaphoreType.DMA((len(turned),)), pltpu.SemaphoreType.DMA((blocks,))],
         compiler_params=params(),
         cost_estimate=cost(4 * 1024 * inner * latents, 6 << 20),
         name="encoder_grad",
@@ -463,7 +582,8 @@
 
 
 def decoder_grad_kernel(*refs):
-    latent_refs, res_ref, out_ref = refs[:-2], refs[-2], refs[-1]
+    latent_refs, res_ref, out_ref, token_ref = refs[:-3], refs[-3], refs[-2], refs[-1]
+    token_ref[...] = jnp.zeros_like(token_ref)
     block = out_ref.shape[0]
     here = pl.ds(pl.multiple_of(pl.program_id(0) * block, block), block)
     total = None
@@ -485,9 +605,9 @@
     return pl.pallas_call(
         decoder_grad_kernel,
         grid=(latents // block,),
-        out_shape=jax.ShapeDtypeStruct((latents, inner), BF16),
+        out_shape=(jax.ShapeDtypeStruct((latents, inner), BF16), TOKEN),
         in_specs=[whole()] * (len(latent) + 1),
-        out_specs=pl.BlockSpec((block, inner), lambda i: (i, 0)),
+        out_specs=(pl.BlockSpec((block, inner), lambda i: (i, 0)), token_spec()),
         compiler_params=params(),
         cost_estimate=cost(2 * 1024 * inner * latents, 6 << 20),
         name="decoder_grad",
@@ -501,10 +621,31 @@
     ).reshape(count, width)
 
 
-def width_sum(part):
+def add_kernel(*refs):
+    total = refs[0][...]
+    for ref in refs[1:-1]:
+        total = total + ref[...]
+    refs[-1][...] = total
+
+
+def add_after(parts, after):
+    return pl.pallas_call(
+        skipping(add_kernel, len(parts), 1),
+        out_shape=jax.ShapeDtypeStruct(parts[0].shape, F32),
+        in_specs=[whole()] * (len(parts) + 1),
+        out_specs=whole(),
+        compiler_params=params(),
+        name="add_parts",
+    )(*parts, after)
+
+
+def width_sum(part, between=None):
     for masks in ((1,), (4, 8, 12), (2,)):
         size = lax.axis_size("width")
         moved = [lax.ppermute(part, "width", [(a, a ^ m) for a in range(size)]) for m in masks]
+        if between is not None and len(masks) > 1:
+            part = add_after([part, *moved], between)
+            continue
         for other in moved:
             part = part + other
     return part
@@ -516,7 +657,7 @@
     latents = enc_weight.shape[3]
     scale = 1.0 / math.sqrt(L * D)
     x_home = in_vmem(acts.reshape(tokens, inner))
-    enc = in_vmem(enc_weight.reshape(inner, latents))
+    enc = enc_weight.reshape(inner, latents)
     dec = in_vmem(dec_weight.reshape(latents, inner))
     bias = jnp.where(lax.axis_index("width") == 0, enc_bias, 0.0)
 
@@ -526,19 +667,22 @@
     *later, token = slot_maps(index[1])
     maps.append(later)
 
-    pre, latent, back, after, tokens_in = [], [], [], (), (token,)
-    for c, cap in enumerate(CHUNKS):
-        part = encode(in_vmem(arrived[c]), enc, bias, index[c], after)
+    pre, back, after, tokens_in = [], [], (), (token,)
+    for c in range(len(CHUNKS)):
+        if c == 0:
+            part = encode(arrived[c], in_vmem(enc), bias, index[c], after)
+        else:
+            part = encode_streamed(arrived[c], enc, bias, index[c], after)
         pre.append(width_sum(part))
-        lat, decoded, token = decode(pre[c], *maps[c], dec, cap // PER, tokens_in)
+        decoded, token = decode(pre[c], *maps[c], dec, tokens_in)
         after, tokens_in = (token,), ()
-        latent.append(lat)
         back.append(exchange(decoded))
 
     *turned, token = turn(arrived, inner)
-    res = exchange(form_residual(info, x_home, dec_bias.reshape(1, inner), back, (token,)))
-    lg = width_sum(latent_gradient(res, dec, index))
-    grad_dec = decoder_grad(latent, res)
+    latent, later = make_latents(pre, maps, latents)
+    res = exchange(form_residual(info, x_home, dec_bias.reshape(1, inner), back, (token, later)))
+    grad_dec, token = decoder_grad(latent, res)
+    lg = width_sum(latent_gradient(res, dec, index), token)
     grad_enc = encoder_grad(lg, pre, maps, turned, scale)
     return (
         grad_enc.reshape(1, layers, width_dev, latents),

time: 228 us -> 225 us (0.987)
  waiting for transfers between devices: 48.4 us -> 43.5 us
    pallas_call x4 -> x7, Pallas kernels: 18.5 us -> 23.4 us  [the longest x2 7.52 us: decode(): pl.pallas_call(skipping(decode_kernel, 4, len(after)), out_shape=(hbm((to...]
    all_to_all x3, waiting for transfers between devices: 22.9 us -> 19.9 us  [exchange(): lax.all_to_all(rows.reshape(GROUPS, count // GROUPS, width), 'feat', spli...]
    pallas_call x2 -> x1, Pallas kernels: 4.35 us -> 1.49 us  [encode(): pl.pallas_call(skipping(encode_kernel, 4, len(after)), out_shape=jax.Shap...]
    unnamed x41 -> x57, local copies, waits for them, and re-layouts: 5.29 us -> 3.87 us
  transfers between devices with their start and end apart: 18 -> 18, of which waited for: 13 -> 15; matrix products, arithmetic and copies ran while one was open for 1% -> 2% of each run, Pallas kernels for 10% -> 12%
where the time goes in v4:
time: 225 us; the launch traced here: 224 us
  blocking collectives  93.9 us (42%)
  waiting for transfers between devices  43.5 us (19%)
  starting transfers between devices  39.5 us (18%)
  Pallas kernels  38.2 us (17%)
  local copies, waits for them, and re-layouts  7.56 us (3%)
    all_to_all x2, blocking collectives, exchange(): lax.all_to_all(rows.reshape(GROUPS, count // GROUPS, width), 'feat', spli...  93.9 us
    ppermute x15, waiting for transfers between devices, width_sum(): lax.ppermute(part, 'width', [(a, a ^ m) for a in range(size)])  23.6 us
    ppermute x15, starting transfers between devices, width_sum(): lax.ppermute(part, 'width', [(a, a ^ m) for a in range(size)])  20.9 us
    all_to_all x3, waiting for transfers between devices, exchange(): lax.all_to_all(rows.reshape(GROUPS, count // GROUPS, width), 'feat', spli...  19.9 us
    all_to_all x3, starting transfers between devices, exchange(): lax.all_to_all(rows.reshape(GROUPS, count // GROUPS, width), 'feat', spli...  18.6 us
    pallas_call x2, Pallas kernels, decode(): pl.pallas_call(skipping(decode_kernel, 4, len(after)), out_shape=(hbm((to...  7.52 us
    pallas_call x1, Pallas kernels, encoder_grad(): pl.pallas_call(functools.partial(encoder_grad_kernel, scale), out_shape=j...  5.55 us
  transfers between devices with their start and end apart: 18, of which 15 were waited for; matrix products, arithmetic and copies ran while one was open for 2% of the time, Pallas kernels for 12%

profile of v4, /device:TPU:32, one launch (start us, length us, event | category | flops | bytes accessed | tf_op | source)
XLA Modules:
  0.0 224.1 jit_solution(12987419871953001496)
XLA Ops:
  0.6 0.9 copy.10.index_ref
  1.6 1.1 copy.11
  2.7 0.7 copy-done.7
  3.4 1.8 pack_tokens.1
  5.2 39.8 %all_to_all.25 = bf16[16,32,1152]{2,1,0:T(8,128)(2,1)S(1)} all-to-all(bf16[16,32,1152]{2,1,0:T(8,128)(2,1)S(1)} %bitcast.35), channel_id=1, replica_groups=mesh['width'=16,'feat'=16] {'feat'}, dimensions={0} | all-to-all | bytes 2359296 | tf_op jit(solution)/shard_map/all_to_all | solution.py:619
  45.1 4.8 %all-to-all-start.2 = ((bf16[16,32,1024]{2,1,0:T(8,128)(2,1)}), bf16[16,32,1024]{2,1,0:T(8,128)(2,1)}, u32[]{:S(2)}, u32[]{:S(2)}) async-start(bf16[16,32,1024]{2,1,0:T(8,128)(2,1)} %bitcast.7), calls=%async_computation.2 | async-start | bytes 2097152 | tf_op jit(solution)/shard_map/all_to_all | solution.py:619
  49.9 2.1 slot_numbers.1
  52.0 1.5 encode.1
  53.6 1.2 collective-permute-done
  54.9 3.1 %collective-permute-start.3 = (f32[128,128]{1,0:T(8,128)S(1)}, f32[128,128]{1,0:T(8,128)S(1)}, u32[]{:S(2)}, u32[]{:S(2)}) collective-permute-start(f32[128,128]{1,0:T(8,128)S(1)} %add.36), channel_id=1, source_target_pairs={{0,192},{16,208},{32,224},{48,240},{64,128},{80,144},{96,160},{112... | collective-permute-start | bytes 196616 | tf_op jit(solution)/shard_map/ppermute | solution.py:645
  58.0 0.6 collective-permute-start.2
  59.1 0.6 copy.13
  59.7 1.4 collective-permute-done.3
  61.1 3.0 %collective-permute-done.2 = f32[128,128]{1,0:T(8,128)S(1)} collective-permute-done((f32[128,128]{1,0:T(8,128)S(1)}, f32[128,128]{1,0:T(8,128)S(1)}, u32[]{:S(2)}, u32[]{:S(2)}) %collective-permute-start.2) | collective-permute-done | bytes 65568 | tf_op jit(solution)/shard_map/ppermute | solution.py:645
  64.1 3.0 %collective-permute-start.4 = (f32[128,128]{1,0:T(8,128)S(1)}, f32[128,128]{1,0:T(8,128)S(1)}, u32[]{:S(2)}, u32[]{:S(2)}) collective-permute-start(f32[128,128]{1,0:T(8,128)S(1)} %add_add_fusion.1), channel_id=1, source_target_pairs={{0,32},{16,48},{32,0},{48,16},{64,96},{80,112},{96,64},{112,80},{1... | collective-permute-start | bytes 196616 | tf_op jit(solution)/shard_map/ppermute | solution.py:645
  67.1 2.0 slot_maps.1
  69.1 0.7 copy-done.16
  69.8 0.7 copy-done.20
  70.5 1.2 collective-permute-done.4
  71.7 3.4 %decode.2 = (bf16[512,1024]{1,0:T(8,128)(2,1)}, f32[8,128]{1,0:T(8,128)S(1)}) custom-call(f32[128,128]{1,0:T(8,128)S(1)} %add.40.refs_0_, s32[512,128]{1,0:T(8,128)S(1)} %get-tuple-element.26.refs_1_.refs_2_, s32[512,128]{1,0:T(8,128)S(1)} %get-tuple-element.27.refs_2_.refs_3_, bf16[1024,1024]{1,0:T(8,128)(2,1)S(1)} %bitcast.25, ...), custom_call_target="tpu_custom_call" | custom-call | flops 2147483648 | bytes 6291456 | tf_op jit(solution)/shard_map/decode/pallas_call | solution.py:407
  75.2 8.2 %all-to-all-start.1 = ((bf16[16,32,1024]{2,1,0:T(8,128)(2,1)}), bf16[16,32,1024]{2,1,0:T(8,128)(2,1)S(1)}, u32[]{:S(2)}, u32[]{:S(2)}) async-start(bf16[16,32,1024]{2,1,0:T(8,128)(2,1)} %bitcast.41), calls=%async_computation.1 | async-start | bytes 2097152 | tf_op jit(solution)/shard_map/all_to_all | solution.py:619
  83.4 3.1 %encode_streamed.1 = f32[128,128]{1,0:T(8,128)S(1)} custom-call(bf16[512,1024]{1,0:T(8,128)(2,1)} %bitcast.8.refs_0_.refs_1_, bf16[1024,1024]{1,0:T(8,128)(2,1)} %bitcast.37, f32[1,1024]{1,0:T(1,128)S(1)} %broadcast_select_fusion.refs_2_, s32[16,8,128]{2,1,0:T(8,128)S(1)} %get-tuple-element.28.index_ref.refs_3_.refs_1_, f32[8,128]{1,0:T(8,128)S(1)} %get-tuple-element.32.refs_4_), custom_call_target="tpu_custom_call" | custom-call | flops 2147483648 | bytes 4194304 | tf_op jit(solution)/shard_map/encode_streamed/pallas_call | solution.py:314
  86.6 1.2 collective-permute-done.5
  87.8 0.6 collective-permute-start.8
  88.5 0.9 collective-permute-start.7
  89.4 2.6 %collective-permute-start.6 = (f32[128,128]{1,0:T(8,128)S(1)}, f32[128,128]{1,0:T(8,128)S(1)}, u32[]{:S(2)}, u32[]{:S(2)}) collective-permute-start(f32[128,128]{1,0:T(8,128)S(1)} %add.41), channel_id=1, source_target_pairs={{0,64},{16,80},{32,96},{48,112},{64,0},{80,16},{96,32},{112,48},{1... | collective-permute-start | bytes 196616 | tf_op jit(solution)/shard_map/ppermute | solution.py:645
  92.0 2.4 %collective-permute-done.8 = f32[128,128]{1,0:T(8,128)S(1)} collective-permute-done((f32[128,128]{1,0:T(8,128)S(1)}, f32[128,128]{1,0:T(8,128)S(1)}, u32[]{:S(2)}, u32[]{:S(2)}) %collective-permute-start.8) | collective-permute-done | bytes 65568 | tf_op jit(solution)/shard_map/ppermute | solution.py:645
  95.3 2.4 %collective-permute-start.9 = (f32[128,128]{1,0:T(8,128)S(1)}, f32[128,128]{1,0:T(8,128)S(1)}, u32[]{:S(2)}, u32[]{:S(2)}) collective-permute-start(f32[128,128]{1,0:T(8,128)S(1)} %add_add_fusion), channel_id=1, source_target_pairs={{0,32},{16,48},{32,0},{48,16},{64,96},{80,112},{96,64},{112,80},{1... | collective-permute-start | bytes 196616 | tf_op jit(solution)/shard_map/ppermute | solution.py:645
  97.7 5.1 %collective-permute-done.9 = f32[128,128]{1,0:T(8,128)S(1)} collective-permute-done((f32[128,128]{1,0:T(8,128)S(1)}, f32[128,128]{1,0:T(8,128)S(1)}, u32[]{:S(2)}, u32[]{:S(2)}) %collective-permute-start.9) | collective-permute-done | bytes 65568 | tf_op jit(solution)/shard_map/ppermute | solution.py:645
  102.9 4.1 %decode.3 = (bf16[512,1024]{1,0:T(8,128)(2,1)}, f32[8,128]{1,0:T(8,128)}) custom-call(f32[128,128]{1,0:T(8,128)S(1)} %add.45.refs_0_.refs_1_, s32[512,128]{1,0:T(8,128)S(1)} %copy-done.17, s32[512,128]{1,0:T(8,128)S(1)} %copy-done.21, bf16[1024,1024]{1,0:T(8,128)(2,1)S(1)} %bitcast.26), custom_call_target="tpu_custom_call" | custom-call | flops 2147483648 | bytes 6291456 | tf_op jit(solution)/shard_map/decode/pallas_call | solution.py:407
  107.0 1.8 all-to-all-done.1
  108.7 5.6 %all-to-all-start.3 = ((bf16[16,32,1024]{2,1,0:T(8,128)(2,1)}), bf16[16,32,1024]{2,1,0:T(8,128)(2,1)S(1)}, u32[]{:S(2)}, u32[]{:S(2)}) async-start(bf16[16,32,1024]{2,1,0:T(8,128)(2,1)} %bitcast.42), calls=%async_computation.3 | async-start | bytes 2097152 | tf_op jit(solution)/shard_map/all_to_all | solution.py:619
  114.4 3.4 %turn_rows.1 = (bf16[1024,512]{1,0:T(8,128)(2,1)}, bf16[1024,512]{1,0:T(8,128)(2,1)}, f32[8,128]{1,0:T(8,128)S(1)}) custom-call(bf16[512,1152]{1,0:T(8,128)(2,1)S(1)} %bitcast.34, bf16[512,1024]{1,0:T(8,128)(2,1)} %bitcast.8.refs_0_.refs_1_), custom_call_target="tpu_custom_call" | custom-call | flops 4000000000 | bytes 4194304 | tf_op jit(solution)/shard_map/turn_rows/pallas_call | solution.py:496
  117.8 4.2 %make_latents.1 = (bf16[512,1024]{1,0:T(8,128)(2,1)}, bf16[512,1024]{1,0:T(8,128)(2,1)}, f32[8,128]{1,0:T(8,128)S(1)}) custom-call(f32[128,128]{1,0:T(8,128)S(1)} %add.40.refs_0_, f32[128,128]{1,0:T(8,128)S(1)} %add.45.refs_0_.refs_1_, s32[512,128]{1,0:T(8,128)S(1)} %copy-done.11, s32[512,128]{1,0:T(8,128)S(1)} %copy-done.14, s32[512,128]{1,0:T(8,128)S(1)} %copy-done.18, ...), custom_call_target="tpu_custom_call" | custom-call | flops 4000000000 | bytes 4194304 | tf_op jit(solution)/shard_map/make_latents/pallas_call | solution.py:441
  122.0 18.2 %all-to-all-done.3 = bf16[16,32,1024]{2,1,0:T(8,128)(2,1)S(1)} async-done(((bf16[16,32,1024]{2,1,0:T(8,128)(2,1)}), bf16[16,32,1024]{2,1,0:T(8,128)(2,1)S(1)}, u32[]{:S(2)}, u32[]{:S(2)}) %all-to-all-start.3) | async-done | bytes 1048608 | tf_op jit(solution)/shard_map/all_to_all | solution.py:619
  140.1 1.4 form_residual.1
  141.5 54.0 %all_to_all.26 = bf16[16,64,1024]{2,1,0:T(8,128)(2,1)S(1)} all-to-all(bf16[16,64,1024]{2,1,0:T(8,128)(2,1)S(1)} %bitcast.22), channel_id=1, replica_groups=mesh['width'=16,'feat'=16] {'feat'}, dimensions={0} | all-to-all | bytes 4194304 | tf_op jit(solution)/shard_map/all_to_all | solution.py:619
  195.5 2.8 %latent_gradient.1 = f32[256,128]{1,0:T(8,128)S(1)} custom-call(bf16[1024,1024]{1,0:T(8,128)(2,1)S(1)} %bitcast.28, bf16[1024,1024]{1,0:T(8,128)(2,1)S(1)} %bitcast.27, s32[16,8,128]{2,1,0:T(8,128)S(1)} %get-tuple-element.25.refs_3_.refs_0_, s32[16,8,128]{2,1,0:T(8,128)S(1)} %get-tuple-element.28.index_ref.refs_3_.refs_1_), custom_call_target="tpu_custom_call" | custom-call | flops 4294967296 | bytes 4194304 | tf_op jit(solution)/shard_map/latent_gradient/pallas_call | solution.py:344
  198.4 1.3 collective-permute-done.10
  199.8 3.7 %collective-permute-start.13 = (f32[256,128]{1,0:T(8,128)S(1)}, f32[256,128]{1,0:T(8,128)S(1)}, u32[]{:S(2)}, u32[]{:S(2)}) collective-permute-start(f32[256,128]{1,0:T(8,128)S(1)} %add.46.refs_0_), channel_id=1, source_target_pairs={{0,192},{16,208},{32,224},{48,240},{64,128},{80,144},{96,160},{112... | collective-permute-start | bytes 393224 | tf_op jit(solution)/shard_map/ppermute | solution.py:645
  203.5 1.1 collective-permute-start.12
  204.6 3.0 %decoder_grad.1 = (bf16[1024,1024]{1,0:T(8,128)(2,1)S(1)}, f32[8,128]{1,0:T(8,128)S(1)}) custom-call(bf16[512,1024]{1,0:T(8,128)(2,1)S(1)} %copy-done.8, bf16[512,1024]{1,0:T(8,128)(2,1)S(1)} %copy-done.9, bf16[1024,1024]{1,0:T(8,128)(2,1)S(1)} %bitcast.29), custom_call_target="tpu_custom_call" | custom-call | flops 2147483648 | bytes 6291456 | tf_op jit(solution)/shard_map/decoder_grad/pallas_call | solution.py:605
  207.7 1.7 collective-permute-done.13.refs_3_
  209.4 2.0 collective-permute-done.12.refs_2_
  211.4 2.0 collective-permute-start.14
  213.4 2.8 %reshape.71 = bf16[1,1024,2,512]{3,2,1,0:T(2,128)(2,1)} reshape(bf16[1024,1024]{1,0:T(8,128)(2,1)S(1)} %get-tuple-element.43) | data formatting | bytes 4194304 | tf_op jit(solution)/shard_map/reshape | solution.py:689
  216.2 2.1 collective-permute-done.14
  218.3 5.6 %encoder_grad.1 = bf16[1024,1024]{1,0:T(8,128)(2,1)} custom-call(f32[256,128]{1,0:T(8,128)S(1)} %add.47.lg_ref, f32[128,128]{1,0:T(8,128)S(1)} %add.40.refs_0_, f32[128,128]{1,0:T(8,128)S(1)} %add.45.refs_0_.refs_1_, s32[512,128]{1,0:T(8,128)S(1)} %copy-done.12, s32[512,128]{1,0:T(8,128)S(1)} %copy-done.15, s32[512,128]{1,0:T(8,128)S(1)} %copy-done.19, ...), custom_call_target="tpu_custom_call" | custom-call | flops 4294967296 | bytes 6291456 | tf_op jit(solution)/shard_map/encoder_grad/pallas_call | solution.py:566
  (72 shorter events, 1.8 us)
Async XLA Ops:
  2.7 42.4 %copy-start.2 = (bf16[32,8,2,512]{3,1,2,0:T(8,128)(2,1)}, bf16[32,8,2,512]{3,1,2,0:T(8,128)(2,1)S(1)}, u32[]{:S(2)}) copy-start(bf16[32,8,2,512]{3,1,2,0:T(8,128)(2,1)S(1)} %copy.11) | copy-start | bytes 1572868
  2.7 0.7 copy-start.7
  5.2 44.7 %copy-start.25 = (f32[1,1024]{1,0:T(1,128)S(1)}, f32[1,1024]{1,0:T(1,128)}, u32[]{:S(2)}) copy-start(f32[1,1024]{1,0:T(1,128)} %param.9) | copy-start | bytes 12292
  45.1 6.9 %copy-start.4 = (bf16[16,32,1152]{2,1,0:T(8,128)(2,1)}, bf16[16,32,1152]{2,1,0:T(8,128)(2,1)S(1)}, u32[]{:S(2)}) copy-start(bf16[16,32,1152]{2,1,0:T(8,128)(2,1)S(1)} %all_to_all.25) | copy-start | bytes 3538948
  45.1 30.1 %all-to-all-start.2 = ((bf16[16,32,1024]{2,1,0:T(8,128)(2,1)}), bf16[16,32,1024]{2,1,0:T(8,128)(2,1)}, u32[]{:S(2)}, u32[]{:S(2)}) async-start(bf16[16,32,1024]{2,1,0:T(8,128)(2,1)} %bitcast.7), calls=%async_computation.2 | async-start | bytes 2097152 | tf_op jit(solution)/shard_map/all_to_all | solution.py:619
  49.9 2.1 copy-start.6
  52.0 19.7 %copy-start.10 = (s32[512,128]{1,0:T(8,128)}, s32[512,128]{1,0:T(8,128)S(1)}, u32[]{:S(2)}) copy-start(s32[512,128]{1,0:T(8,128)S(1)} %get-tuple-element.26.refs_1_.refs_2_) | copy-start | bytes 786436
  52.0 19.7 %copy-start.13 = (s32[512,128]{1,0:T(8,128)}, s32[512,128]{1,0:T(8,128)S(1)}, u32[]{:S(2)}) copy-start(s32[512,128]{1,0:T(8,128)S(1)} %get-tuple-element.27.refs_2_.refs_3_) | copy-start | bytes 786436
  52.0 7.0 %copy-start.24 = (bf16[1,1024,2,512]{3,2,1,0:T(2,128)(2,1)S(1)}, bf16[1,1024,2,512]{3,2,1,0:T(2,128)(2,1)}, u32[]{:S(2)}) copy-start(bf16[1,1024,2,512]{3,2,1,0:T(2,128)(2,1)} %param.10) | copy-start | bytes 6291460
  53.5 1.3 collective-permute-start
  54.9 6.2 %collective-permute-start.3 = (f32[128,128]{1,0:T(8,128)S(1)}, f32[128,128]{1,0:T(8,128)S(1)}, u32[]{:S(2)}, u32[]{:S(2)}) collective-permute-start(f32[128,128]{1,0:T(8,128)S(1)} %add.36), channel_id=1, source_target_pairs={{0,192},{16,208},{32,224},{48,240},{64,128},{80,144},{96,160},{112... | collective-permute-start | bytes 196616 | tf_op jit(solution)/shard_map/ppermute | solution.py:645
  58.0 6.1 %collective-permute-start.2 = (f32[128,128]{1,0:T(8,128)S(1)}, f32[128,128]{1,0:T(8,128)S(1)}, u32[]{:S(2)}, u32[]{:S(2)}) collective-permute-start(f32[128,128]{1,0:T(8,128)S(1)} %add.36), channel_id=1, source_target_pairs={{0,128},{16,144},{32,160},{48,176},{64,192},{80,208},{96,224},{112... | collective-permute-start | bytes 196616 | tf_op jit(solution)/shard_map/ppermute | solution.py:645
  58.6 5.5 %collective-permute-start.1 = (f32[128,128]{1,0:T(8,128)S(1)}, f32[128,128]{1,0:T(8,128)S(1)}, u32[]{:S(2)}, u32[]{:S(2)}) collective-permute-start(f32[128,128]{1,0:T(8,128)S(1)} %add.36), channel_id=1, source_target_pairs={{0,64},{16,80},{32,96},{48,112},{64,0},{80,16},{96,32},{112,48},{1... | collective-permute-start | bytes 196616 | tf_op jit(solution)/shard_map/ppermute | solution.py:645
  59.7 43.2 %copy-start = (bf16[128,8,2,512]{3,1,2,0:T(8,128)(2,1)}, bf16[128,8,2,512]{3,1,2,0:T(8,128)(2,1)S(1)}, u32[]{:S(2)}) copy-start(bf16[128,8,2,512]{3,1,2,0:T(8,128)(2,1)S(1)} %copy.13) | copy-start | bytes 6291460
  64.1 7.6 %collective-permute-start.4 = (f32[128,128]{1,0:T(8,128)S(1)}, f32[128,128]{1,0:T(8,128)S(1)}, u32[]{:S(2)}, u32[]{:S(2)}) collective-permute-start(f32[128,128]{1,0:T(8,128)S(1)} %add_add_fusion.1), channel_id=1, source_target_pairs={{0,32},{16,48},{32,0},{48,16},{64,96},{80,112},{96,64},{112,80},{1... | collective-permute-start | bytes 196616 | tf_op jit(solution)/shard_map/ppermute | solution.py:645
  69.1 0.7 copy-start.16
  69.8 0.7 copy-start.20
  75.2 33.5 %all-to-all-start.1 = ((bf16[16,32,1024]{2,1,0:T(8,128)(2,1)}), bf16[16,32,1024]{2,1,0:T(8,128)(2,1)S(1)}, u32[]{:S(2)}, u32[]{:S(2)}) async-start(bf16[16,32,1024]{2,1,0:T(8,128)(2,1)} %bitcast.41), calls=%async_computation.1 | async-start | bytes 2097152 | tf_op jit(solution)/shard_map/all_to_all | solution.py:619
  83.4 19.5 %copy-start.17 = (s32[512,128]{1,0:T(8,128)S(1)}, s32[512,128]{1,0:T(8,128)}, u32[]{:S(2)}) copy-start(s32[512,128]{1,0:T(8,128)} %copy-done.16) | copy-start | bytes 786436
  83.4 19.5 %copy-start.21 = (s32[512,128]{1,0:T(8,128)S(1)}, s32[512,128]{1,0:T(8,128)}, u32[]{:S(2)}) copy-start(s32[512,128]{1,0:T(8,128)} %copy-done.20) | copy-start | bytes 786436
  86.5 1.3 collective-permute-start.5
  87.8 6.6 %collective-permute-start.8 = (f32[128,128]{1,0:T(8,128)S(1)}, f32[128,128]{1,0:T(8,128)S(1)}, u32[]{:S(2)}, u32[]{:S(2)}) collective-permute-start(f32[128,128]{1,0:T(8,128)S(1)} %add.41), channel_id=1, source_target_pairs={{0,192},{16,208},{32,224},{48,240},{64,128},{80,144},{96,160},{112... | collective-permute-start | bytes 196616 | tf_op jit(solution)/shard_map/ppermute | solution.py:645
  88.5 6.5 %collective-permute-start.7 = (f32[128,128]{1,0:T(8,128)S(1)}, f32[128,128]{1,0:T(8,128)S(1)}, u32[]{:S(2)}, u32[]{:S(2)}) collective-permute-start(f32[128,128]{1,0:T(8,128)S(1)} %add.41), channel_id=1, source_target_pairs={{0,128},{16,144},{32,160},{48,176},{64,192},{80,208},{96,224},{112... | collective-permute-start | bytes 196616 | tf_op jit(solution)/shard_map/ppermute | solution.py:645
  89.4 5.9 %collective-permute-start.6 = (f32[128,128]{1,0:T(8,128)S(1)}, f32[128,128]{1,0:T(8,128)S(1)}, u32[]{:S(2)}, u32[]{:S(2)}) collective-permute-start(f32[128,128]{1,0:T(8,128)S(1)} %add.41), channel_id=1, source_target_pairs={{0,64},{16,80},{32,96},{48,112},{64,0},{80,16},{96,32},{112,48},{1... | collective-permute-start | bytes 196616 | tf_op jit(solution)/shard_map/ppermute | solution.py:645
  95.3 7.5 %collective-permute-start.9 = (f32[128,128]{1,0:T(8,128)S(1)}, f32[128,128]{1,0:T(8,128)S(1)}, u32[]{:S(2)}, u32[]{:S(2)}) collective-permute-start(f32[128,128]{1,0:T(8,128)S(1)} %add_add_fusion), channel_id=1, source_target_pairs={{0,32},{16,48},{32,0},{48,16},{64,96},{80,112},{96,64},{112,80},{1... | collective-permute-start | bytes 196616 | tf_op jit(solution)/shard_map/ppermute | solution.py:645
  106.9 7.4 %copy-start.26 = (f32[2,512]{1,0:T(2,128)S(1)}, f32[2,512]{1,0:T(2,128)}, u32[]{:S(2)}) copy-start(f32[2,512]{1,0:T(2,128)} %param.11) | copy-start | bytes 12292
  107.0 7.4 %copy-start.5 = (bf16[16,32,1152]{2,1,0:T(8,128)(2,1)S(1)}, bf16[16,32,1152]{2,1,0:T(8,128)(2,1)}, u32[]{:S(2)}) copy-start(bf16[16,32,1152]{2,1,0:T(8,128)(2,1)} %copy-done.4) | copy-start | bytes 3538948
  108.7 31.4 %all-to-all-start.3 = ((bf16[16,32,1024]{2,1,0:T(8,128)(2,1)}), bf16[16,32,1024]{2,1,0:T(8,128)(2,1)S(1)}, u32[]{:S(2)}, u32[]{:S(2)}) async-start(bf16[16,32,1024]{2,1,0:T(8,128)(2,1)} %bitcast.42), calls=%async_computation.3 | async-start | bytes 2097152 | tf_op jit(solution)/shard_map/all_to_all | solution.py:619
  114.3 3.4 %copy-start.11 = (s32[512,128]{1,0:T(8,128)S(1)}, s32[512,128]{1,0:T(8,128)}, u32[]{:S(2)}) copy-start(s32[512,128]{1,0:T(8,128)} %copy-done.10) | copy-start | bytes 786436
  114.3 3.4 %copy-start.14 = (s32[512,128]{1,0:T(8,128)S(1)}, s32[512,128]{1,0:T(8,128)}, u32[]{:S(2)}) copy-start(s32[512,128]{1,0:T(8,128)} %copy-done.13) | copy-start | bytes 786436
  114.4 3.4 %copy-start.18 = (s32[512,128]{1,0:T(8,128)S(1)}, s32[512,128]{1,0:T(8,128)}, u32[]{:S(2)}) copy-start(s32[512,128]{1,0:T(8,128)} %copy-done.16) | copy-start | bytes 786436
  114.4 3.4 %copy-start.22 = (s32[512,128]{1,0:T(8,128)S(1)}, s32[512,128]{1,0:T(8,128)}, u32[]{:S(2)}) copy-start(s32[512,128]{1,0:T(8,128)} %copy-done.20) | copy-start | bytes 786436
  117.8 22.3 %copy-start.3 = (bf16[32,8,2,512]{3,1,2,0:T(8,128)(2,1)S(1)}, bf16[32,8,2,512]{3,1,2,0:T(8,128)(2,1)}, u32[]{:S(2)}) copy-start(bf16[32,8,2,512]{3,1,2,0:T(8,128)(2,1)} %copy-done.2) | copy-start | bytes 1572868
  141.5 54.1 %copy-start.1 = (bf16[128,8,2,512]{3,1,2,0:T(8,128)(2,1)S(1)}, bf16[128,8,2,512]{3,1,2,0:T(8,128)(2,1)}, u32[]{:S(2)}) copy-start(bf16[128,8,2,512]{3,1,2,0:T(8,128)(2,1)} %copy-done) | copy-start | bytes 6291460
  195.5 9.1 %copy-start.8 = (bf16[512,1024]{1,0:T(8,128)(2,1)S(1)}, bf16[512,1024]{1,0:T(8,128)(2,1)}, u32[]{:S(2)}) copy-start(bf16[512,1024]{1,0:T(8,128)(2,1)} %get-tuple-element.38.refs_0_) | copy-start | bytes 3145732
  195.5 9.1 %copy-start.9 = (bf16[512,1024]{1,0:T(8,128)(2,1)S(1)}, bf16[512,1024]{1,0:T(8,128)(2,1)}, u32[]{:S(2)}) copy-start(bf16[512,1024]{1,0:T(8,128)(2,1)} %get-tuple-element.39.refs_1_) | copy-start | bytes 3145732
  198.3 1.4 collective-permute-start.10
  199.8 9.6 %collective-permute-start.13 = (f32[256,128]{1,0:T(8,128)S(1)}, f32[256,128]{1,0:T(8,128)S(1)}, u32[]{:S(2)}, u32[]{:S(2)}) collective-permute-start(f32[256,128]{1,0:T(8,128)S(1)} %add.46.refs_0_), channel_id=1, source_target_pairs={{0,192},{16,208},{32,224},{48,240},{64,128},{80,144},{96,160},{112... | collective-permute-start | bytes 393224 | tf_op jit(solution)/shard_map/ppermute | solution.py:645
  203.5 7.9 %collective-permute-start.12 = (f32[256,128]{1,0:T(8,128)S(1)}, f32[256,128]{1,0:T(8,128)S(1)}, u32[]{:S(2)}, u32[]{:S(2)}) collective-permute-start(f32[256,128]{1,0:T(8,128)S(1)} %add.46.refs_0_), channel_id=1, source_target_pairs={{0,128},{16,144},{32,160},{48,176},{64,192},{80,208},{96,224},{112... | collective-permute-start | bytes 393224 | tf_op jit(solution)/shard_map/ppermute | solution.py:645
  204.6 6.8 %collective-permute-start.11 = (f32[256,128]{1,0:T(8,128)S(1)}, f32[256,128]{1,0:T(8,128)S(1)}, u32[]{:S(2)}, u32[]{:S(2)}) collective-permute-start(f32[256,128]{1,0:T(8,128)S(1)} %add.46.refs_0_), channel_id=1, source_target_pairs={{0,64},{16,80},{32,96},{48,112},{64,0},{80,16},{96,32},{112,48},{1... | collective-permute-start | bytes 393224 | tf_op jit(solution)/shard_map/ppermute | solution.py:645
  211.4 6.8 %collective-permute-start.14 = (f32[256,128]{1,0:T(8,128)S(1)}, f32[256,128]{1,0:T(8,128)S(1)}, u32[]{:S(2)}, u32[]{:S(2)}) collective-permute-start(f32[256,128]{1,0:T(8,128)S(1)} %add_parts.1), channel_id=1, source_target_pairs={{0,32},{16,48},{32,0},{48,16},{64,96},{80,112},{96,64},{112,80},{1... | collective-permute-start | bytes 393224 | tf_op jit(solution)/shard_map/ppermute | solution.py:645
  213.4 4.9 %copy-start.12 = (s32[512,128]{1,0:T(8,128)S(1)}, s32[512,128]{1,0:T(8,128)}, u32[]{:S(2)}) copy-start(s32[512,128]{1,0:T(8,128)} %copy-done.10) | copy-start | bytes 786436
  213.4 4.9 %copy-start.15 = (s32[512,128]{1,0:T(8,128)S(1)}, s32[512,128]{1,0:T(8,128)}, u32[]{:S(2)}) copy-start(s32[512,128]{1,0:T(8,128)} %copy-done.13) | copy-start | bytes 786436
  213.4 4.9 %copy-start.19 = (s32[512,128]{1,0:T(8,128)S(1)}, s32[512,128]{1,0:T(8,128)}, u32[]{:S(2)}) copy-start(s32[512,128]{1,0:T(8,128)} %copy-done.16) | copy-start | bytes 786436
  213.4 4.9 %copy-start.23 = (s32[512,128]{1,0:T(8,128)S(1)}, s32[512,128]{1,0:T(8,128)}, u32[]{:S(2)}) copy-start(s32[512,128]{1,0:T(8,128)} %copy-done.20) | copy-start | bytes 786436

commit v5 on v4

--- a/solution.py
+++ b/solution.py
@@ -55,27 +55,30 @@
     return pl.BlockSpec(memory_space=pltpu.VMEM)
 
 
-def offsets():
-    out, start = [], 0
-    for cap in CHUNKS:
-        out.append((start, cap))
-        start += cap
-    return out
-
-
-def chunk_hits(info, off, cap, tokens):
-    rows = iota((GROUPS * cap, tokens), 0)
-
-    def slot(route, pos):
-        inside = (pos >= off) & (pos < off + cap)
-        return jnp.where(inside, route * cap + (pos - off), -1)
-
-    return (rows == slot(info[0:1], info[1:2])) | (rows == slot(info[2:3], info[3:4]))
+PLACES = CHUNKS[0] // PER
+PACKED = GROUPS * PLACES
+
+
+def quarter_keys(tokens):
+    row = iota((PACKED, tokens), 0)
+    return (row // PLACES) * CAP + row % PLACES
+
+
+def token_keys(info):
+    return [info[2 * j : 2 * j + 1] * CAP + info[2 * j + 1 : 2 * j + 2] for j in range(2)]
+
+
+def as_ones(hit):
+    return hit.astype(F32).astype(BF16)
+
+
+def quarters(x, width=1024):
+    return jnp.concatenate([x[:, i * width : (i + 1) * width] for i in range(x.shape[1] // width)], axis=0)
 
 
 def pack_kernel(routes_ref, acts_ref, index_ref, info_ref, *send_refs):
     tokens, inner = acts_ref.shape
-    upper = (iota((tokens, tokens), 0) < iota((tokens, tokens), 1)).astype(F32).astype(BF16)
+    upper = as_ones(iota((tokens, tokens), 0) < iota((tokens, tokens), 1))
     experts = iota((GROUPS, tokens), 0)
     total = jnp.zeros((GROUPS, 1), F32)
     rows = []
@@ -90,47 +93,38 @@
     info = jnp.concatenate(rows + [jnp.zeros((4, tokens), I32)], axis=0)
     info_ref[...] = info
     x = acts_ref[...]
-    for (off, cap), send_ref in zip(offsets(), send_refs):
-        hits = chunk_hits(info, off, cap, tokens).astype(F32).astype(BF16)
-        send_ref[:, :inner] = jnp.dot(hits, x, preferred_element_type=F32).astype(BF16)
-    send_refs[0][:, inner:] = index_codes(info, index_ref[...])
-
-
-def index_codes(info, index):
-    tokens, cols = index.shape
+    index = index_ref[...]
     code = (((index & 127) + 128) << (index >> 7)).astype(F32).astype(BF16)
+    cols = index.shape[1]
     col = iota((cols, LANES), 0)
     lane = iota((cols, LANES), 1)
-    first = CHUNKS[0]
-    rows_total = GROUPS * first
-    row = iota((rows_total, tokens), 0)
-    expert, inner = row // first, row % first
-    base = jnp.full((rows_total, tokens), -(1 << 20), I32)
-    step = jnp.zeros((rows_total, tokens), I32)
-    for off, cap in offsets():
-        here = (inner >= off // PER) & (inner < (off + cap) // PER)
-        base = jnp.where(here, expert * CAP + off + inner - off // PER, base)
-        step = jnp.where(here, cap // PER, step)
-    lane_q = iota((rows_total, LANES), 1) // KEPT
-    result = jnp.zeros((rows_total, LANES), F32)
-    for j in range(2):
-        spread = (col == j * KEPT + lane % KEPT).astype(F32).astype(BF16)
-        codes = jnp.dot(code, spread, preferred_element_type=F32).astype(BF16)
-        key = info[2 * j : 2 * j + 1] * CAP + info[2 * j + 1 : 2 * j + 2]
+    codes = [
+        jnp.dot(code, as_ones(col == j * KEPT + lane % KEPT), preferred_element_type=F32).astype(BF16)
+        for j in range(2)
+    ]
+    first = quarter_keys(tokens)
+    keys = token_keys(info)
+    lane_q = iota((PACKED, LANES), 1) // KEPT
+    for c, send_ref in enumerate(send_refs):
+        kept = jnp.zeros((PACKED, LANES), F32)
         for q in range(PER):
-            hit = (base + step * q == key).astype(F32).astype(BF16)
-            picked = jnp.dot(hit, codes, preferred_element_type=F32)
-            result = result + jnp.where(lane_q == q, picked, 0.0)
-    return result.astype(BF16)
+            slot = first + (c * PER + q) * PLACES
+            hits = [slot == key for key in keys]
+            send_ref[:, q * inner : (q + 1) * inner] = jnp.dot(
+                as_ones(hits[0] | hits[1]), x, preferred_element_type=F32
+            ).astype(BF16)
+            for hit, route_codes in zip(hits, codes):
+                picked = jnp.dot(as_ones(hit), route_codes, preferred_element_type=F32)
+                kept = kept + jnp.where(lane_q == q, picked, 0.0)
+        send_ref[:, PER * inner :] = kept.astype(BF16)
 
 
 def pack(routes_t, x, index):
     tokens, width = x.shape
-    widths = [width + LANES] + [width] * (len(CHUNKS) - 1)
+    send = jax.ShapeDtypeStruct((PACKED, PER * width + LANES), BF16)
     return pl.pallas_call(
         pack_kernel,
-        out_shape=(jax.ShapeDtypeStruct((8, tokens), I32),)
-        + tuple(jax.ShapeDtypeStruct((GROUPS * c, w), BF16) for c, w in zip(CHUNKS, widths)),
+        out_shape=(jax.ShapeDtypeStruct((8, tokens), I32),) + (send,) * len(CHUNKS),
         in_specs=[whole()] * 3,
         out_specs=(whole(),) * (1 + len(CHUNKS)),
         compiler_params=params(),
@@ -139,24 +133,14 @@
     )(routes_t, x, index)
 
 
-def numbers_kernel(codes_ref, *refs):
-    first = CHUNKS[0]
+def maps_kernel(codes_ref, index_ref, low_ref, high_ref, scratch_ref):
     code = codes_ref[...].astype(F32).astype(I32)
     tile = jnp.zeros(code.shape, I32)
     for h in range(7):
         tile = tile + jnp.where(code >= (256 << h), 1, 0)
     numbers = jnp.where(code > 0, tile * 128 + (code >> tile) - 128, -1)
-    for (off, cap), index_ref in zip(offsets(), refs):
-        for src in range(GROUPS):
-            start = src * first + off // PER
-            index_ref[src] = numbers[start : start + cap // PER]
-    maps_kernel(refs[0], *refs[len(CHUNKS) :])
-
-
-def maps_kernel(index_ref, low_ref, high_ref, scratch_ref):
-    packed = index_ref.shape[1]
-    cap = packed * PER
-    turned = jnp.concatenate([index_ref[src] for src in range(GROUPS)], axis=0).T
+    index_ref[...] = numbers
+    turned = numbers.T
     tile = turned >> 7
     scratch_ref[0] = jnp.where(turned >= 0, turned & 127, -1)
     place = (iota(turned.shape, 0) % KEPT) + 1
@@ -176,55 +160,27 @@
                 high = high + jnp.where(same, scratch_ref[2, at : at + 1, :], 0)
             lows.append(low)
             highs.append(high)
-        low = jnp.concatenate(lows, axis=0).T
-        high = jnp.concatenate(highs, axis=0).T
-        for src in range(GROUPS):
-            row = src * cap + q * packed
-            low_ref[row : row + packed, :] = low[src * packed : (src + 1) * packed]
-            high_ref[row : row + packed, :] = high[src * packed : (src + 1) * packed]
-
-
-def map_shapes(cap):
-    return [jax.ShapeDtypeStruct((GROUPS * cap, LANES), I32)] * 2
-
-
-def slot_numbers(arrived):
+        rows = slice(q * PACKED, (q + 1) * PACKED)
+        low_ref[rows, :] = jnp.concatenate(lows, axis=0).T
+        high_ref[rows, :] = jnp.concatenate(highs, axis=0).T
+
+
+def slot_maps(arrived):
     rows, width = arrived.shape
-    shapes = [jax.ShapeDtypeStruct((GROUPS, cap // PER, LANES), I32) for cap in CHUNKS]
-    shapes += map_shapes(CHUNKS[0])
-    out = pl.pallas_call(
-        numbers_kernel,
+    shapes = [jax.ShapeDtypeStruct((PACKED, LANES), I32)]
+    shapes += [jax.ShapeDtypeStruct((PER * PACKED, LANES), I32)] * 2
+    index, low, high = pl.pallas_call(
+        maps_kernel,
         grid=(1,),
         out_shape=tuple(shapes),
         in_specs=[pl.BlockSpec((rows, LANES), lambda i: (0, width // LANES - 1))],
-        out_specs=tuple(
-            pl.BlockSpec(s.shape, functools.partial(lambda n, i: (0,) * n, len(s.shape))) for s in shapes
-        ),
-        scratch_shapes=[pltpu.VMEM((3, LANES, LANES), I32)],
-        compiler_params=params(),
-        cost_estimate=cost(2_000_000_000, 1 << 20),
-        name="slot_numbers",
-    )(arrived)
-    return out[: len(CHUNKS)], [out[len(CHUNKS) :]]
-
-
-def later_maps_kernel(index_ref, low_ref, high_ref, token_ref, scratch_ref):
-    token_ref[...] = jnp.zeros_like(token_ref)
-    maps_kernel(index_ref, low_ref, high_ref, scratch_ref)
-
-
-def slot_maps(index):
-    cap = index.shape[1] * PER
-    return pl.pallas_call(
-        later_maps_kernel,
-        out_shape=tuple(map_shapes(cap)) + (TOKEN,),
-        in_specs=[whole()],
-        out_specs=(whole(),) * 3,
+        out_specs=tuple(pl.BlockSpec(s.shape, lambda i: (0, 0)) for s in shapes),
         scratch_shapes=[pltpu.VMEM((3, LANES, LANES), I32)],
         compiler_params=params(),
         cost_estimate=cost(2_000_000_000, 1 << 20),
         name="slot_maps",
-    )(index)
+    )(arrived)
+    return index, (low, high)
 
 
 def skipping(kernel, inputs, extra):
@@ -241,44 +197,39 @@
     return pl.BlockSpec((8, LANES), lambda *i: (0, 0))
 
 
-def gather_kept(values_ref, index_ref, out_ref, stride, base, start):
+def gather_kept(values_ref, index_ref, out_ref, base, start):
     tiles = values_ref.shape[1] // LANES
-    packed_rows = index_ref.shape[1]
     lane_q = iota((8, LANES), 1) // KEPT
-    for src in range(GROUPS):
-        for half in range(packed_rows // 8):
-            idx = index_ref[src, half * 8 : half * 8 + 8, :]
-            spot, tile = idx & 127, idx >> 7
-            result = jnp.zeros((8, LANES), F32)
-            for q in range(PER):
-                row = src * stride + base + q * packed_rows + half * 8
-                here = jnp.where(lane_q == q, tile, -1)
-                for t in range(tiles):
-                    part = values_ref[row : row + 8, t * LANES : (t + 1) * LANES]
-                    taken = jnp.take_along_axis(part, spot, axis=1, mode="promise_in_bounds")
-                    result = jnp.where(here == t, taken, result)
-            place = start + src * packed_rows + half * 8
-            out_ref[place : place + 8, :] = result
+    for group in range(0, PACKED, 8):
+        idx = index_ref[group : group + 8, :]
+        spot, tile = idx & 127, idx >> 7
+        result = jnp.zeros((8, LANES), F32)
+        for q in range(PER):
+            row = base + q * PACKED + group
+            here = jnp.where(lane_q == q, tile, -1)
+            for t in range(tiles):
+                part = values_ref[row : row + 8, t * LANES : (t + 1) * LANES]
+                taken = jnp.take_along_axis(part, spot, axis=1, mode="promise_in_bounds")
+                result = jnp.where(here == t, taken, result)
+        out_ref[start + group : start + group + 8, :] = result
 
 
 def encode_kernel(x_ref, w_ref, bias_ref, index_ref, out_ref, values_ref):
-    inner = w_ref.shape[0]
-    values_ref[...] = (
-        jnp.dot(x_ref[:, :inner], w_ref[...], preferred_element_type=F32) + bias_ref[...]
-    )
-    gather_kept(values_ref, index_ref, out_ref, index_ref.shape[1] * PER, 0, 0)
+    x = quarters(x_ref[:, : PER * w_ref.shape[0]])
+    values_ref[...] = jnp.dot(x, w_ref[...], preferred_element_type=F32) + bias_ref[...]
+    gather_kept(values_ref, index_ref, out_ref, 0, 0)
 
 
 def encode(rows, weight, bias, index, after):
-    total, latents = rows.shape[0], weight.shape[1]
+    inner, latents = weight.shape
     return pl.pallas_call(
         skipping(encode_kernel, 4, len(after)),
-        out_shape=jax.ShapeDtypeStruct((total // PER, LANES), F32),
+        out_shape=jax.ShapeDtypeStruct((PACKED, LANES), F32),
         in_specs=[whole()] * (4 + len(after)),
         out_specs=whole(),
-        scratch_shapes=[pltpu.VMEM((total, latents), F32)],
-        compiler_params=params(),
-        cost_estimate=cost(4 * total * 1024 * latents, 4 << 20),
+        scratch_shapes=[pltpu.VMEM((PER * PACKED, latents), F32)],
+        compiler_params=params(),
+        cost_estimate=cost(4 * PER * PACKED * inner * latents, 4 << 20),
         name="encode",
     )(rows, weight, bias, index, *after)
 
@@ -289,12 +240,11 @@
     reads = []
     for k in range(steps):
         here = pl.ds(k * BLOCK, BLOCK)
-        reads.append(
-            (
-                pltpu.make_async_copy(x_ref.at[:, here], x_held.at[:, here], sem_ref.at[0, k]),
-                pltpu.make_async_copy(w_ref.at[here, :], w_held.at[here, :], sem_ref.at[1, k]),
-            )
-        )
+        reads.append([pltpu.make_async_copy(w_ref.at[here, :], w_held.at[here, :], sem_ref.at[PER, k])])
+        for q in range(PER):
+            source = x_ref.at[:, pl.ds(q * inner + k * BLOCK, BLOCK)]
+            target = x_held.at[pl.ds(q * PACKED, PACKED), here]
+            reads[-1].append(pltpu.make_async_copy(source, target, sem_ref.at[q, k]))
         for copy in reads[-1]:
             copy.start()
     for k in range(steps):
@@ -306,21 +256,21 @@
             values_ref[...] = part + bias_ref[...]
         else:
             values_ref[...] += part
-    gather_kept(values_ref, index_ref, out_ref, index_ref.shape[1] * PER, 0, 0)
+    gather_kept(values_ref, index_ref, out_ref, 0, 0)
 
 
 def encode_streamed(rows, weight, bias, index, after):
-    total, (inner, latents) = rows.shape[0], weight.shape
+    total, (inner, latents) = PER * PACKED, weight.shape
     return pl.pallas_call(
         skipping(encode_streamed_kernel, 4, len(after)),
-        out_shape=jax.ShapeDtypeStruct((total // PER, LANES), F32),
+        out_shape=jax.ShapeDtypeStruct((PACKED, LANES), F32),
         in_specs=[pl.BlockSpec(memory_space=pl.ANY)] * 2 + [whole()] * (2 + len(after)),
         out_specs=whole(),
         scratch_shapes=[
             pltpu.VMEM((total, latents), F32),
             pltpu.VMEM((total, inner), BF16),
             pltpu.VMEM((inner, latents), BF16),
-            pltpu.SemaphoreType.DMA((2, inner // BLOCK)),
+            pltpu.SemaphoreType.DMA((PER + 1, inner // BLOCK)),
         ],
         compiler_params=params(),
         cost_estimate=cost(4 * total * inner * latents, 4 << 20),
@@ -331,16 +281,15 @@
 def latent_gradient_kernel(r_ref, w_ref, *refs):
     index_refs, out_ref, values_ref = refs[:-2], refs[-2], refs[-1]
     values_ref[...] = lax.dot_general(
-        r_ref[...], w_ref[...], (((1,), (1,)), ((), ())), preferred_element_type=F32
+        quarters(r_ref[...]), w_ref[...], (((1,), (1,)), ((), ())), preferred_element_type=F32
     )
-    start = 0
-    for (off, cap), index_ref in zip(offsets(), index_refs):
-        gather_kept(values_ref, index_ref, out_ref, CAP, off, start)
-        start += GROUPS * cap // PER
+    for c, index_ref in enumerate(index_refs):
+        gather_kept(values_ref, index_ref, out_ref, c * PER * PACKED, c * PACKED)
 
 
 def latent_gradient(rows, weight, index):
-    total, latents = rows.shape[0], weight.shape[0]
+    latents = weight.shape[0]
+    total = GROUPS * CAP
     return pl.pallas_call(
         latent_gradient_kernel,
         out_shape=jax.ShapeDtypeStruct((total // PER, LANES), F32),
@@ -353,46 +302,43 @@
     )(rows, weight, *index)
 
 
-def spread_kept(kept_ref, low_ref, high_ref, dense_ref, packed_rows, tiles, source=0, target=0):
-    for src in range(GROUPS):
-        place = source + src * packed_rows
-        kept = kept_ref[place : place + packed_rows, :]
-        for q in range(0, PER, 2):
-            row = src * packed_rows * PER + q * packed_rows
+def spread_kept(kept_ref, low_ref, high_ref, dense_ref, tiles, source=0, target=0):
+    for group in range(0, PACKED, 16):
+        kept = kept_ref[source + group : source + group + 16, :]
+        for q in range(PER):
+            row = q * PACKED + group
             for column, t in enumerate(tiles):
                 word_ref = (low_ref, high_ref)[t // 4]
-                pieces = []
-                for half in range(2):
-                    start = row + half * packed_rows
-                    which = (word_ref[start : start + packed_rows, :] >> (6 * (t % 4))) & 63
-                    spot = jnp.maximum(which - 1, 0) + (q + half) * KEPT
-                    taken = jnp.take_along_axis(kept, spot, axis=1, mode="promise_in_bounds")
-                    pieces.append(jnp.where(which > 0, taken, 0.0))
-                rows = slice(target + row, target + row + 2 * packed_rows)
-                dense_ref[rows, column * LANES : (column + 1) * LANES] = jnp.concatenate(
-                    pieces, axis=0
-                ).astype(BF16)
+                which = (word_ref[row : row + 16, :] >> (6 * (t % 4))) & 63
+                spot = jnp.maximum(which - 1, 0) + q * KEPT
+                taken = jnp.take_along_axis(kept, spot, axis=1, mode="promise_in_bounds")
+                dense_ref[target + row : target + row + 16, column * LANES : (column + 1) * LANES] = (
+                    jnp.where(which > 0, taken, 0.0).astype(BF16)
+                )
 
 
 def spread_latents(pre_ref, low_ref, high_ref, kept_ref, rows_ref):
     pre = pre_ref[...]
     kept_ref[...] = (pre / (1.0 + jnp.exp(-pre))).astype(BF16).astype(F32)
     tiles = range(rows_ref.shape[1] // LANES)
-    spread_kept(kept_ref, low_ref, high_ref, rows_ref, pre_ref.shape[0] // GROUPS, tiles)
+    spread_kept(kept_ref, low_ref, high_ref, rows_ref, tiles)
 
 
 def decode_kernel(pre_ref, low_ref, high_ref, w_ref, out_ref, token_ref, kept_ref, rows_ref, made_ref, sem_ref):
     token_ref[...] = jnp.zeros_like(token_ref)
     spread_latents(pre_ref, low_ref, high_ref, kept_ref, rows_ref)
     copies = []
-    for j in range(w_ref.shape[1] // BLOCK):
+    inner = w_ref.shape[1]
+    for j in range(inner // BLOCK):
         here = pl.ds(j * BLOCK, BLOCK)
         made_ref[:, here] = jnp.dot(
             rows_ref[...], w_ref[:, here], preferred_element_type=F32
         ).astype(BF16)
-        copy = pltpu.make_async_copy(made_ref.at[:, here], out_ref.at[:, here], sem_ref.at[j])
-        copy.start()
-        copies.append(copy)
+        for q in range(PER):
+            source = made_ref.at[pl.ds(q * PACKED, PACKED), here]
+            target = out_ref.at[:, pl.ds(q * inner + j * BLOCK, BLOCK)]
+            copies.append(pltpu.make_async_copy(source, target, sem_ref.at[j, q]))
+            copies[-1].start()
     for copy in copies:
         copy.wait()
 
@@ -406,14 +352,14 @@
     latents, inner = weight.shape
     return pl.pallas_call(
         skipping(decode_kernel, 4, len(after)),
-        out_shape=(hbm((total, inner), BF16), TOKEN),
+        out_shape=(hbm((PACKED, PER * inner), BF16), TOKEN),
         in_specs=[whole()] * (4 + len(after)),
         out_specs=(anywhere(), whole()),
         scratch_shapes=[
             pltpu.VMEM(pre.shape, F32),
             pltpu.VMEM((total, latents), BF16),
             pltpu.VMEM((total, inner), BF16),
-            pltpu.SemaphoreType.DMA((inner // BLOCK,)),
+            pltpu.SemaphoreType.DMA((inner // BLOCK, PER)),
         ],
         compiler_params=params(),
         cost_estimate=cost(4 * total * inner * latents, 6 << 20),
@@ -459,22 +405,33 @@
     back_refs, send_ref = refs[3 : 3 + count], refs[3 + count]
     tokens = x_ref.shape[0]
     info = info_ref[...]
+    width = x_ref.shape[1]
+    first = quarter_keys(tokens)
+    keys = token_keys(info)
+    hits = []
+    for i in range(count * PER):
+        slot = first + i * PLACES
+        hits.append(as_ones((slot == keys[0]) | (slot == keys[1])))
     total = jnp.zeros(x_ref.shape, F32)
-    for (off, cap), back_ref in zip(offsets(), back_refs):
-        hit = chunk_hits(info, off, cap, tokens).astype(F32).astype(BF16)
+    for c, back_ref in enumerate(back_refs):
         total = total + lax.dot_general(
-            hit, back_ref[...], (((0,), (0,)), ((), ())), preferred_element_type=F32
+            jnp.concatenate(hits[c * PER : (c + 1) * PER], axis=0),
+            quarters(back_ref[...]),
+            (((0,), (0,)), ((), ())),
+            preferred_element_type=F32,
         )
     residual = (total + bias_ref[...] - x_ref[...].astype(F32)).astype(BF16)
-    hit = chunk_hits(info, 0, CAP, tokens).astype(F32).astype(BF16)
-    send_ref[...] = jnp.dot(hit, residual, preferred_element_type=F32).astype(BF16)
+    for i, hit in enumerate(hits):
+        send_ref[:, i * width : (i + 1) * width] = jnp.dot(
+            hit, residual, preferred_element_type=F32
+        ).astype(BF16)
 
 
 def form_residual(info, x, bias, back, after):
     tokens, width = x.shape
     return pl.pallas_call(
         skipping(residual_kernel, 3 + len(CHUNKS), len(after)),
-        out_shape=jax.ShapeDtypeStruct((GROUPS * CAP, width), BF16),
+        out_shape=jax.ShapeDtypeStruct((PACKED, len(CHUNKS) * PER * width), BF16),
         in_specs=[whole()] * (3 + len(CHUNKS) + len(after)),
         out_specs=whole(),
         compiler_params=params(),
@@ -488,17 +445,19 @@
     refs[-1][...] = jnp.zeros(refs[-1].shape, F32)
     for src, dst in zip(refs[:half], refs[half:]):
         block = dst.shape[0]
-        here = pl.ds(pl.multiple_of(pl.program_id(0) * block, block), block)
-        dst[...] = src[:, here].T
+        for q in range(PER):
+            start = q * block * pl.num_programs(0) + pl.program_id(0) * block
+            here = pl.ds(pl.multiple_of(start, block), block)
+            dst[:, q * PACKED : (q + 1) * PACKED] = src[:, here].T
 
 
 def turn(arrived, inner):
     return pl.pallas_call(
         turn_kernel,
         grid=(4,),
-        out_shape=tuple(hbm((inner, a.shape[0]), BF16) for a in arrived) + (TOKEN,),
+        out_shape=tuple(hbm((inner, PER * PACKED), BF16) for a in arrived) + (TOKEN,),
         in_specs=[whole()] * len(arrived),
-        out_specs=tuple(pl.BlockSpec((inner // 4, a.shape[0]), lambda i: (i, 0)) for a in arrived)
+        out_specs=tuple(pl.BlockSpec((inner // 4, PER * PACKED), lambda i: (i, 0)) for a in arrived)
         + (token_spec(),),
         compiler_params=params(),
         cost_estimate=cost(4_000_000_000, 4 << 20),
@@ -531,9 +490,7 @@
         for c, cap in enumerate(CHUNKS):
             tiles = range(j * BLOCK // LANES, (j + 1) * BLOCK // LANES)
             words = map_refs[2 * c : 2 * c + 2]
-            spread_kept(
-                kept_ref, *words, grad_ref.at[j], cap // PER, tiles, starts[c], starts[c] * PER
-            )
+            spread_kept(kept_ref, *words, grad_ref.at[j], tiles, starts[c], starts[c] * PER)
 
     blocks = grad_ref.shape[0]
     spread(0)
@@ -587,11 +544,11 @@
     block = out_ref.shape[0]
     here = pl.ds(pl.multiple_of(pl.program_id(0) * block, block), block)
     total = None
-    for (off, cap), latent_ref in zip(offsets(), latent_refs):
-        rows = [res_ref[src * CAP + off : src * CAP + off + cap, :] for src in range(GROUPS)]
+    width = out_ref.shape[1]
+    for c, latent_ref in enumerate(latent_refs):
         part = lax.dot_general(
             latent_ref[:, here],
-            jnp.concatenate(rows, axis=0),
+            quarters(res_ref[:, c * PER * width : (c + 1) * PER * width]),
             (((0,), (0,)), ((), ())),
             preferred_element_type=F32,
         )
@@ -600,7 +557,7 @@
 
 
 def decoder_grad(latent, res):
-    latents, inner = latent[0].shape[1], res.shape[1]
+    latents, inner = latent[0].shape[1], 1024
     block = 256
     return pl.pallas_call(
         decoder_grad_kernel,
@@ -663,19 +620,17 @@
 
     info, *sends = pack(routes.T, x_home, latent_index.reshape(tokens, 2 * KEPT))
     arrived = [exchange(s) for s in sends]
-    index, maps = slot_numbers(arrived[0])
-    *later, token = slot_maps(index[1])
-    maps.append(later)
-
-    pre, back, after, tokens_in = [], [], (), (token,)
+    index, maps = zip(*[slot_maps(a) for a in arrived])
+
+    pre, back, after = [], [], ()
     for c in range(len(CHUNKS)):
         if c == 0:
             part = encode(arrived[c], in_vmem(enc), bias, index[c], after)
         else:
             part = encode_streamed(arrived[c], enc, bias, index[c], after)
         pre.append(width_sum(part))
-        decoded, token = decode(pre[c], *maps[c], dec, tokens_in)
-        after, tokens_in = (token,), ()
+        decoded, token = decode(pre[c], *maps[c], dec, ())
+        after = (token,)
         back.append(exchange(decoded))
 
     *turned, token = turn(arrived, inner)

time: 225 us -> 228 us (1.013)
  starting transfers between devices: 39.5 us -> 44.1 us
  blocking collectives: 93.9 us -> 90 us
  Pallas kernels: 38.2 us -> 40.5 us
    all_to_all x2, blocking collectives: 93.9 us -> 90 us  [exchange(): lax.all_to_all(rows.reshape(GROUPS, count // GROUPS, width), 'feat', spli...]
    ppermute x15, starting transfers between devices: 20.9 us -> 24.5 us  [width_sum(): lax.ppermute(part, 'width', [(a, a ^ m) for a in range(size)])]
    all_to_all x3, waiting for transfers between devices: 19.9 us -> 16.5 us  [exchange(): lax.all_to_all(rows.reshape(GROUPS, count // GROUPS, width), 'feat', spli...]
    ppermute x15, waiting for transfers between devices: 23.6 us -> 26.8 us  [width_sum(): lax.ppermute(part, 'width', [(a, a ^ m) for a in range(size)])]
  transfers between devices with their start and end apart: 18 -> 18, of which waited for: 15 -> 14; matrix products, arithmetic and copies ran while one was open for 2% -> 1% of each run, Pallas kernels for 12% -> 12%
where the time goes in v5:
time: 228 us; the launch traced here: 227 us
  blocking collectives  90 us (39%)
  starting transfers between devices  44.1 us (19%)
  waiting for transfers between devices  43.3 us (19%)
  Pallas kernels  40.5 us (18%)
  local copies, waits for them, and re-layouts  7.85 us (3%)
    all_to_all x2, blocking collectives, exchange(): lax.all_to_all(rows.reshape(GROUPS, count // GROUPS, width), 'feat', spli...  90 us
    ppermute x15, waiting for transfers between devices, width_sum(): lax.ppermute(part, 'width', [(a, a ^ m) for a in range(size)])  26.8 us
    ppermute x15, starting transfers between devices, width_sum(): lax.ppermute(part, 'width', [(a, a ^ m) for a in range(size)])  24.5 us
    all_to_all x3, starting transfers between devices, exchange(): lax.all_to_all(rows.reshape(GROUPS, count // GROUPS, width), 'feat', spli...  19.6 us
    all_to_all x3, waiting for transfers between devices, exchange(): lax.all_to_all(rows.reshape(GROUPS, count // GROUPS, width), 'feat', spli...  16.5 us
    pallas_call x2, Pallas kernels, decode(): pl.pallas_call(skipping(decode_kernel, 4, len(after)), out_shape=(hbm((PA...  7.73 us
    pallas_call x1, Pallas kernels, encoder_grad(): pl.pallas_call(functools.partial(encoder_grad_kernel, scale), out_shape=j...  5.56 us
    pallas_call x2, Pallas kernels, slot_maps(): pl.pallas_call(maps_kernel, grid=(1,), out_shape=tuple(shapes), in_specs=...  4.77 us
  transfers between devices with their start and end apart: 18, of which 14 were waited for; matrix products, arithmetic and copies ran while one was open for 1% of the time, Pallas kernels for 12%

profile of v5, /device:TPU:32, one launch (start us, length us, event | category | flops | bytes accessed | tf_op | source)
XLA Modules:
  0.0 227.1 jit_solution(5711698994390848288)
XLA Ops:
  0.6 0.9 copy.10.index_ref
  1.6 1.1 copy.11
  2.7 0.7 copy-done.7
  3.4 2.3 pack_tokens.1
  5.6 0.8 copy-done.2
  6.4 38.2 %all_to_all.25 = bf16[16,8,4224]{2,1,0:T(8,128)(2,1)S(1)} all-to-all(bf16[16,8,4224]{2,1,0:T(8,128)(2,1)S(1)} %bitcast.35), channel_id=1, replica_groups=mesh['width'=16,'feat'=16] {'feat'}, dimensions={0} | all-to-all | bytes 2162688 | tf_op jit(solution)/shard_map/all_to_all | solution.py:576
  44.6 5.4 %all-to-all-start.2 = ((bf16[16,8,4224]{2,1,0:T(8,128)(2,1)}), bf16[16,8,4224]{2,1,0:T(8,128)(2,1)}, u32[]{:S(2)}, u32[]{:S(2)}) async-start(bf16[16,8,4224]{2,1,0:T(8,128)(2,1)} %bitcast.7), calls=%async_computation.2 | async-start | bytes 2162688 | tf_op jit(solution)/shard_map/all_to_all | solution.py:576
  50.0 2.0 slot_maps.2
  52.1 1.6 encode.1
  53.8 1.2 collective-permute-done
  55.1 3.1 %collective-permute-start.3 = (f32[128,128]{1,0:T(8,128)S(1)}, f32[128,128]{1,0:T(8,128)S(1)}, u32[]{:S(2)}, u32[]{:S(2)}) collective-permute-start(f32[128,128]{1,0:T(8,128)S(1)} %add.36), channel_id=1, source_target_pairs={{0,192},{16,208},{32,224},{48,240},{64,128},{80,144},{96,160},{112... | collective-permute-start | bytes 196616 | tf_op jit(solution)/shard_map/ppermute | solution.py:602
  58.2 0.6 collective-permute-start.2
  59.3 2.0 collective-permute-done.3
  61.3 3.0 %collective-permute-done.2 = f32[128,128]{1,0:T(8,128)S(1)} collective-permute-done((f32[128,128]{1,0:T(8,128)S(1)}, f32[128,128]{1,0:T(8,128)S(1)}, u32[]{:S(2)}, u32[]{:S(2)}) %collective-permute-start.2) | collective-permute-done | bytes 65568 | tf_op jit(solution)/shard_map/ppermute | solution.py:602
  64.3 2.8 %collective-permute-start.4 = (f32[128,128]{1,0:T(8,128)S(1)}, f32[128,128]{1,0:T(8,128)S(1)}, u32[]{:S(2)}, u32[]{:S(2)}) collective-permute-start(f32[128,128]{1,0:T(8,128)S(1)} %add_add_fusion.1), channel_id=1, source_target_pairs={{0,32},{16,48},{32,0},{48,16},{64,96},{80,112},{96,64},{112,80},{1... | collective-permute-start | bytes 196616 | tf_op jit(solution)/shard_map/ppermute | solution.py:602
  67.1 0.6 copy.13
  67.7 4.0 %collective-permute-done.4 = f32[128,128]{1,0:T(8,128)S(1)} collective-permute-done((f32[128,128]{1,0:T(8,128)S(1)}, f32[128,128]{1,0:T(8,128)S(1)}, u32[]{:S(2)}, u32[]{:S(2)}) %collective-permute-start.4) | collective-permute-done | bytes 65568 | tf_op jit(solution)/shard_map/ppermute | solution.py:602
  71.8 3.6 %decode.2 = (bf16[128,4096]{1,0:T(8,128)(2,1)}, f32[8,128]{1,0:T(8,128)S(1)}) custom-call(f32[128,128]{1,0:T(8,128)S(1)} %add.40.refs_0_, s32[512,128]{1,0:T(8,128)S(1)} %get-tuple-element.25.refs_1_.refs_2_, s32[512,128]{1,0:T(8,128)S(1)} %get-tuple-element.26.refs_2_.refs_3_, bf16[1024,1024]{1,0:T(8,128)(2,1)S(1)} %bitcast.25), custom_call_target="tpu_custom_call" | custom-call | flops 2147483648 | bytes 6291456 | tf_op jit(solution)/shard_map/decode/pallas_call | solution.py:353
  75.5 6.8 %all-to-all-start.1 = ((bf16[16,8,4096]{2,1,0:T(8,128)(2,1)}), bf16[16,8,4096]{2,1,0:T(8,128)(2,1)S(1)}, u32[]{:S(2)}, u32[]{:S(2)}) async-start(bf16[16,8,4096]{2,1,0:T(8,128)(2,1)} %bitcast.41), calls=%async_computation.1 | async-start | bytes 2097152 | tf_op jit(solution)/shard_map/all_to_all | solution.py:576
  82.3 2.8 %slot_maps.3 = (s32[128,128]{1,0:T(8,128)S(1)}, s32[512,128]{1,0:T(8,128)S(1)}, s32[512,128]{1,0:T(8,128)S(1)}) custom-call(bf16[128,4224]{1,0:T(8,128)(2,1)} %bitcast.8.codes_ref.refs_0_.refs_1_), custom_call_target="tpu_custom_call" | custom-call | flops 2000000000 | bytes 1048576 | tf_op jit(solution)/shard_map/slot_maps/pallas_call | solution.py:172
  85.1 3.4 %encode_streamed.1 = f32[128,128]{1,0:T(8,128)S(1)} custom-call(bf16[128,4224]{1,0:T(8,128)(2,1)} %bitcast.8.codes_ref.refs_0_.refs_1_, bf16[1024,1024]{1,0:T(8,128)(2,1)} %bitcast.37, f32[1,1024]{1,0:T(1,128)S(1)} %broadcast_select_fusion.refs_2_, s32[128,128]{1,0:T(8,128)S(1)} %get-tuple-element.29.refs_3_.refs_1_, f32[8,128]{1,0:T(8,128)S(1)} %get-tuple-element.30.refs_4_), custom_call_target="tpu_custom_call" | custom-call | flops 2147483648 | bytes 4194304 | tf_op jit(solution)/shard_map/encode_streamed/pallas_call | solution.py:264
  88.6 1.2 collective-permute-done.5
  89.9 2.0 collective-permute-start.8
  91.9 0.9 collective-permute-start.7
  92.8 1.2 collective-permute-start.6
  94.0 1.4 collective-permute-done.8
  95.4 2.5 %collective-permute-done.7 = f32[128,128]{1,0:T(8,128)S(1)} collective-permute-done((f32[128,128]{1,0:T(8,128)S(1)}, f32[128,128]{1,0:T(8,128)S(1)}, u32[]{:S(2)}, u32[]{:S(2)}) %collective-permute-start.7) | collective-permute-done | bytes 65568 | tf_op jit(solution)/shard_map/ppermute | solution.py:602
  98.0 3.3 %collective-permute-start.9 = (f32[128,128]{1,0:T(8,128)S(1)}, f32[128,128]{1,0:T(8,128)S(1)}, u32[]{:S(2)}, u32[]{:S(2)}) collective-permute-start(f32[128,128]{1,0:T(8,128)S(1)} %add_add_fusion), channel_id=1, source_target_pairs={{0,32},{16,48},{32,0},{48,16},{64,96},{80,112},{96,64},{112,80},{1... | collective-permute-start | bytes 196616 | tf_op jit(solution)/shard_map/ppermute | solution.py:602
  101.3 4.1 %collective-permute-done.9 = f32[128,128]{1,0:T(8,128)S(1)} collective-permute-done((f32[128,128]{1,0:T(8,128)S(1)}, f32[128,128]{1,0:T(8,128)S(1)}, u32[]{:S(2)}, u32[]{:S(2)}) %collective-permute-start.9) | collective-permute-done | bytes 65568 | tf_op jit(solution)/shard_map/ppermute | solution.py:602
  105.5 4.1 %decode.3 = (bf16[128,4096]{1,0:T(8,128)(2,1)}, f32[8,128]{1,0:T(8,128)}) custom-call(f32[128,128]{1,0:T(8,128)S(1)} %add.45.refs_0_.refs_1_, s32[512,128]{1,0:T(8,128)S(1)} %get-tuple-element.31.refs_1_.refs_4_, s32[512,128]{1,0:T(8,128)S(1)} %get-tuple-element.32.refs_2_.refs_5_, bf16[1024,1024]{1,0:T(8,128)(2,1)S(1)} %bitcast.26), custom_call_target="tpu_custom_call" | custom-call | flops 2147483648 | bytes 6291456 | tf_op jit(solution)/shard_map/decode/pallas_call | solution.py:353
  109.6 7.4 %all-to-all-start.3 = ((bf16[16,8,4096]{2,1,0:T(8,128)(2,1)}), bf16[16,8,4096]{2,1,0:T(8,128)(2,1)S(1)}, u32[]{:S(2)}, u32[]{:S(2)}) async-start(bf16[16,8,4096]{2,1,0:T(8,128)(2,1)} %bitcast.42), calls=%async_computation.3 | async-start | bytes 2097152 | tf_op jit(solution)/shard_map/all_to_all | solution.py:576
  117.1 3.4 %turn_rows.1 = (bf16[1024,512]{1,0:T(8,128)(2,1)}, bf16[1024,512]{1,0:T(8,128)(2,1)}, f32[8,128]{1,0:T(8,128)S(1)}) custom-call(bf16[128,4224]{1,0:T(8,128)(2,1)S(1)} %bitcast.34, bf16[128,4224]{1,0:T(8,128)(2,1)} %bitcast.8.codes_ref.refs_0_.refs_1_), custom_call_target="tpu_custom_call" | custom-call | flops 4000000000 | bytes 4194304 | tf_op jit(solution)/shard_map/turn_rows/pallas_call | solution.py:455
  120.5 4.2 %make_latents.1 = (bf16[512,1024]{1,0:T(8,128)(2,1)}, bf16[512,1024]{1,0:T(8,128)(2,1)}, f32[8,128]{1,0:T(8,128)S(1)}) custom-call(f32[128,128]{1,0:T(8,128)S(1)} %add.40.refs_0_, f32[128,128]{1,0:T(8,128)S(1)} %add.45.refs_0_.refs_1_, s32[512,128]{1,0:T(8,128)S(1)} %copy-done.11, s32[512,128]{1,0:T(8,128)S(1)} %copy-done.14, s32[512,128]{1,0:T(8,128)S(1)} %copy-done.17, ...), custom_call_target="tpu_custom_call" | custom-call | flops 4000000000 | bytes 4194304 | tf_op jit(solution)/shard_map/make_latents/pallas_call | solution.py:387
  124.8 16.4 %all-to-all-done.3 = bf16[16,8,4096]{2,1,0:T(8,128)(2,1)S(1)} async-done(((bf16[16,8,4096]{2,1,0:T(8,128)(2,1)}), bf16[16,8,4096]{2,1,0:T(8,128)(2,1)S(1)}, u32[]{:S(2)}, u32[]{:S(2)}) %all-to-all-start.3) | async-done | bytes 1048608 | tf_op jit(solution)/shard_map/all_to_all | solution.py:576
  141.1 1.5 form_residual.1
  142.7 51.8 %all_to_all.26 = bf16[16,8,8192]{2,1,0:T(8,128)(2,1)S(1)} all-to-all(bf16[16,8,8192]{2,1,0:T(8,128)(2,1)S(1)} %bitcast.22), channel_id=1, replica_groups=mesh['width'=16,'feat'=16] {'feat'}, dimensions={0} | all-to-all | bytes 4194304 | tf_op jit(solution)/shard_map/all_to_all | solution.py:576
  194.5 3.0 %latent_gradient.1 = f32[256,128]{1,0:T(8,128)S(1)} custom-call(bf16[128,8192]{1,0:T(8,128)(2,1)S(1)} %bitcast.28, bf16[1024,1024]{1,0:T(8,128)(2,1)S(1)} %bitcast.27, s32[128,128]{1,0:T(8,128)S(1)} %get-tuple-element.24.refs_3_.refs_0_, s32[128,128]{1,0:T(8,128)S(1)} %get-tuple-element.29.refs_3_.refs_1_), custom_call_target="tpu_custom_call" | custom-call | flops 4294967296 | bytes 4194304 | tf_op jit(solution)/shard_map/latent_gradient/pallas_call | solution.py:293
  197.6 1.3 collective-permute-done.10
  198.9 6.6 %collective-permute-start.13 = (f32[256,128]{1,0:T(8,128)S(1)}, f32[256,128]{1,0:T(8,128)S(1)}, u32[]{:S(2)}, u32[]{:S(2)}) collective-permute-start(f32[256,128]{1,0:T(8,128)S(1)} %add.46.refs_0_), channel_id=1, source_target_pairs={{0,192},{16,208},{32,224},{48,240},{64,128},{80,144},{96,160},{112... | collective-permute-start | bytes 393224 | tf_op jit(solution)/shard_map/ppermute | solution.py:602
  205.6 0.7 collective-permute-start.12
  206.5 3.0 %decoder_grad.1 = (bf16[1024,1024]{1,0:T(8,128)(2,1)S(1)}, f32[8,128]{1,0:T(8,128)S(1)}) custom-call(bf16[512,1024]{1,0:T(8,128)(2,1)S(1)} %copy-done.8, bf16[512,1024]{1,0:T(8,128)(2,1)S(1)} %copy-done.9, bf16[128,8192]{1,0:T(8,128)(2,1)S(1)} %bitcast.29), custom_call_target="tpu_custom_call" | custom-call | flops 2147483648 | bytes 6291456 | tf_op jit(solution)/shard_map/decoder_grad/pallas_call | solution.py:562
  209.6 1.9 collective-permute-done.13.refs_3_
  211.5 2.0 collective-permute-done.12.refs_2_
  213.5 2.1 collective-permute-start.14
  215.6 2.7 %reshape.71 = bf16[1,1024,2,512]{3,2,1,0:T(2,128)(2,1)} reshape(bf16[1024,1024]{1,0:T(8,128)(2,1)S(1)} %get-tuple-element.41) | data formatting | bytes 4194304 | tf_op jit(solution)/shard_map/reshape | solution.py:644
  218.3 2.0 collective-permute-done.14
  220.4 0.9 copy-done.21
  221.3 5.6 %encoder_grad.1 = bf16[1024,1024]{1,0:T(8,128)(2,1)} custom-call(f32[256,128]{1,0:T(8,128)S(1)} %add.47.lg_ref, f32[128,128]{1,0:T(8,128)S(1)} %add.40.refs_0_, f32[128,128]{1,0:T(8,128)S(1)} %add.45.refs_0_.refs_1_, s32[512,128]{1,0:T(8,128)S(1)} %copy-done.12, s32[512,128]{1,0:T(8,128)S(1)} %copy-done.15, s32[512,128]{1,0:T(8,128)S(1)} %copy-done.18, ...), custom_call_target="tpu_custom_call" | custom-call | flops 4294967296 | bytes 6291456 | tf_op jit(solution)/shard_map/encoder_grad/pallas_call | solution.py:523
  (68 shorter events, 1.4 us)
Async XLA Ops:
  2.7 0.7 copy-start.7
  5.6 0.8 copy-start.2
  6.4 43.6 %copy-start.23 = (f32[1,1024]{1,0:T(1,128)S(1)}, f32[1,1024]{1,0:T(1,128)}, u32[]{:S(2)}) copy-start(f32[1,1024]{1,0:T(1,128)} %param.9) | copy-start | bytes 12292
  44.6 7.5 %copy-start.4 = (bf16[16,8,4224]{2,1,0:T(8,128)(2,1)}, bf16[16,8,4224]{2,1,0:T(8,128)(2,1)S(1)}, u32[]{:S(2)}) copy-start(bf16[16,8,4224]{2,1,0:T(8,128)(2,1)S(1)} %all_to_all.25) | copy-start | bytes 3244036
  44.6 30.9 %all-to-all-start.2 = ((bf16[16,8,4224]{2,1,0:T(8,128)(2,1)}), bf16[16,8,4224]{2,1,0:T(8,128)(2,1)}, u32[]{:S(2)}, u32[]{:S(2)}) async-start(bf16[16,8,4224]{2,1,0:T(8,128)(2,1)} %bitcast.7), calls=%async_computation.2 | async-start | bytes 2162688 | tf_op jit(solution)/shard_map/all_to_all | solution.py:576
  50.0 2.1 copy-start.6
  52.0 19.7 %copy-start.10 = (s32[512,128]{1,0:T(8,128)}, s32[512,128]{1,0:T(8,128)S(1)}, u32[]{:S(2)}) copy-start(s32[512,128]{1,0:T(8,128)S(1)} %get-tuple-element.25.refs_1_.refs_2_) | copy-start | bytes 786436
  52.1 19.7 %copy-start.13 = (s32[512,128]{1,0:T(8,128)}, s32[512,128]{1,0:T(8,128)S(1)}, u32[]{:S(2)}) copy-start(s32[512,128]{1,0:T(8,128)S(1)} %get-tuple-element.26.refs_2_.refs_3_) | copy-start | bytes 786436
  52.1 15.0 %copy-start.22 = (bf16[1,1024,2,512]{3,2,1,0:T(2,128)(2,1)S(1)}, bf16[1,1024,2,512]{3,2,1,0:T(2,128)(2,1)}, u32[]{:S(2)}) copy-start(bf16[1,1024,2,512]{3,2,1,0:T(2,128)(2,1)} %param.10) | copy-start | bytes 6291460
  53.7 1.3 collective-permute-start
  55.1 6.2 %collective-permute-start.3 = (f32[128,128]{1,0:T(8,128)S(1)}, f32[128,128]{1,0:T(8,128)S(1)}, u32[]{:S(2)}, u32[]{:S(2)}) collective-permute-start(f32[128,128]{1,0:T(8,128)S(1)} %add.36), channel_id=1, source_target_pairs={{0,192},{16,208},{32,224},{48,240},{64,128},{80,144},{96,160},{112... | collective-permute-start | bytes 196616 | tf_op jit(solution)/shard_map/ppermute | solution.py:602
  58.2 6.1 %collective-permute-start.2 = (f32[128,128]{1,0:T(8,128)S(1)}, f32[128,128]{1,0:T(8,128)S(1)}, u32[]{:S(2)}, u32[]{:S(2)}) collective-permute-start(f32[128,128]{1,0:T(8,128)S(1)} %add.36), channel_id=1, source_target_pairs={{0,128},{16,144},{32,160},{48,176},{64,192},{80,208},{96,224},{112... | collective-permute-start | bytes 196616 | tf_op jit(solution)/shard_map/ppermute | solution.py:602
  58.8 5.5 %collective-permute-start.1 = (f32[128,128]{1,0:T(8,128)S(1)}, f32[128,128]{1,0:T(8,128)S(1)}, u32[]{:S(2)}, u32[]{:S(2)}) collective-permute-start(f32[128,128]{1,0:T(8,128)S(1)} %add.36), channel_id=1, source_target_pairs={{0,64},{16,80},{32,96},{48,112},{64,0},{80,16},{96,32},{112,48},{1... | collective-permute-start | bytes 196616 | tf_op jit(solution)/shard_map/ppermute | solution.py:602
  64.3 7.5 %collective-permute-start.4 = (f32[128,128]{1,0:T(8,128)S(1)}, f32[128,128]{1,0:T(8,128)S(1)}, u32[]{:S(2)}, u32[]{:S(2)}) collective-permute-start(f32[128,128]{1,0:T(8,128)S(1)} %add_add_fusion.1), channel_id=1, source_target_pairs={{0,32},{16,48},{32,0},{48,16},{64,96},{80,112},{96,64},{112,80},{1... | collective-permute-start | bytes 196616 | tf_op jit(solution)/shard_map/ppermute | solution.py:602
  67.7 37.7 %copy-start = (bf16[128,8,2,512]{3,1,2,0:T(8,128)(2,1)}, bf16[128,8,2,512]{3,1,2,0:T(8,128)(2,1)S(1)}, u32[]{:S(2)}) copy-start(bf16[128,8,2,512]{3,1,2,0:T(8,128)(2,1)S(1)} %copy.13) | copy-start | bytes 6291460
  75.5 34.1 %all-to-all-start.1 = ((bf16[16,8,4096]{2,1,0:T(8,128)(2,1)}), bf16[16,8,4096]{2,1,0:T(8,128)(2,1)S(1)}, u32[]{:S(2)}, u32[]{:S(2)}) async-start(bf16[16,8,4096]{2,1,0:T(8,128)(2,1)} %bitcast.41), calls=%async_computation.1 | async-start | bytes 2097152 | tf_op jit(solution)/shard_map/all_to_all | solution.py:576
  85.0 20.4 %copy-start.16 = (s32[512,128]{1,0:T(8,128)}, s32[512,128]{1,0:T(8,128)S(1)}, u32[]{:S(2)}) copy-start(s32[512,128]{1,0:T(8,128)S(1)} %get-tuple-element.31.refs_1_.refs_4_) | copy-start | bytes 786436
  85.0 20.4 %copy-start.19 = (s32[512,128]{1,0:T(8,128)}, s32[512,128]{1,0:T(8,128)S(1)}, u32[]{:S(2)}) copy-start(s32[512,128]{1,0:T(8,128)S(1)} %get-tuple-element.32.refs_2_.refs_5_) | copy-start | bytes 786436
  88.5 1.3 collective-permute-start.5
  89.9 5.6 %collective-permute-start.8 = (f32[128,128]{1,0:T(8,128)S(1)}, f32[128,128]{1,0:T(8,128)S(1)}, u32[]{:S(2)}, u32[]{:S(2)}) collective-permute-start(f32[128,128]{1,0:T(8,128)S(1)} %add.41), channel_id=1, source_target_pairs={{0,192},{16,208},{32,224},{48,240},{64,128},{80,144},{96,160},{112... | collective-permute-start | bytes 196616 | tf_op jit(solution)/shard_map/ppermute | solution.py:602
  91.9 6.1 %collective-permute-start.7 = (f32[128,128]{1,0:T(8,128)S(1)}, f32[128,128]{1,0:T(8,128)S(1)}, u32[]{:S(2)}, u32[]{:S(2)}) collective-permute-start(f32[128,128]{1,0:T(8,128)S(1)} %add.41), channel_id=1, source_target_pairs={{0,128},{16,144},{32,160},{48,176},{64,192},{80,208},{96,224},{112... | collective-permute-start | bytes 196616 | tf_op jit(solution)/shard_map/ppermute | solution.py:602
  92.8 5.1 %collective-permute-start.6 = (f32[128,128]{1,0:T(8,128)S(1)}, f32[128,128]{1,0:T(8,128)S(1)}, u32[]{:S(2)}, u32[]{:S(2)}) collective-permute-start(f32[128,128]{1,0:T(8,128)S(1)} %add.41), channel_id=1, source_target_pairs={{0,64},{16,80},{32,96},{48,112},{64,0},{80,16},{96,32},{112,48},{1... | collective-permute-start | bytes 196616 | tf_op jit(solution)/shard_map/ppermute | solution.py:602
  98.0 7.4 %collective-permute-start.9 = (f32[128,128]{1,0:T(8,128)S(1)}, f32[128,128]{1,0:T(8,128)S(1)}, u32[]{:S(2)}, u32[]{:S(2)}) collective-permute-start(f32[128,128]{1,0:T(8,128)S(1)} %add_add_fusion), channel_id=1, source_target_pairs={{0,32},{16,48},{32,0},{48,16},{64,96},{80,112},{96,64},{112,80},{1... | collective-permute-start | bytes 196616 | tf_op jit(solution)/shard_map/ppermute | solution.py:602
  109.6 7.4 %copy-start.24 = (f32[2,512]{1,0:T(2,128)S(1)}, f32[2,512]{1,0:T(2,128)}, u32[]{:S(2)}) copy-start(f32[2,512]{1,0:T(2,128)} %param.11) | copy-start | bytes 12292
  109.6 7.5 %copy-start.5 = (bf16[16,8,4224]{2,1,0:T(8,128)(2,1)S(1)}, bf16[16,8,4224]{2,1,0:T(8,128)(2,1)}, u32[]{:S(2)}) copy-start(bf16[16,8,4224]{2,1,0:T(8,128)(2,1)} %copy-done.4) | copy-start | bytes 3244036
  109.6 31.5 %all-to-all-start.3 = ((bf16[16,8,4096]{2,1,0:T(8,128)(2,1)}), bf16[16,8,4096]{2,1,0:T(8,128)(2,1)S(1)}, u32[]{:S(2)}, u32[]{:S(2)}) async-start(bf16[16,8,4096]{2,1,0:T(8,128)(2,1)} %bitcast.42), calls=%async_computation.3 | async-start | bytes 2097152 | tf_op jit(solution)/shard_map/all_to_all | solution.py:576
  117.1 3.4 %copy-start.11 = (s32[512,128]{1,0:T(8,128)S(1)}, s32[512,128]{1,0:T(8,128)}, u32[]{:S(2)}) copy-start(s32[512,128]{1,0:T(8,128)} %copy-done.10) | copy-start | bytes 786436
  117.1 3.4 %copy-start.14 = (s32[512,128]{1,0:T(8,128)S(1)}, s32[512,128]{1,0:T(8,128)}, u32[]{:S(2)}) copy-start(s32[512,128]{1,0:T(8,128)} %copy-done.13) | copy-start | bytes 786436
  117.1 3.4 %copy-start.17 = (s32[512,128]{1,0:T(8,128)S(1)}, s32[512,128]{1,0:T(8,128)}, u32[]{:S(2)}) copy-start(s32[512,128]{1,0:T(8,128)} %copy-done.16) | copy-start | bytes 786436
  117.1 3.4 %copy-start.20 = (s32[512,128]{1,0:T(8,128)S(1)}, s32[512,128]{1,0:T(8,128)}, u32[]{:S(2)}) copy-start(s32[512,128]{1,0:T(8,128)} %copy-done.19) | copy-start | bytes 786436
  120.5 20.6 %copy-start.3 = (bf16[32,8,2,512]{3,1,2,0:T(8,128)(2,1)S(1)}, bf16[32,8,2,512]{3,1,2,0:T(8,128)(2,1)}, u32[]{:S(2)}) copy-start(bf16[32,8,2,512]{3,1,2,0:T(8,128)(2,1)} %copy-done.2) | copy-start | bytes 1572868
  142.7 51.8 %copy-start.1 = (bf16[128,8,2,512]{3,1,2,0:T(8,128)(2,1)S(1)}, bf16[128,8,2,512]{3,1,2,0:T(8,128)(2,1)}, u32[]{:S(2)}) copy-start(bf16[128,8,2,512]{3,1,2,0:T(8,128)(2,1)} %copy-done) | copy-start | bytes 6291460
  194.5 12.1 %copy-start.8 = (bf16[512,1024]{1,0:T(8,128)(2,1)S(1)}, bf16[512,1024]{1,0:T(8,128)(2,1)}, u32[]{:S(2)}) copy-start(bf16[512,1024]{1,0:T(8,128)(2,1)} %get-tuple-element.36.refs_0_) | copy-start | bytes 3145732
  194.5 12.1 %copy-start.9 = (bf16[512,1024]{1,0:T(8,128)(2,1)S(1)}, bf16[512,1024]{1,0:T(8,128)(2,1)}, u32[]{:S(2)}) copy-start(bf16[512,1024]{1,0:T(8,128)(2,1)} %get-tuple-element.37.refs_1_) | copy-start | bytes 3145732
  197.5 1.4 collective-permute-start.10
  198.9 12.5 %collective-permute-start.13 = (f32[256,128]{1,0:T(8,128)S(1)}, f32[256,128]{1,0:T(8,128)S(1)}, u32[]{:S(2)}, u32[]{:S(2)}) collective-permute-start(f32[256,128]{1,0:T(8,128)S(1)} %add.46.refs_0_), channel_id=1, source_target_pairs={{0,192},{16,208},{32,224},{48,240},{64,128},{80,144},{96,160},{112... | collective-permute-start | bytes 393224 | tf_op jit(solution)/shard_map/ppermute | solution.py:602
  205.6 7.9 %collective-permute-start.12 = (f32[256,128]{1,0:T(8,128)S(1)}, f32[256,128]{1,0:T(8,128)S(1)}, u32[]{:S(2)}, u32[]{:S(2)}) collective-permute-start(f32[256,128]{1,0:T(8,128)S(1)} %add.46.refs_0_), channel_id=1, source_target_pairs={{0,128},{16,144},{32,160},{48,176},{64,192},{80,208},{96,224},{112... | collective-permute-start | bytes 393224 | tf_op jit(solution)/shard_map/ppermute | solution.py:602
  206.3 7.2 %collective-permute-start.11 = (f32[256,128]{1,0:T(8,128)S(1)}, f32[256,128]{1,0:T(8,128)S(1)}, u32[]{:S(2)}, u32[]{:S(2)}) collective-permute-start(f32[256,128]{1,0:T(8,128)S(1)} %add.46.refs_0_), channel_id=1, source_target_pairs={{0,64},{16,80},{32,96},{48,112},{64,0},{80,16},{96,32},{112,48},{1... | collective-permute-start | bytes 393224 | tf_op jit(solution)/shard_map/ppermute | solution.py:602
  213.5 6.8 %collective-permute-start.14 = (f32[256,128]{1,0:T(8,128)S(1)}, f32[256,128]{1,0:T(8,128)S(1)}, u32[]{:S(2)}, u32[]{:S(2)}) collective-permute-start(f32[256,128]{1,0:T(8,128)S(1)} %add_parts.1), channel_id=1, source_target_pairs={{0,32},{16,48},{32,0},{48,16},{64,96},{80,112},{96,64},{112,80},{1... | collective-permute-start | bytes 393224 | tf_op jit(solution)/shard_map/ppermute | solution.py:602
  215.6 4.7 %copy-start.12 = (s32[512,128]{1,0:T(8,128)S(1)}, s32[512,128]{1,0:T(8,128)}, u32[]{:S(2)}) copy-start(s32[512,128]{1,0:T(8,128)} %copy-done.10) | copy-start | bytes 786436
  215.6 4.8 %copy-start.15 = (s32[512,128]{1,0:T(8,128)S(1)}, s32[512,128]{1,0:T(8,128)}, u32[]{:S(2)}) copy-start(s32[512,128]{1,0:T(8,128)} %copy-done.13) | copy-start | bytes 786436
  215.6 4.8 %copy-start.18 = (s32[512,128]{1,0:T(8,128)S(1)}, s32[512,128]{1,0:T(8,128)}, u32[]{:S(2)}) copy-start(s32[512,128]{1,0:T(8,128)} %copy-done.16) | copy-start | bytes 786436
  220.4 1.0 copy-start.21

commit v6 on v5

--- a/solution.py
+++ b/solution.py
@@ -116,15 +116,17 @@
             for hit, route_codes in zip(hits, codes):
                 picked = jnp.dot(as_ones(hit), route_codes, preferred_element_type=F32)
                 kept = kept + jnp.where(lane_q == q, picked, 0.0)
-        send_ref[:, PER * inner :] = kept.astype(BF16)
+        start = PER * inner + c * LANES
+        send_refs[0][:, start : start + LANES] = kept.astype(BF16)
 
 
 def pack(routes_t, x, index):
     tokens, width = x.shape
-    send = jax.ShapeDtypeStruct((PACKED, PER * width + LANES), BF16)
+    widths = [PER * width + len(CHUNKS) * LANES] + [PER * width] * (len(CHUNKS) - 1)
     return pl.pallas_call(
         pack_kernel,
-        out_shape=(jax.ShapeDtypeStruct((8, tokens), I32),) + (send,) * len(CHUNKS),
+        out_shape=(jax.ShapeDtypeStruct((8, tokens), I32),)
+        + tuple(jax.ShapeDtypeStruct((PACKED, w), BF16) for w in widths),
         in_specs=[whole()] * 3,
         out_specs=(whole(),) * (1 + len(CHUNKS)),
         compiler_params=params(),
@@ -133,7 +135,8 @@
     )(routes_t, x, index)
 
 
-def maps_kernel(codes_ref, index_ref, low_ref, high_ref, scratch_ref):
+def maps_kernel(codes_ref, index_ref, low_ref, high_ref, token_ref, scratch_ref):
+    token_ref[...] = jnp.zeros_like(token_ref)
     code = codes_ref[...].astype(F32).astype(I32)
     tile = jnp.zeros(code.shape, I32)
     for h in range(7):
@@ -165,22 +168,24 @@
         high_ref[rows, :] = jnp.concatenate(highs, axis=0).T
 
 
-def slot_maps(arrived):
+def slot_maps(arrived, chunk):
     rows, width = arrived.shape
+    block = width // LANES - len(CHUNKS) + chunk
     shapes = [jax.ShapeDtypeStruct((PACKED, LANES), I32)]
     shapes += [jax.ShapeDtypeStruct((PER * PACKED, LANES), I32)] * 2
-    index, low, high = pl.pallas_call(
+    shapes.append(TOKEN)
+    index, low, high, token = pl.pallas_call(
         maps_kernel,
         grid=(1,),
         out_shape=tuple(shapes),
-        in_specs=[pl.BlockSpec((rows, LANES), lambda i: (0, width // LANES - 1))],
+        in_specs=[pl.BlockSpec((rows, LANES), lambda i: (0, block))],
         out_specs=tuple(pl.BlockSpec(s.shape, lambda i: (0, 0)) for s in shapes),
         scratch_shapes=[pltpu.VMEM((3, LANES, LANES), I32)],
         compiler_params=params(),
         cost_estimate=cost(2_000_000_000, 1 << 20),
         name="slot_maps",
     )(arrived)
-    return index, (low, high)
+    return index, (low, high), token
 
 
 def skipping(kernel, inputs, extra):
@@ -620,7 +625,7 @@
 
     info, *sends = pack(routes.T, x_home, latent_index.reshape(tokens, 2 * KEPT))
     arrived = [exchange(s) for s in sends]
-    index, maps = zip(*[slot_maps(a) for a in arrived])
+    index, maps, ready = zip(*[slot_maps(arrived[0], c) for c in range(len(CHUNKS))])
 
     pre, back, after = [], [], ()
     for c in range(len(CHUNKS)):
@@ -629,7 +634,7 @@
         else:
             part = encode_streamed(arrived[c], enc, bias, index[c], after)
         pre.append(width_sum(part))
-        decoded, token = decode(pre[c], *maps[c], dec, ())
+        decoded, token = decode(pre[c], *maps[c], dec, ready[1:] if c == 0 else ())
         after = (token,)
         back.append(exchange(decoded))
 

time: 228 us -> 227 us (level)
  starting transfers between devices: 44.1 us -> 40.9 us
  blocking collectives: 90 us -> 92.8 us
    ppermute x15, starting transfers between devices: 24.5 us -> 19.4 us  [width_sum(): lax.ppermute(part, 'width', [(a, a ^ m) for a in range(size)])]
    all_to_all x2, blocking collectives: 90 us -> 92.8 us  [exchange(): lax.all_to_all(rows.reshape(GROUPS, count // GROUPS, width), 'feat', spli...]
    ppermute x15, waiting for transfers between devices: 26.8 us -> 24 us  [width_sum(): lax.ppermute(part, 'width', [(a, a ^ m) for a in range(size)])]
    unnamed x53 -> x59, local copies, waits for them, and re-layouts: 4.18 us -> 4.83 us
  transfers between devices with their start and end apart: 18 -> 18, of which waited for: 14 -> 13; matrix products, arithmetic and copies ran while one was open for 1% -> 2% of each run, Pallas kernels for 12% -> 12%
where the time goes in v6:
time: 227 us; the launch traced here: 226 us
  blocking collectives  92.8 us (41%)
  waiting for transfers between devices  42.7 us (19%)
  starting transfers between devices  40.9 us (18%)
  Pallas kernels  40.1 us (18%)
  local copies, waits for them, and re-layouts  8.51 us (4%)
    all_to_all x2, blocking collectives, exchange(): lax.all_to_all(rows.reshape(GROUPS, count // GROUPS, width), 'feat', spli...  92.8 us
    ppermute x15, waiting for transfers between devices, width_sum(): lax.ppermute(part, 'width', [(a, a ^ m) for a in range(size)])  24 us
    all_to_all x3, starting transfers between devices, exchange(): lax.all_to_all(rows.reshape(GROUPS, count // GROUPS, width), 'feat', spli...  21.5 us
    ppermute x15, starting transfers between devices, width_sum(): lax.ppermute(part, 'width', [(a, a ^ m) for a in range(size)])  19.4 us
    all_to_all x3, waiting for transfers between devices, exchange(): lax.all_to_all(rows.reshape(GROUPS, count // GROUPS, width), 'feat', spli...  18.7 us
    pallas_call x2, Pallas kernels, decode(): pl.pallas_call(skipping(decode_kernel, 4, len(after)), out_shape=(hbm((PA...  7.73 us
    pallas_call x1, Pallas kernels, encoder_grad(): pl.pallas_call(functools.partial(encoder_grad_kernel, scale), out_shape=j...  5.54 us
    unnamed x59, local copies, waits for them, and re-layouts  4.83 us
  transfers between devices with their start and end apart: 18, of which 13 were waited for; matrix products, arithmetic and copies ran while one was open for 2% of the time, Pallas kernels for 12%

profile of v6, /device:TPU:32, one launch (start us, length us, event | category | flops | bytes accessed | tf_op | source)
XLA Modules:
  0.0 226.4 jit_solution(13968785153427535433)
XLA Ops:
  0.6 0.9 copy.10.index_ref
  1.6 1.1 copy.11
  2.7 0.7 copy-done.8
  3.4 2.2 pack_tokens.1
  5.6 38.7 %all_to_all.25 = bf16[16,8,4352]{2,1,0:T(8,128)(2,1)S(1)} all-to-all(bf16[16,8,4352]{2,1,0:T(8,128)(2,1)S(1)} %bitcast.36), channel_id=1, replica_groups=mesh['width'=16,'feat'=16] {'feat'}, dimensions={0} | all-to-all | bytes 2228224 | tf_op jit(solution)/shard_map/all_to_all | solution.py:581
  44.3 5.3 %all-to-all-start.2 = ((bf16[16,8,4096]{2,1,0:T(8,128)(2,1)}), bf16[16,8,4096]{2,1,0:T(8,128)(2,1)}, u32[]{:S(2)}, u32[]{:S(2)}) async-start(bf16[16,8,4096]{2,1,0:T(8,128)(2,1)} %bitcast.7), calls=%async_computation.2 | async-start | bytes 2097152 | tf_op jit(solution)/shard_map/all_to_all | solution.py:581
  49.6 2.5 %slot_maps.2 = (s32[128,128]{1,0:T(8,128)S(1)}, s32[512,128]{1,0:T(8,128)S(1)}, s32[512,128]{1,0:T(8,128)S(1)}, f32[8,128]{1,0:T(8,128)}) custom-call(bf16[128,4352]{1,0:T(8,128)(2,1)S(1)} %bitcast.32), custom_call_target="tpu_custom_call" | custom-call | flops 2000000000 | bytes 1048576 | tf_op jit(solution)/shard_map/slot_maps/pallas_call | solution.py:177
  52.2 1.6 encode.1
  53.9 1.2 collective-permute-done
  55.1 3.1 %collective-permute-start.3 = (f32[128,128]{1,0:T(8,128)S(1)}, f32[128,128]{1,0:T(8,128)S(1)}, u32[]{:S(2)}, u32[]{:S(2)}) collective-permute-start(f32[128,128]{1,0:T(8,128)S(1)} %add.36), channel_id=1, source_target_pairs={{0,192},{16,208},{32,224},{48,240},{64,128},{80,144},{96,160},{112... | collective-permute-start | bytes 196616 | tf_op jit(solution)/shard_map/ppermute | solution.py:607
  58.2 0.6 collective-permute-start.2
  58.9 0.5 collective-permute-start.1
  59.3 0.6 copy.13
  59.9 1.4 collective-permute-done.3
  61.3 3.0 %collective-permute-done.2 = f32[128,128]{1,0:T(8,128)S(1)} collective-permute-done((f32[128,128]{1,0:T(8,128)S(1)}, f32[128,128]{1,0:T(8,128)S(1)}, u32[]{:S(2)}, u32[]{:S(2)}) %collective-permute-start.2) | collective-permute-done | bytes 65568 | tf_op jit(solution)/shard_map/ppermute | solution.py:607
  64.3 3.0 %collective-permute-start.4 = (f32[128,128]{1,0:T(8,128)S(1)}, f32[128,128]{1,0:T(8,128)S(1)}, u32[]{:S(2)}, u32[]{:S(2)}) collective-permute-start(f32[128,128]{1,0:T(8,128)S(1)} %add_add_fusion.1), channel_id=1, source_target_pairs={{0,32},{16,48},{32,0},{48,16},{64,96},{80,112},{96,64},{112,80},{1... | collective-permute-start | bytes 196616 | tf_op jit(solution)/shard_map/ppermute | solution.py:607
  67.3 2.0 slot_maps.3
  69.4 0.7 copy-done.17
  70.1 0.7 copy-done.21
  70.8 1.0 collective-permute-done.4
  71.8 3.6 %decode.2 = (bf16[128,4096]{1,0:T(8,128)(2,1)}, f32[8,128]{1,0:T(8,128)S(1)}) custom-call(f32[128,128]{1,0:T(8,128)S(1)} %add.40.refs_0_, s32[512,128]{1,0:T(8,128)S(1)} %get-tuple-element.26.refs_1_.refs_2_, s32[512,128]{1,0:T(8,128)S(1)} %get-tuple-element.27.refs_2_.refs_3_, bf16[1024,1024]{1,0:T(8,128)(2,1)S(1)} %bitcast.25, ...), custom_call_target="tpu_custom_call" | custom-call | flops 2147483648 | bytes 6291456 | tf_op jit(solution)/shard_map/decode/pallas_call | solution.py:358
  75.4 7.8 %all-to-all-start.1 = ((bf16[16,8,4096]{2,1,0:T(8,128)(2,1)}), bf16[16,8,4096]{2,1,0:T(8,128)(2,1)S(1)}, u32[]{:S(2)}, u32[]{:S(2)}) async-start(bf16[16,8,4096]{2,1,0:T(8,128)(2,1)} %bitcast.42), calls=%async_computation.1 | async-start | bytes 2097152 | tf_op jit(solution)/shard_map/all_to_all | solution.py:581
  83.2 3.3 %encode_streamed.1 = f32[128,128]{1,0:T(8,128)S(1)} custom-call(bf16[128,4096]{1,0:T(8,128)(2,1)} %bitcast.8.refs_0_.refs_1_, bf16[1024,1024]{1,0:T(8,128)(2,1)} %bitcast.38, f32[1,1024]{1,0:T(1,128)S(1)} %broadcast_select_fusion.refs_2_, s32[128,128]{1,0:T(8,128)S(1)} %get-tuple-element.31.refs_3_.refs_1_, f32[8,128]{1,0:T(8,128)S(1)} %get-tuple-element.32.refs_4_), custom_call_target="tpu_custom_call" | custom-call | flops 2147483648 | bytes 4194304 | tf_op jit(solution)/shard_map/encode_streamed/pallas_call | solution.py:269
  86.6 1.2 collective-permute-done.5
  87.8 0.9 collective-permute-start.8
  88.7 2.5 %collective-permute-start.7 = (f32[128,128]{1,0:T(8,128)S(1)}, f32[128,128]{1,0:T(8,128)S(1)}, u32[]{:S(2)}, u32[]{:S(2)}) collective-permute-start(f32[128,128]{1,0:T(8,128)S(1)} %add.41), channel_id=1, source_target_pairs={{0,128},{16,144},{32,160},{48,176},{64,192},{80,208},{96,224},{112... | collective-permute-start | bytes 196616 | tf_op jit(solution)/shard_map/ppermute | solution.py:607
  91.3 0.7 collective-permute-start.6
  92.0 2.8 %collective-permute-done.8 = f32[128,128]{1,0:T(8,128)S(1)} collective-permute-done((f32[128,128]{1,0:T(8,128)S(1)}, f32[128,128]{1,0:T(8,128)S(1)}, u32[]{:S(2)}, u32[]{:S(2)}) %collective-permute-start.8) | collective-permute-done | bytes 65568 | tf_op jit(solution)/shard_map/ppermute | solution.py:607
  94.8 0.8 collective-permute-done.6
  95.6 3.2 %collective-permute-start.9 = (f32[128,128]{1,0:T(8,128)S(1)}, f32[128,128]{1,0:T(8,128)S(1)}, u32[]{:S(2)}, u32[]{:S(2)}) collective-permute-start(f32[128,128]{1,0:T(8,128)S(1)} %add_add_fusion), channel_id=1, source_target_pairs={{0,32},{16,48},{32,0},{48,16},{64,96},{80,112},{96,64},{112,80},{1... | collective-permute-start | bytes 196616 | tf_op jit(solution)/shard_map/ppermute | solution.py:607
  98.8 4.6 %collective-permute-done.9 = f32[128,128]{1,0:T(8,128)S(1)} collective-permute-done((f32[128,128]{1,0:T(8,128)S(1)}, f32[128,128]{1,0:T(8,128)S(1)}, u32[]{:S(2)}, u32[]{:S(2)}) %collective-permute-start.9) | collective-permute-done | bytes 65568 | tf_op jit(solution)/shard_map/ppermute | solution.py:607
  103.4 4.2 %decode.3 = (bf16[128,4096]{1,0:T(8,128)(2,1)}, f32[8,128]{1,0:T(8,128)}) custom-call(f32[128,128]{1,0:T(8,128)S(1)} %add.45.refs_0_.refs_1_, s32[512,128]{1,0:T(8,128)S(1)} %copy-done.18, s32[512,128]{1,0:T(8,128)S(1)} %copy-done.22, bf16[1024,1024]{1,0:T(8,128)(2,1)S(1)} %bitcast.26), custom_call_target="tpu_custom_call" | custom-call | flops 2147483648 | bytes 6291456 | tf_op jit(solution)/shard_map/decode/pallas_call | solution.py:358
  107.6 8.4 %all-to-all-start.3 = ((bf16[16,8,4096]{2,1,0:T(8,128)(2,1)}), bf16[16,8,4096]{2,1,0:T(8,128)(2,1)S(1)}, u32[]{:S(2)}, u32[]{:S(2)}) async-start(bf16[16,8,4096]{2,1,0:T(8,128)(2,1)} %bitcast.43), calls=%async_computation.3 | async-start | bytes 2097152 | tf_op jit(solution)/shard_map/all_to_all | solution.py:581
  116.1 3.4 %turn_rows.1 = (bf16[1024,512]{1,0:T(8,128)(2,1)}, bf16[1024,512]{1,0:T(8,128)(2,1)}, f32[8,128]{1,0:T(8,128)S(1)}) custom-call(bf16[128,4352]{1,0:T(8,128)(2,1)S(1)} %bitcast.35, bf16[128,4096]{1,0:T(8,128)(2,1)} %bitcast.8.refs_0_.refs_1_), custom_call_target="tpu_custom_call" | custom-call | flops 4000000000 | bytes 4194304 | tf_op jit(solution)/shard_map/turn_rows/pallas_call | solution.py:460
  119.5 4.2 %make_latents.1 = (bf16[512,1024]{1,0:T(8,128)(2,1)}, bf16[512,1024]{1,0:T(8,128)(2,1)}, f32[8,128]{1,0:T(8,128)S(1)}) custom-call(f32[128,128]{1,0:T(8,128)S(1)} %add.40.refs_0_, f32[128,128]{1,0:T(8,128)S(1)} %add.45.refs_0_.refs_1_, s32[512,128]{1,0:T(8,128)S(1)} %copy-done.12, s32[512,128]{1,0:T(8,128)S(1)} %copy-done.15, s32[512,128]{1,0:T(8,128)S(1)} %copy-done.19, ...), custom_call_target="tpu_custom_call" | custom-call | flops 4000000000 | bytes 4194304 | tf_op jit(solution)/shard_map/make_latents/pallas_call | solution.py:392
  123.7 18.7 %all-to-all-done.3 = bf16[16,8,4096]{2,1,0:T(8,128)(2,1)S(1)} async-done(((bf16[16,8,4096]{2,1,0:T(8,128)(2,1)}), bf16[16,8,4096]{2,1,0:T(8,128)(2,1)S(1)}, u32[]{:S(2)}, u32[]{:S(2)}) %all-to-all-start.3) | async-done | bytes 1048608 | tf_op jit(solution)/shard_map/all_to_all | solution.py:581
  142.5 1.5 form_residual.1
  144.0 54.1 %all_to_all.26 = bf16[16,8,8192]{2,1,0:T(8,128)(2,1)S(1)} all-to-all(bf16[16,8,8192]{2,1,0:T(8,128)(2,1)S(1)} %bitcast.22), channel_id=1, replica_groups=mesh['width'=16,'feat'=16] {'feat'}, dimensions={0} | all-to-all | bytes 4194304 | tf_op jit(solution)/shard_map/all_to_all | solution.py:581
  198.1 3.0 %latent_gradient.1 = f32[256,128]{1,0:T(8,128)S(1)} custom-call(bf16[128,8192]{1,0:T(8,128)(2,1)S(1)} %bitcast.28, bf16[1024,1024]{1,0:T(8,128)(2,1)S(1)} %bitcast.27, s32[128,128]{1,0:T(8,128)S(1)} %get-tuple-element.25.refs_3_.refs_0_, s32[128,128]{1,0:T(8,128)S(1)} %get-tuple-element.31.refs_3_.refs_1_), custom_call_target="tpu_custom_call" | custom-call | flops 4294967296 | bytes 4194304 | tf_op jit(solution)/shard_map/latent_gradient/pallas_call | solution.py:298
  201.2 1.3 collective-permute-done.10
  202.8 4.0 %collective-permute-start.11 = (f32[256,128]{1,0:T(8,128)S(1)}, f32[256,128]{1,0:T(8,128)S(1)}, u32[]{:S(2)}, u32[]{:S(2)}) collective-permute-start(f32[256,128]{1,0:T(8,128)S(1)} %add.46.refs_0_), channel_id=1, source_target_pairs={{0,64},{16,80},{32,96},{48,112},{64,0},{80,16},{96,32},{112,48},{1... | collective-permute-start | bytes 393224 | tf_op jit(solution)/shard_map/ppermute | solution.py:607
  206.7 3.0 %decoder_grad.1 = (bf16[1024,1024]{1,0:T(8,128)(2,1)S(1)}, f32[8,128]{1,0:T(8,128)S(1)}) custom-call(bf16[512,1024]{1,0:T(8,128)(2,1)S(1)} %copy-done.9, bf16[512,1024]{1,0:T(8,128)(2,1)S(1)} %copy-done.10, bf16[128,8192]{1,0:T(8,128)(2,1)S(1)} %bitcast.29), custom_call_target="tpu_custom_call" | custom-call | flops 2147483648 | bytes 6291456 | tf_op jit(solution)/shard_map/decoder_grad/pallas_call | solution.py:567
  209.8 2.4 %collective-permute-done.13.refs_3_ = f32[256,128]{1,0:T(8,128)S(1)} collective-permute-done((f32[256,128]{1,0:T(8,128)S(1)}, f32[256,128]{1,0:T(8,128)S(1)}, u32[]{:S(2)}, u32[]{:S(2)}) %collective-permute-start.13) | collective-permute-done | bytes 131104 | tf_op jit(solution)/shard_map/ppermute | solution.py:607
  212.2 0.6 collective-permute-done.11.refs_1_
  213.2 2.8 %reshape.71 = bf16[1,1024,2,512]{3,2,1,0:T(2,128)(2,1)} reshape(bf16[1024,1024]{1,0:T(8,128)(2,1)S(1)} %get-tuple-element.43) | data formatting | bytes 4194304 | tf_op jit(solution)/shard_map/reshape | solution.py:649
  216.0 3.7 %collective-permute-done.14 = f32[256,128]{1,0:T(8,128)S(1)} collective-permute-done((f32[256,128]{1,0:T(8,128)S(1)}, f32[256,128]{1,0:T(8,128)S(1)}, u32[]{:S(2)}, u32[]{:S(2)}) %collective-permute-start.14) | collective-permute-done | bytes 131104 | tf_op jit(solution)/shard_map/ppermute | solution.py:607
  219.7 0.9 copy-done.24
  220.6 5.5 %encoder_grad.1 = bf16[1024,1024]{1,0:T(8,128)(2,1)} custom-call(f32[256,128]{1,0:T(8,128)S(1)} %add.47.lg_ref, f32[128,128]{1,0:T(8,128)S(1)} %add.40.refs_0_, f32[128,128]{1,0:T(8,128)S(1)} %add.45.refs_0_.refs_1_, s32[512,128]{1,0:T(8,128)S(1)} %copy-done.13, s32[512,128]{1,0:T(8,128)S(1)} %copy-done.16, s32[512,128]{1,0:T(8,128)S(1)} %copy-done.20, ...), custom_call_target="tpu_custom_call" | custom-call | flops 4294967296 | bytes 6291456 | tf_op jit(solution)/shard_map/encoder_grad/pallas_call | solution.py:528
  (74 shorter events, 1.1 us)
Async XLA Ops:
  2.7 41.6 %copy-start.2 = (bf16[32,8,2,512]{3,1,2,0:T(8,128)(2,1)}, bf16[32,8,2,512]{3,1,2,0:T(8,128)(2,1)S(1)}, u32[]{:S(2)}) copy-start(bf16[32,8,2,512]{3,1,2,0:T(8,128)(2,1)S(1)} %copy.11) | copy-start | bytes 1572868
  2.7 0.7 copy-start.8
  5.6 44.0 %copy-start.26 = (f32[1,1024]{1,0:T(1,128)S(1)}, f32[1,1024]{1,0:T(1,128)}, u32[]{:S(2)}) copy-start(f32[1,1024]{1,0:T(1,128)} %param.9) | copy-start | bytes 12292
  44.3 7.8 %copy-start.4 = (bf16[16,8,4352]{2,1,0:T(8,128)(2,1)}, bf16[16,8,4352]{2,1,0:T(8,128)(2,1)S(1)}, u32[]{:S(2)}) copy-start(bf16[16,8,4352]{2,1,0:T(8,128)(2,1)S(1)} %all_to_all.25) | copy-start | bytes 3342340
  44.3 31.0 %all-to-all-start.2 = ((bf16[16,8,4096]{2,1,0:T(8,128)(2,1)}), bf16[16,8,4096]{2,1,0:T(8,128)(2,1)}, u32[]{:S(2)}, u32[]{:S(2)}) async-start(bf16[16,8,4096]{2,1,0:T(8,128)(2,1)} %bitcast.7), calls=%async_computation.2 | async-start | bytes 2097152 | tf_op jit(solution)/shard_map/all_to_all | solution.py:581
  49.6 2.5 %copy-start.7 = (bf16[1,2,512,1024]{3,2,1,0:T(8,128)(2,1)S(1)}, bf16[1,2,512,1024]{3,2,1,0:T(8,128)(2,1)}, u32[]{:S(2)}) copy-start(bf16[1,2,512,1024]{3,2,1,0:T(8,128)(2,1)} %param.8) | copy-start | bytes 6291460
  52.2 19.6 %copy-start.11 = (s32[512,128]{1,0:T(8,128)}, s32[512,128]{1,0:T(8,128)S(1)}, u32[]{:S(2)}) copy-start(s32[512,128]{1,0:T(8,128)S(1)} %get-tuple-element.26.refs_1_.refs_2_) | copy-start | bytes 786436
  52.2 19.6 %copy-start.14 = (s32[512,128]{1,0:T(8,128)}, s32[512,128]{1,0:T(8,128)S(1)}, u32[]{:S(2)}) copy-start(s32[512,128]{1,0:T(8,128)S(1)} %get-tuple-element.27.refs_2_.refs_3_) | copy-start | bytes 786436
  52.2 7.2 %copy-start.25 = (bf16[1,1024,2,512]{3,2,1,0:T(2,128)(2,1)S(1)}, bf16[1,1024,2,512]{3,2,1,0:T(2,128)(2,1)}, u32[]{:S(2)}) copy-start(bf16[1,1024,2,512]{3,2,1,0:T(2,128)(2,1)} %param.10) | copy-start | bytes 6291460
  53.8 1.3 collective-permute-start
  55.1 6.2 %collective-permute-start.3 = (f32[128,128]{1,0:T(8,128)S(1)}, f32[128,128]{1,0:T(8,128)S(1)}, u32[]{:S(2)}, u32[]{:S(2)}) collective-permute-start(f32[128,128]{1,0:T(8,128)S(1)} %add.36), channel_id=1, source_target_pairs={{0,192},{16,208},{32,224},{48,240},{64,128},{80,144},{96,160},{112... | collective-permute-start | bytes 196616 | tf_op jit(solution)/shard_map/ppermute | solution.py:607
  58.2 6.1 %collective-permute-start.2 = (f32[128,128]{1,0:T(8,128)S(1)}, f32[128,128]{1,0:T(8,128)S(1)}, u32[]{:S(2)}, u32[]{:S(2)}) collective-permute-start(f32[128,128]{1,0:T(8,128)S(1)} %add.36), channel_id=1, source_target_pairs={{0,128},{16,144},{32,160},{48,176},{64,192},{80,208},{96,224},{112... | collective-permute-start | bytes 196616 | tf_op jit(solution)/shard_map/ppermute | solution.py:607
  58.9 5.5 %collective-permute-start.1 = (f32[128,128]{1,0:T(8,128)S(1)}, f32[128,128]{1,0:T(8,128)S(1)}, u32[]{:S(2)}, u32[]{:S(2)}) collective-permute-start(f32[128,128]{1,0:T(8,128)S(1)} %add.36), channel_id=1, source_target_pairs={{0,64},{16,80},{32,96},{48,112},{64,0},{80,16},{96,32},{112,48},{1... | collective-permute-start | bytes 196616 | tf_op jit(solution)/shard_map/ppermute | solution.py:607
  59.3 8.0 %copy-start.5 = (bf16[16,8,4352]{2,1,0:T(8,128)(2,1)S(1)}, bf16[16,8,4352]{2,1,0:T(8,128)(2,1)}, u32[]{:S(2)}) copy-start(bf16[16,8,4352]{2,1,0:T(8,128)(2,1)} %copy-done.4) | copy-start | bytes 3342340
  59.9 43.5 %copy-start = (bf16[128,8,2,512]{3,1,2,0:T(8,128)(2,1)}, bf16[128,8,2,512]{3,1,2,0:T(8,128)(2,1)S(1)}, u32[]{:S(2)}) copy-start(bf16[128,8,2,512]{3,1,2,0:T(8,128)(2,1)S(1)} %copy.13) | copy-start | bytes 6291460
  64.3 7.4 %collective-permute-start.4 = (f32[128,128]{1,0:T(8,128)S(1)}, f32[128,128]{1,0:T(8,128)S(1)}, u32[]{:S(2)}, u32[]{:S(2)}) collective-permute-start(f32[128,128]{1,0:T(8,128)S(1)} %add_add_fusion.1), channel_id=1, source_target_pairs={{0,32},{16,48},{32,0},{48,16},{64,96},{80,112},{96,64},{112,80},{1... | collective-permute-start | bytes 196616 | tf_op jit(solution)/shard_map/ppermute | solution.py:607
  69.4 0.7 copy-start.17
  70.1 0.7 copy-start.21
  75.4 32.3 %all-to-all-start.1 = ((bf16[16,8,4096]{2,1,0:T(8,128)(2,1)}), bf16[16,8,4096]{2,1,0:T(8,128)(2,1)S(1)}, u32[]{:S(2)}, u32[]{:S(2)}) async-start(bf16[16,8,4096]{2,1,0:T(8,128)(2,1)} %bitcast.42), calls=%async_computation.1 | async-start | bytes 2097152 | tf_op jit(solution)/shard_map/all_to_all | solution.py:581
  83.1 20.3 %copy-start.18 = (s32[512,128]{1,0:T(8,128)S(1)}, s32[512,128]{1,0:T(8,128)}, u32[]{:S(2)}) copy-start(s32[512,128]{1,0:T(8,128)} %copy-done.17) | copy-start | bytes 786436
  83.1 20.3 %copy-start.22 = (s32[512,128]{1,0:T(8,128)S(1)}, s32[512,128]{1,0:T(8,128)}, u32[]{:S(2)}) copy-start(s32[512,128]{1,0:T(8,128)} %copy-done.21) | copy-start | bytes 786436
  86.5 1.3 collective-permute-start.5
  87.8 7.0 %collective-permute-start.8 = (f32[128,128]{1,0:T(8,128)S(1)}, f32[128,128]{1,0:T(8,128)S(1)}, u32[]{:S(2)}, u32[]{:S(2)}) collective-permute-start(f32[128,128]{1,0:T(8,128)S(1)} %add.41), channel_id=1, source_target_pairs={{0,192},{16,208},{32,224},{48,240},{64,128},{80,144},{96,160},{112... | collective-permute-start | bytes 196616 | tf_op jit(solution)/shard_map/ppermute | solution.py:607
  88.7 6.1 %collective-permute-start.7 = (f32[128,128]{1,0:T(8,128)S(1)}, f32[128,128]{1,0:T(8,128)S(1)}, u32[]{:S(2)}, u32[]{:S(2)}) collective-permute-start(f32[128,128]{1,0:T(8,128)S(1)} %add.41), channel_id=1, source_target_pairs={{0,128},{16,144},{32,160},{48,176},{64,192},{80,208},{96,224},{112... | collective-permute-start | bytes 196616 | tf_op jit(solution)/shard_map/ppermute | solution.py:607
  91.3 4.3 %collective-permute-start.6 = (f32[128,128]{1,0:T(8,128)S(1)}, f32[128,128]{1,0:T(8,128)S(1)}, u32[]{:S(2)}, u32[]{:S(2)}) collective-permute-start(f32[128,128]{1,0:T(8,128)S(1)} %add.41), channel_id=1, source_target_pairs={{0,64},{16,80},{32,96},{48,112},{64,0},{80,16},{96,32},{112,48},{1... | collective-permute-start | bytes 196616 | tf_op jit(solution)/shard_map/ppermute | solution.py:607
  95.6 7.8 %collective-permute-start.9 = (f32[128,128]{1,0:T(8,128)S(1)}, f32[128,128]{1,0:T(8,128)S(1)}, u32[]{:S(2)}, u32[]{:S(2)}) collective-permute-start(f32[128,128]{1,0:T(8,128)S(1)} %add_add_fusion), channel_id=1, source_target_pairs={{0,32},{16,48},{32,0},{48,16},{64,96},{80,112},{96,64},{112,80},{1... | collective-permute-start | bytes 196616 | tf_op jit(solution)/shard_map/ppermute | solution.py:607
  107.6 8.5 %copy-start.27 = (f32[2,512]{1,0:T(2,128)S(1)}, f32[2,512]{1,0:T(2,128)}, u32[]{:S(2)}) copy-start(f32[2,512]{1,0:T(2,128)} %param.11) | copy-start | bytes 12292
  107.6 8.5 %copy-start.6 = (bf16[16,8,4352]{2,1,0:T(8,128)(2,1)S(1)}, bf16[16,8,4352]{2,1,0:T(8,128)(2,1)}, u32[]{:S(2)}) copy-start(bf16[16,8,4352]{2,1,0:T(8,128)(2,1)} %copy-done.4) | copy-start | bytes 3342340
  107.6 34.8 %all-to-all-start.3 = ((bf16[16,8,4096]{2,1,0:T(8,128)(2,1)}), bf16[16,8,4096]{2,1,0:T(8,128)(2,1)S(1)}, u32[]{:S(2)}, u32[]{:S(2)}) async-start(bf16[16,8,4096]{2,1,0:T(8,128)(2,1)} %bitcast.43), calls=%async_computation.3 | async-start | bytes 2097152 | tf_op jit(solution)/shard_map/all_to_all | solution.py:581
  116.1 3.4 %copy-start.12 = (s32[512,128]{1,0:T(8,128)S(1)}, s32[512,128]{1,0:T(8,128)}, u32[]{:S(2)}) copy-start(s32[512,128]{1,0:T(8,128)} %copy-done.11) | copy-start | bytes 786436
  116.1 3.4 %copy-start.15 = (s32[512,128]{1,0:T(8,128)S(1)}, s32[512,128]{1,0:T(8,128)}, u32[]{:S(2)}) copy-start(s32[512,128]{1,0:T(8,128)} %copy-done.14) | copy-start | bytes 786436
  116.1 3.4 %copy-start.19 = (s32[512,128]{1,0:T(8,128)S(1)}, s32[512,128]{1,0:T(8,128)}, u32[]{:S(2)}) copy-start(s32[512,128]{1,0:T(8,128)} %copy-done.17) | copy-start | bytes 786436
  116.1 3.4 %copy-start.23 = (s32[512,128]{1,0:T(8,128)S(1)}, s32[512,128]{1,0:T(8,128)}, u32[]{:S(2)}) copy-start(s32[512,128]{1,0:T(8,128)} %copy-done.21) | copy-start | bytes 786436
  119.5 22.9 %copy-start.3 = (bf16[32,8,2,512]{3,1,2,0:T(8,128)(2,1)S(1)}, bf16[32,8,2,512]{3,1,2,0:T(8,128)(2,1)}, u32[]{:S(2)}) copy-start(bf16[32,8,2,512]{3,1,2,0:T(8,128)(2,1)} %copy-done.2) | copy-start | bytes 1572868
  144.0 54.1 %copy-start.1 = (bf16[128,8,2,512]{3,1,2,0:T(8,128)(2,1)S(1)}, bf16[128,8,2,512]{3,1,2,0:T(8,128)(2,1)}, u32[]{:S(2)}) copy-start(bf16[128,8,2,512]{3,1,2,0:T(8,128)(2,1)} %copy-done) | copy-start | bytes 6291460
  198.1 8.7 %copy-start.9 = (bf16[512,1024]{1,0:T(8,128)(2,1)S(1)}, bf16[512,1024]{1,0:T(8,128)(2,1)}, u32[]{:S(2)}) copy-start(bf16[512,1024]{1,0:T(8,128)(2,1)} %get-tuple-element.38.refs_0_) | copy-start | bytes 3145732
  198.1 8.7 %copy-start.10 = (bf16[512,1024]{1,0:T(8,128)(2,1)S(1)}, bf16[512,1024]{1,0:T(8,128)(2,1)}, u32[]{:S(2)}) copy-start(bf16[512,1024]{1,0:T(8,128)(2,1)} %get-tuple-element.39.refs_1_) | copy-start | bytes 3145732
  201.1 1.4 collective-permute-start.10
  202.6 9.7 %collective-permute-start.13 = (f32[256,128]{1,0:T(8,128)S(1)}, f32[256,128]{1,0:T(8,128)S(1)}, u32[]{:S(2)}, u32[]{:S(2)}) collective-permute-start(f32[256,128]{1,0:T(8,128)S(1)} %add.46.refs_0_), channel_id=1, source_target_pairs={{0,192},{16,208},{32,224},{48,240},{64,128},{80,144},{96,160},{112... | collective-permute-start | bytes 393224 | tf_op jit(solution)/shard_map/ppermute | solution.py:607
  202.7 9.6 %collective-permute-start.12 = (f32[256,128]{1,0:T(8,128)S(1)}, f32[256,128]{1,0:T(8,128)S(1)}, u32[]{:S(2)}, u32[]{:S(2)}) collective-permute-start(f32[256,128]{1,0:T(8,128)S(1)} %add.46.refs_0_), channel_id=1, source_target_pairs={{0,128},{16,144},{32,160},{48,176},{64,192},{80,208},{96,224},{112... | collective-permute-start | bytes 393224 | tf_op jit(solution)/shard_map/ppermute | solution.py:607
  202.8 10.0 %collective-permute-start.11 = (f32[256,128]{1,0:T(8,128)S(1)}, f32[256,128]{1,0:T(8,128)S(1)}, u32[]{:S(2)}, u32[]{:S(2)}) collective-permute-start(f32[256,128]{1,0:T(8,128)S(1)} %add.46.refs_0_), channel_id=1, source_target_pairs={{0,64},{16,80},{32,96},{48,112},{64,0},{80,16},{96,32},{112,48},{1... | collective-permute-start | bytes 393224 | tf_op jit(solution)/shard_map/ppermute | solution.py:607
  212.8 6.8 %collective-permute-start.14 = (f32[256,128]{1,0:T(8,128)S(1)}, f32[256,128]{1,0:T(8,128)S(1)}, u32[]{:S(2)}, u32[]{:S(2)}) collective-permute-start(f32[256,128]{1,0:T(8,128)S(1)} %add_parts.1), channel_id=1, source_target_pairs={{0,32},{16,48},{32,0},{48,16},{64,96},{80,112},{96,64},{112,80},{1... | collective-permute-start | bytes 393224 | tf_op jit(solution)/shard_map/ppermute | solution.py:607
  213.2 6.5 %copy-start.13 = (s32[512,128]{1,0:T(8,128)S(1)}, s32[512,128]{1,0:T(8,128)}, u32[]{:S(2)}) copy-start(s32[512,128]{1,0:T(8,128)} %copy-done.11) | copy-start | bytes 786436
  213.2 6.5 %copy-start.16 = (s32[512,128]{1,0:T(8,128)S(1)}, s32[512,128]{1,0:T(8,128)}, u32[]{:S(2)}) copy-start(s32[512,128]{1,0:T(8,128)} %copy-done.14) | copy-start | bytes 786436
  213.2 6.5 %copy-start.20 = (s32[512,128]{1,0:T(8,128)S(1)}, s32[512,128]{1,0:T(8,128)}, u32[]{:S(2)}) copy-start(s32[512,128]{1,0:T(8,128)} %copy-done.17) | copy-start | bytes 786436
  219.7 1.0 copy-start.24
